TPU v7x, 256 devices: a whole 4x4x8 slice. The times are simulated.
256 devices in a mesh: dp: 32 (over z_hi, x, y), graph: 8 (over z_lo, core).
Axes of the slice: x: 4, y: 4, z: 8 (z_hi: 2, z_lo: 4; z = z_hi * 4 + z_lo), core: 2. Of those that a mesh axis runs over, the one named last changes fastest.
Arguments:
- node_feats: bfloat16 [32, 512, 512], P('dp', 'graph'), may hold values from -6 to 6
- positions: float32 [32, 3, 512], P('dp', None, 'graph'), may hold values from -8 to 8
- edge_src: int32 [32, 2048], P('dp', 'graph'), may hold values from 0 to 511
- edge_dst: int32 [32, 2048], P('dp', 'graph'), may hold values from 0 to 511
- edge_count: int32 [32, 8], P('dp', 'graph'), may hold values from 64 to 256, as said below
- trip_in: int32 [32, 8192], P('dp', 'graph'), may hold values from 0 to 127
- trip_out: int32 [32, 8192], P('dp', 'graph'), may hold values from 0 to 127
- trip_count: int32 [32, 8], P('dp', 'graph'), may hold values from 256 to 1024, as said below
- graph_ids: int32 [32, 512], P('dp', 'graph'), may hold values from 0 to 15, never falling along the last dimension, each value on 1 to 64 neighbouring positions
- w_src: bfloat16 [512, 512], replicated, may hold values from -0.25 to 0.25
- w_dst: bfloat16 [512, 512], replicated, may hold values from -0.25 to 0.25
- w_radial: bfloat16 [128, 512], replicated, may hold values from -1 to 1
- w_trip: bfloat16 [512, 512], replicated, may hold values from -0.25 to 0.25
- w_out: bfloat16 [512, 512], replicated, may hold values from -0.25 to 0.25
- w_energy: bfloat16 [512], replicated, may hold values from -0.25 to 0.25
- energy_cot: float32 [32, 16], P('dp'), may hold values from -6 to 6
Outputs:
- energy: float32 [32, 16], P('dp')
- position_grad: float32 [32, 3, 512], P('dp', None, 'graph')
- node_grad: float32 [32, 512, 512], P('dp', 'graph')
- grad_src: float32 [512, 512], replicated
- grad_dst: float32 [512, 512], replicated
- grad_radial: float32 [128, 512], replicated
- grad_trip: float32 [512, 512], replicated
- grad_out: float32 [512, 512], replicated
- grad_energy: float32 [512], replicated
Inputs may be any that keep to these rules, and one draw needn't show every extreme that they name: `edge_count`: the live slots of a device are the first ones of its shard; in every draw one device holds 256 live edges and one holds 64. `trip_count`: in every draw one device holds 1024 live triplets and one holds 256.
All inputs are finite; a program needn't handle non-finite values.
Results may differ from a plain program's by a relative error of at most 0.02.
Values may be sent and summed in bfloat16 or wider, within the bound.
No kernel may reach another device: no remote copies, remote signals or barrier semaphores. Data moves between devices by JAX's collectives and lax.ppermute only.
A program may use at most 64 MiB of HBM per device.

v0:
```python
import jax
import jax.numpy as jnp
from jax import lax
from jax.sharding import PartitionSpec as P

EBLK = 128
TPB = 512


def edge_forward(
    trip_in,
    trip_out,
    live_e,
    live_t,
    rows_src,
    rows_dst,
    pos_src,
    pos_dst,
    w_src,
    w_dst,
    w_radial,
    w_trip,
):
    vec = pos_dst - pos_src
    dist = jnp.sqrt(jnp.sum(vec * vec, axis=0) + 0.25)
    count = w_radial.shape[0]
    centers = jnp.arange(count, dtype=jnp.float32) * (16.0 / count)
    basis = jnp.exp(-jnp.square((dist[:, None] - centers[None, :]) * (count / 24.0))).astype(
        jnp.bfloat16
    )
    pre = jnp.dot(rows_src, w_src, preferred_element_type=jnp.float32) + jnp.dot(
        rows_dst, w_dst, preferred_element_type=jnp.float32
    )
    radial = jnp.dot(basis, w_radial, preferred_element_type=jnp.float32)
    message = (jax.nn.silu(pre) * radial * live_e[:, None]).astype(jnp.bfloat16)
    edges, width = message.shape
    blocks = edges // EBLK
    unit = (vec / dist[None, :]).reshape(3, blocks, EBLK)
    incoming = trip_in.reshape(blocks, TPB)
    outgoing = trip_out.reshape(blocks, TPB)
    slots = jnp.arange(EBLK, dtype=jnp.int32)
    pick_in = (incoming[:, :, None] == slots[None, None, :]).astype(jnp.bfloat16)
    pick_out = (outgoing[:, :, None] == slots[None, None, :]).astype(jnp.bfloat16)
    in_dir = jnp.take_along_axis(unit, jnp.broadcast_to(incoming[None], (3, blocks, TPB)), axis=2)
    out_dir = jnp.take_along_axis(unit, jnp.broadcast_to(outgoing[None], (3, blocks, TPB)), axis=2)
    cosine = jnp.sum(in_dir * out_dir, axis=0).reshape(-1)
    gathered = jnp.einsum(
        "bte,bed->btd",
        pick_in,
        message.reshape(blocks, EBLK, width),
        preferred_element_type=jnp.float32,
    ).astype(jnp.bfloat16)
    projected = jnp.dot(gathered.reshape(-1, width), w_trip, preferred_element_type=jnp.float32)
    weighted = (
        (projected * (cosine * live_t)[:, None]).astype(jnp.bfloat16).reshape(blocks, TPB, width)
    )
    triplet = jnp.einsum(
        "bte,btd->bed", pick_out, weighted, preferred_element_type=jnp.float32
    ).reshape(edges, width)
    return (message.astype(jnp.float32) + triplet) * live_e[:, None]


def node_forward(h_float, agg, w_out, w_energy):
    out = jax.nn.silu(jnp.dot(agg.astype(jnp.bfloat16), w_out, preferred_element_type=jnp.float32))
    return jnp.sum((h_float + out) * w_energy.astype(jnp.float32)[None, :], axis=1)


def per_device(
    node_feats,
    positions,
    edge_src,
    edge_dst,
    edge_count,
    trip_in,
    trip_out,
    trip_count,
    graph_ids,
    w_src,
    w_dst,
    w_radial,
    w_trip,
    w_out,
    w_energy,
    energy_cot,
):
    h_own = node_feats[0]
    table = lax.all_gather(h_own, "graph", axis=0, tiled=True)
    pos_all = lax.all_gather(positions[0], "graph", axis=1, tiled=True)
    atoms = table.shape[0]
    src = edge_src[0]
    dst = edge_dst[0]
    live_e = (jnp.arange(src.shape[0], dtype=jnp.int32) < edge_count[0, 0]).astype(jnp.float32)
    live_t = (jnp.arange(trip_in.shape[1], dtype=jnp.int32) < trip_count[0, 0]).astype(jnp.float32)
    tin = trip_in[0]
    tout = trip_out[0]

    def local(rows_src, rows_dst, pos_src, pos_dst, a, b, c, d):
        return edge_forward(
            tin, tout, live_e, live_t, rows_src, rows_dst, pos_src, pos_dst, a, b, c, d
        )

    update, edge_back = jax.vjp(
        local,
        table[src],
        table[dst],
        pos_all[:, src],
        pos_all[:, dst],
        w_src,
        w_dst,
        w_radial,
        w_trip,
    )
    partial_agg = jax.ops.segment_sum(update, dst, num_segments=atoms)
    agg_own = lax.psum_scatter(partial_agg, "graph", scatter_dimension=0, tiled=True)
    atom_energy, node_back = jax.vjp(
        node_forward, h_own.astype(jnp.float32), agg_own, w_out, w_energy
    )
    onehot = (
        graph_ids[0][:, None] == jnp.arange(energy_cot.shape[1], dtype=jnp.int32)[None, :]
    ).astype(jnp.float32)
    energy = lax.psum(jnp.sum(onehot * atom_energy[:, None], axis=0), "graph")
    cot_atom = jnp.sum(onehot * energy_cot[0][None, :], axis=1)
    direct, agg_grad, g_out, g_energy = node_back(cot_atom)
    agg_cot = lax.all_gather(agg_grad.astype(jnp.bfloat16), "graph", axis=0, tiled=True)
    d_rs, d_rd, d_ps, d_pd, g_s, g_d, g_r, g_t = edge_back(agg_cot[dst].astype(jnp.float32))
    node_part = jax.ops.segment_sum(
        d_rs.astype(jnp.float32), src, num_segments=atoms
    ) + jax.ops.segment_sum(d_rd.astype(jnp.float32), dst, num_segments=atoms)
    pos_part = (
        jax.ops.segment_sum(d_ps.T, src, num_segments=atoms)
        + jax.ops.segment_sum(d_pd.T, dst, num_segments=atoms)
    ).T
    node_own, pos_own = (
        lax.psum_scatter(node_part, "graph", scatter_dimension=0, tiled=True),
        lax.psum_scatter(pos_part, "graph", scatter_dimension=1, tiled=True),
    )
    node_grad = direct + node_own
    grads = (
        g_s.astype(jnp.float32),
        g_d.astype(jnp.float32),
        g_r.astype(jnp.float32),
        g_t.astype(jnp.float32),
        g_out.astype(jnp.float32),
        g_energy.astype(jnp.float32),
    )
    summed = lax.psum((grads[0], grads[1], grads[2], grads[3], grads[4], grads[5]), ("dp", "graph"))
    return (
        energy[None],
        pos_own[None],
        node_grad[None],
        summed[0],
        summed[1],
        summed[2],
        summed[3],
        summed[4],
        summed[5],
    )


def solution(mesh):
    placed = (
        P("dp", "graph", None),
        P("dp", None, "graph"),
        P("dp", "graph"),
        P("dp", "graph"),
        P("dp", "graph"),
        P("dp", "graph"),
        P("dp", "graph"),
        P("dp", "graph"),
        P("dp", "graph"),
        P(),
        P(),
        P(),
        P(),
        P(),
        P(),
        P("dp", None),
    )
    return jax.shard_map(
        per_device,
        mesh=mesh,
        in_specs=placed,
        out_specs=(
            P("dp", None),
            P("dp", None, "graph"),
            P("dp", "graph", None),
            P(),
            P(),
            P(),
            P(),
            P(),
            P(),
        ),
        check_vma=False,
    )
```

profile of v0, /device:TPU:1, one launch (start us, length us, event | category | flops | bytes accessed | tf_op | source)
XLA Modules:
  0.0 590.1 jit_solution(17765661992243974407)
XLA Ops:
  7.2 0.5 broadcast.317
  7.8 1.3 reduce.15
  9.1 1.3 reduce.16
  10.5 0.8 copy.46
  11.3 17.3 %all-gather.1 = f32[1,3,512]{1,2,0:T(8,128)S(1)} all-gather(f32[1,3,64]{1,2,0:T(8,128)S(1)} %copy.46), channel_id=3, replica_groups=mesh['dp'=32,'graph'=8] {'graph'}, dimensions={2}, use_global_device_ids=true | all-gather | bytes 6912 | tf_op jit(solution)/shard_map/all_gather | solution.py:88
  28.6 0.7 compare_select_fusion
  29.3 0.7 compare_select_fusion.1
  30.0 0.7 gather_fusion.2
  30.7 0.7 gather_fusion.3
  31.4 14.9 %all-gather = bf16[1,512,512]{2,1,0:T(8,128)(2,1)S(1)} all-gather(bf16[1,64,512]{2,1,0:T(8,128)(2,1)} %param.18), channel_id=2, replica_groups=mesh['dp'=32,'graph'=8] {'graph'}, dimensions={1}, use_global_device_ids=true | all-gather | bytes 589824 | tf_op jit(solution)/shard_map/all_gather | solution.py:87
  46.4 1.2 gather_fusion
  47.5 1.2 gather_fusion.1
  49.1 0.4 copy-done.32
  49.7 25.9 %gather_fusion.5 = f32[3072]{0:T(1024)S(1)} fusion(f32[3,2,128]{0,2,1:T(8,128)S(1)} %broadcast_divide_fusion, s32[3072]{0:T(1024)S(1)} %bitcast.119), kind=kCustom, calls=%fused_computation.clone | custom fusion | bytes 61440 | tf_op jit(solution)/shard_map/jvp(jit(take_along_axis))/gather | solution.py:44
  75.6 25.9 %gather_fusion.6 = f32[3072]{0:T(1024)S(1)} fusion(f32[3,2,128]{0,2,1:T(8,128)S(1)} %broadcast_divide_fusion, s32[3072]{0:T(1024)S(1)} %bitcast.120), kind=kCustom, calls=%fused_computation.1.clone | custom fusion | bytes 61440 | tf_op jit(solution)/shard_map/jvp(jit(take_along_axis))/gather | solution.py:45
  104.0 1.1 multiply_convert_fusion.2
  105.1 0.5 convolution_convert_fusion.1
  105.6 0.7 multiply_convert_fusion
  106.6 0.6 fusion.23
  107.3 3.2 scatter_custom_fusion
  111.0 0.6 copy.66
  111.6 0.6 copy.68
  112.2 0.6 compare_convert_fusion
  112.9 0.6 multiply_divide_fusion
  113.5 32.4 %reduce-scatter.4.cloned.1.call-done = f32[64,512]{1,0:T(8,128)} async-done(((f32[512,512]{1,0:T(8,128)}), f32[64,512]{1,0:T(8,128)}) %reduce-scatter.4.cloned.1.call-update) | async-done | bytes 131088 | tf_op jit(solution)/shard_map/reduce_scatter | solution.py:114
  146.0 1.3 convert_add_fusion
  147.3 0.6 copy-done.18
  147.9 1.3 convolution_convert_fusion.11
  149.2 18.8 %all_gather.11 = bf16[512,512]{1,0:T(8,128)(2,1)S(1)} all-gather(bf16[64,512]{1,0:T(8,128)(2,1)S(1)} %convolution_convert_fusion.11), channel_id=1, replica_groups=mesh['dp'=32,'graph'=8] {'graph'}, dimensions={0}, use_global_device_ids=true | all-gather | bytes 589824 | tf_op jit(solution)/shard_map/all_gather | solution.py:124
  168.1 2.0 gather_fusion.4
  170.1 2.4 bitcast_multiply_fusion
  172.5 1.0 copy-done.1
  173.5 0.3 fusion.1
  173.8 0.3 copy-done.23
  174.2 21.9 %scatter_custom_fusion.5 = f32[768]{0:T(1024)S(1)} fusion(s32[3072]{0:T(1024)} %bitcast.134, f32[3072]{0:T(1024)S(1)} %bitcast.136, f32[]{:T(128)} %constant.18.clone.1), kind=kCustom, calls=%fused_computation.145 | custom fusion | flops 3072 | bytes 3584
  196.1 21.9 %scatter_custom_fusion.6 = f32[768]{0:T(1024)S(1)} fusion(s32[3072]{0:T(1024)} %bitcast.135, f32[3072]{0:T(1024)S(1)} %bitcast.137, f32[]{:T(128)} %constant.18.clone.1), kind=kCustom, calls=%fused_computation.143 | custom fusion | flops 3072 | bytes 3584
  218.1 2.1 fusion.74
  220.6 0.3 fusion.19
  221.2 0.3 fusion.9
  221.6 0.4 fusion.16
  222.6 1.6 scatter_custom_fusion.2
  224.2 1.6 scatter_custom_fusion.1
  225.9 0.7 add_bitcast_fusion
  226.7 1.1 fusion.8
  227.8 2.5 scatter_custom_fusion.3
  230.3 2.8 scatter_custom_fusion.4
  233.1 1.2 add.120
  234.7 2.1 fusion.10
  236.8 1.4 fusion.7
  238.2 1.3 fusion.5
  239.5 1.3 fusion.6
  240.8 1.8 fusion.4
  242.6 14.4 %reduce-scatter.6.cloned.1.call-done = f32[3,64]{0,1:T(8,128)} async-done(((f32[3,512]{0,1:T(8,128)}), f32[3,64]{0,1:T(8,128)}) %reduce-scatter.6.cloned.1.call-update) | async-done | bytes 784 | tf_op jit(solution)/shard_map/reduce_scatter | solution.py:135
  257.0 1.4 copy.57
  258.4 38.0 %reduce-scatter.8.cloned.1.call-done = f32[64,512]{1,0:T(8,128)} async-done(((f32[512,512]{1,0:T(8,128)}), f32[64,512]{1,0:T(8,128)}) %reduce-scatter.8.cloned.1.call-update) | async-done | bytes 131088 | tf_op jit(solution)/shard_map/reduce_scatter | solution.py:134
  296.4 1.7 multiply_reduce_fusion
  298.3 17.5 %psum.49 = f32[1,16]{1,0:T(1,128)} all-reduce(f32[1,16]{1,0:T(1,128)S(1)} %bitcast.148), channel_id=1, replica_groups=mesh['dp'=32,'graph'=8] {'graph'}, use_global_device_ids=true, to_apply=%region_6.8 | all-reduce | flops 16 | bytes 128 | tf_op jit(solution)/shard_map/psum | solution.py:121
  315.8 78.0 %psum.55 = f32[512]{0:T(512)} all-reduce(bf16[512]{0:T(512)(128)(2,1)S(1)} %get-tuple-element.53), channel_id=1, replica_groups=mesh['dp'=32,'graph'=8] {'dp','graph'}, use_global_device_ids=true, to_apply=%region_25.27 | all-reduce | flops 512 | bytes 3072 | tf_op jit(solution)/shard_map/psum | solution.py:146
  393.8 183.7 %all-reduce.3.cloned.1.call-done = (f32[512,512]{1,0:T(8,128)}, f32[512,512]{1,0:T(8,128)}, f32[128,512]{1,0:T(8,128)}, f32[512,512]{1,0:T(8,128)}, f32[512,512]{1,0:T(8,128)}) async-done(((f32[512,512]{1,0:T(8,128)}, f32[512,512]{1,0:T(8,128)}, f32[128,512]{1,0:T(8,128)}, f32[512,512]{1,0:T(8,128)}, f32[512,512]{1,0:T(8,128)}), (f32[512,512]{1,0:T(8,128)}, f32[512,512]{1,0:T(8,128)}, f32[128,512]{1,0:T(8,128)}, ...) | async-done | bytes 4456464 | tf_op jit(solution)/shard_map/psum | solution.py:146
  577.4 2.4 copy.77
  579.8 1.0 copy.78
  580.9 0.7 copy.79
  581.6 1.0 copy.80
  582.6 1.0 copy.81
  (175 shorter events, 4.4 us)
Async XLA Ops:
  7.2 98.5 %copy-start = (bf16[512,512]{1,0:T(8,128)(2,1)S(1)}, bf16[512,512]{1,0:T(8,128)(2,1)}, u32[]{:S(2)}) copy-start(bf16[512,512]{1,0:T(8,128)(2,1)} %param.30) | copy-start | bytes 1572868
  7.2 138.8 %reduce-scatter.4.cloned.1.call-start = ((), (), s32[]{:S(2)}) async-start(), calls=%async_computation.3 | async-start | bytes 1179648 | tf_op jit(solution)/shard_map/reduce_scatter | solution.py:114
  10.5 100.1 %copy-start.28 = (pred[2,512]{1,0:T(4,128)(4,1)}, pred[2,512]{1,0:T(4,128)(4,1)S(1)}, u32[]{:S(2)}) copy-start(pred[2,512]{1,0:T(4,128)(4,1)S(1)} %get-tuple-element.86) | copy-start | bytes 3076
  10.5 100.2 %copy-start.26 = (pred[2,512]{1,0:T(4,128)(4,1)}, pred[2,512]{1,0:T(4,128)(4,1)S(1)}, u32[]{:S(2)}) copy-start(pred[2,512]{1,0:T(4,128)(4,1)S(1)} %get-tuple-element.85) | copy-start | bytes 3076
  29.3 19.4 %copy-start.41 = (s32[1024]{0:T(1024)}, s32[1024]{0:T(1024)S(1)}, u32[]{:S(2)}) copy-start(s32[1024]{0:T(1024)S(1)} %pad_clamp_fusion) | copy-start | bytes 12292
  48.7 54.7 %copy-start.5 = (bf16[256,512]{1,0:T(8,128)(2,1)}, bf16[256,512]{1,0:T(8,128)(2,1)S(1)}, u32[]{:S(2)}) copy-start(bf16[256,512]{1,0:T(8,128)(2,1)S(1)} %gather_fusion.1) | copy-start | bytes 786436
  48.7 55.0 %copy-start.57 = (f32[128]{0:T(128)}, f32[128]{0:T(128)S(1)}, u32[]{:S(2)}) copy-start(f32[128]{0:T(128)S(1)} %iota_multiply_fusion) | copy-start | bytes 1540
  48.9 0.6 copy-start.32
  48.9 64.0 %copy-start.39 = (f32[256]{0:T(256)}, f32[256]{0:T(256)S(1)}, u32[]{:S(2)}) copy-start(f32[256]{0:T(256)S(1)} %get-tuple-element.68) | copy-start | bytes 3076
  48.9 0.6 copy-start.35
  49.1 54.6 %copy-start.42 = (f32[256]{0:T(256)}, f32[256]{0:T(256)S(1)}, u32[]{:S(2)}) copy-start(f32[256]{0:T(256)S(1)} %get-tuple-element.74) | copy-start | bytes 3076
  75.6 26.0 %copy-start.22 = (f32[3,2,512]{2,1,0:T(2,128)}, f32[3,2,512]{2,1,0:T(2,128)S(1)}, u32[]{:S(2)}) copy-start(f32[3,2,512]{2,1,0:T(2,128)S(1)} %reshape.341) | copy-start | bytes 36868
  75.6 27.4 %copy-start.10 = (bf16[512,512]{1,0:T(8,128)(2,1)S(1)}, bf16[512,512]{1,0:T(8,128)(2,1)}, u32[]{:S(2)}) copy-start(bf16[512,512]{1,0:T(8,128)(2,1)} %param.27) | copy-start | bytes 1572868
  101.6 1.8 copy-start.8
  101.6 2.1 copy-start.24
  101.6 2.1 copy-start.30
  103.0 4.1 copy-start.45
  103.0 0.9 copy-start.52
  103.7 1.4 copy-start.12
  105.6 1.0 copy-start.3
  105.6 1.0 copy-start.34
  107.2 3.5 copy-start.49
  107.2 3.6 copy-start.51
  107.2 3.7 copy-start.50
  107.2 5.6 copy-start.54
  107.2 5.6 copy-start.55
  110.6 146.4 %reduce-scatter.6.cloned.1.call-start = ((), (), s32[]{:S(2)}) async-start(), calls=%async_computation.4 | async-start | bytes 294912 | tf_op jit(solution)/shard_map/reduce_scatter | solution.py:135
  110.7 36.6 %copy-start.37 = (f32[512]{0:T(512)}, f32[512]{0:T(512)S(1)}, u32[]{:S(2)}) copy-start(f32[512]{0:T(512)S(1)} %convert_element_type.139) | copy-start | bytes 6148
  112.9 34.4 %copy-start.47 = (f32[64]{0:T(128)}, f32[64]{0:T(128)S(1)}, u32[]{:S(2)}) copy-start(f32[64]{0:T(128)S(1)} %select_reduce_fusion) | copy-start | bytes 772
  147.3 0.7 copy-start.18
  172.5 1.0 copy-start.1
  173.4 0.7 copy-start.23
  173.4 0.7 copy-start.25
  173.5 0.7 copy-start.27
  173.5 0.7 copy-start.29
  218.0 2.4 copy-start.7
  218.0 2.4 copy-start.13
  218.1 2.4 copy-start.20
  218.1 2.4 copy-start.46
  220.1 1.0 copy-start.11
  220.5 1.0 copy-start.43
  220.5 1.0 copy-start.53
  220.5 1.0 copy-start.58
  221.6 0.7 copy-start.36
  221.6 0.7 copy-start.44
  221.6 0.7 copy-start.40
  221.6 0.7 copy-start.33
  222.2 4.4 copy-start.9
  226.6 69.8 %reduce-scatter.8.cloned.1.call-start = ((), (), s32[]{:S(2)}) async-start(), calls=%async_computation.5 | async-start | bytes 1179648 | tf_op jit(solution)/shard_map/reduce_scatter | solution.py:134
  233.1 1.5 copy-start.31
  234.3 2.4 copy-start.17
  234.4 2.4 copy-start.19
  234.4 2.4 copy-start.38
  234.4 2.4 copy-start.48
  234.4 343.0 %all-reduce.3.cloned.1.call-start = ((), (), s32[]{:S(2)}) async-start(), calls=%async_computation.6 | async-start | bytes 8912896 | tf_op jit(solution)/shard_map/psum | solution.py:146
  236.8 2.7 copy-start.6
  238.2 2.6 copy-start.2
  238.2 2.6 copy-start.4
  242.6 55.6 %copy-start.56 = (s32[1,64]{1,0:T(1,128)S(1)}, s32[1,64]{1,0:T(1,128)}, u32[]{:S(2)}) copy-start(s32[1,64]{1,0:T(1,128)} %param.26) | copy-start | bytes 772
  577.4 2.4 copy-start.16
  579.8 1.1 copy-start.21
  579.8 1.8 copy-start.15
  580.9 1.7 copy-start.14
Sparse Core Ops, SparseCore 0:
  110.7 35.2 reduce-scatter.3
  226.7 30.2 reduce-scatter.5
  260.3 36.0 reduce-scatter.7
  304.1 273.2 all-reduce.2
where the time goes:
time: 591 us; the launch traced here: 590 us
  waiting for transfers between devices  269 us (46%)
  blocking collectives  147 us (25%)
  local copies, waits for them, and re-layouts  71.9 us (12%)
  other arithmetic  66 us (11%)
  matrix products  20.6 us (3%)
  between operations  16.2 us (3%)
    psum x1, waiting for transfers between devices, per_device(): lax.psum((grads[0], grads[1], grads[2], grads[3], grads[4], grads[5]), ('...  184 us
    psum x1, blocking collectives, per_device(): lax.psum((grads[0], grads[1], grads[2], grads[3], grads[4], grads[5]), ('...  78 us
    unnamed x11, other arithmetic  46.7 us
    reduce_scatter x1, waiting for transfers between devices, per_device(): lax.psum_scatter(node_part, 'graph', scatter_dimension=0, tiled=True)  38 us
    reduce_scatter x1, waiting for transfers between devices, per_device(): lax.psum_scatter(partial_agg, 'graph', scatter_dimension=0, tiled=True)  32.4 us
    gather x2, local copies, waits for them, and re-layouts, edge_forward(): jnp.take_along_axis(unit, jnp.broadcast_to(outgoing[None], (3, blocks, TP...  25.9 us
    gather x2, local copies, waits for them, and re-layouts, edge_forward(): jnp.take_along_axis(unit, jnp.broadcast_to(incoming[None], (3, blocks, TP...  25.9 us
    all_gather x1, blocking collectives, per_device(): lax.all_gather(agg_grad.astype(jnp.bfloat16), 'graph', axis=0, tiled=True)  18.8 us
  transfers between devices with their start and end apart: 4, of which 4 were waited for; matrix products, arithmetic and copies ran while one was open for 4% of the time, Pallas kernels for 0%

commit v1 on v0

v1 whole, which is shorter than its diff:
```python
import jax
import jax.numpy as jnp
from jax import lax
from jax.experimental import pallas as pl
from jax.experimental.pallas import tpu as pltpu
from jax.sharding import PartitionSpec as P

BF = jnp.bfloat16
F32 = jnp.float32
NG = 8
AT = 64
ATOMS = 512
ES = 256
EDGES = 2048
D = 512
K = 128
BLK = 128
TPB = 512
PIECE = 80
CH = 40
AXES = ("dp", "graph")
HI = lax.Precision.HIGHEST


def nn(a, b):
    return lax.dot_general(a, b, (((1,), (0,)), ((), ())), preferred_element_type=F32)


def nt(a, b):
    return lax.dot_general(a, b, (((1,), (1,)), ((), ())), preferred_element_type=F32)


def tn(a, b):
    return lax.dot_general(a, b, (((0,), (0,)), ((), ())), preferred_element_type=F32)


def pack_kernel(me_ref, h_ref, pos_ref, src_ref, dst_ref, ec_ref, tin_ref, tout_ref, tc_ref, gid_ref, out_ref, meta):
    odd = lax.rem(me_ref[0], 2)
    out_ref[0:AT, :] = h_ref[...]

    def place(row):
        full = jnp.concatenate([row, jnp.zeros_like(row)], axis=1)
        return jnp.where(odd == 1, pltpu.roll(full, AT, 1), full)

    for r, ref in ((0, src_ref), (1, dst_ref)):
        v = ref[...]
        half = lax.shift_right_logical(v, 1)
        meta[r : r + 1, 0:ES] = half.astype(F32)
        meta[r : r + 1, ES : 2 * ES] = (v - 2 * half).astype(F32)
    for r, ref in ((2, tin_ref), (4, tout_ref)):
        v = ref[...].astype(F32)
        meta[r : r + 1, :] = v[:, 0:TPB]
        meta[r + 1 : r + 2, :] = v[:, TPB : 2 * TPB]
    p = pos_ref[...]
    p1 = p.astype(BF).astype(F32)
    p2 = (p - p1).astype(BF).astype(F32)
    p3 = (p - p1) - p2
    meta[6:16, :] = jnp.zeros((10, D), F32)
    meta[6:9, 0:128] = place(p1)
    meta[9:12, 0:128] = place(p2)
    meta[12:15, 0:128] = place(p3)
    meta[15:16, 0:128] = place(gid_ref[...].astype(F32))
    tc = tc_ref[0, 0]
    tc_half = lax.shift_right_logical(tc, 3)
    meta[15:16, 128:256] = jnp.full((1, 128), ec_ref[0, 0].astype(F32))
    meta[15:16, 256:384] = jnp.full((1, 128), tc_half.astype(F32))
    meta[15:16, 384:512] = jnp.full((1, 128), (tc - 8 * tc_half).astype(F32))
    out_ref[AT:PIECE, :] = meta[...].astype(BF)


def pack(me, h, pos, src, dst, ec, tin, tout, tc, gid):
    vm = pl.BlockSpec(memory_space=pltpu.VMEM)
    sm = pl.BlockSpec(memory_space=pltpu.SMEM)
    return pl.pallas_call(
        pack_kernel,
        out_shape=jax.ShapeDtypeStruct((PIECE, D), BF),
        in_specs=[sm, vm, vm, vm, vm, sm, vm, vm, sm, vm],
        out_specs=vm,
        scratch_shapes=[pltpu.VMEM((16, D), F32)],
        name="pack",
    )(me, h, pos, src, dst, ec, tin, tout, tc, gid)


def main_kernel(
    me_ref,
    gat_ref,
    ws_ref,
    wd_ref,
    wr_ref,
    wt_ref,
    wo_ref,
    we_ref,
    ecot_ref,
    energy_ref,
    pos_out_ref,
    node_ref,
    pay_ref,
    h_s,
    ab_s,
    posp_s,
    oht_s,
    ohd_s,
    geo_s,
    msg_s,
    f_s,
    sg_s,
    m2_s,
    n_s,
    tt_s,
    upd_s,
    aggb_s,
    dzb_s,
    ac_s,
    cot_s,
    ge_s,
    bt_s,
    dm2_s,
    dpre_s,
    drad_s,
    dv_s,
    a_s,
    b_s,
    r_s,
):
    me = me_ref[0]
    gid_rows = []
    for j in range(4):
        first, second = gat_ref[2 * j, AT:PIECE, 0:128], gat_ref[2 * j + 1, AT:PIECE, 0:128]
        both = first.astype(F32) + second.astype(F32)
        posp_s[:, 128 * j : 128 * (j + 1)] = both.astype(BF)
        gid_rows.append(both[15:16, :])
    for s in range(NG):
        h_s[AT * s : AT * (s + 1), :] = gat_ref[s, 0:AT, :]
    gid_row = jnp.concatenate(gid_rows, axis=1)
    gid_col = jnp.transpose(jnp.broadcast_to(gid_row, (8, ATOMS)))[:, 0:1]
    h = h_s[...]
    ab_s[0:ATOMS, :] = nn(h, ws_ref[...]).astype(BF)
    ab_s[ATOMS : 2 * ATOMS, :] = nn(h, wd_ref[...]).astype(BF)

    step = 16.0 / K
    inv_width = K / 24.0
    sub_a = lax.broadcasted_iota(jnp.int32, (ATOMS, ES), 0).astype(F32)
    lane_a = lax.broadcasted_iota(jnp.int32, (ES, ATOMS), 1).astype(F32)
    sub_b = lax.broadcasted_iota(jnp.int32, (BLK, TPB), 0).astype(F32)
    lane_e = lax.broadcasted_iota(jnp.int32, (1, ES), 1).astype(F32)
    lane_t = lax.broadcasted_iota(jnp.int32, (1, TPB), 1).astype(F32)
    centers = lax.broadcasted_iota(jnp.int32, (1, K), 1).astype(F32) * step

    def onehot(cond):
        return jnp.where(cond, 1.0, 0.0).astype(BF)

    def forward(s, carry):
        meta = gat_ref[s, AT:PIECE, :].astype(F32)
        src = 2.0 * meta[0:1, 0:ES] + meta[0:1, ES : 2 * ES]
        dst = 2.0 * meta[1:2, 0:ES] + meta[1:2, ES : 2 * ES]
        ec = meta[15:16, 128:256]
        tc = 8.0 * meta[15:16, 256:384] + meta[15:16, 384:512]
        live = jnp.where(lane_e < jnp.concatenate([ec, ec], axis=1), 1.0, 0.0)
        lanes = pl.ds(pl.multiple_of(s * ES, ES), ES)
        ohts = onehot(sub_a == src)
        ohtd = onehot(sub_a == dst)
        oht_s[0:ATOMS, lanes] = ohts
        oht_s[ATOMS : 2 * ATOMS, lanes] = ohtd
        posp = posp_s[...]
        ps = nn(posp, ohts)
        pd = nn(posp, ohtd)
        ps = (ps[6:9] + ps[9:12]) + ps[12:15]
        pd = (pd[6:9] + pd[9:12]) + pd[12:15]
        vec = pd - ps
        sq = vec * vec
        dist = jnp.sqrt(sq[0:1] + sq[1:2] + sq[2:3] + 0.25)
        inv = 1.0 / dist
        unit = vec * inv
        geo = jnp.concatenate([src, dst, live, dist, unit, inv], axis=0)
        geo_s[s] = geo
        cols = jnp.transpose(geo)
        ohs = onehot(lane_a == cols[:, 0:1])
        ohd = onehot(lane_a == cols[:, 1:2])
        ohd_s[s] = ohd
        t = (cols[:, 3:4] - centers) * inv_width
        basis = jnp.exp(-(t * t)).astype(BF)
        bt_s[:, lanes] = jnp.transpose(basis.astype(F32)).astype(BF)
        pre = nn(ohs, ab_s[0:ATOMS, :]) + nn(ohd, ab_s[ATOMS : 2 * ATOMS, :])
        radial = nn(basis, wr_ref[...]) * cols[:, 2:3]
        sig = 0.5 + 0.5 * jnp.tanh(0.5 * pre)
        sil = pre * sig
        msg = (sil * radial).astype(BF)
        msg_s[s] = msg
        f_s[s] = (radial * (sig + sil * (1.0 - sig))).astype(BF)
        sg_s[s] = (sil * cols[:, 2:3]).astype(BF)
        m2 = nn(msg, wt_ref[...]).astype(BF)
        m2_s[s] = m2
        for i in range(2):
            rows = slice(BLK * i, BLK * (i + 1))
            limit = jnp.concatenate([tc] * 4, axis=1) - float(TPB * i)
            tin = meta[2 + i : 3 + i, :]
            tout = jnp.where(lane_t < limit, meta[4 + i : 5 + i, :], -1.0)
            pick_in = onehot(sub_b == tin)
            pick_out = onehot(sub_b == tout)
            count = nt(pick_out, pick_in) * cols[rows, 2:3]
            n_s[2 * s + i] = count
            gram = (
                cols[rows, 4:5] * unit[0:1, rows]
                + cols[rows, 5:6] * unit[1:2, rows]
                + cols[rows, 6:7] * unit[2:3, rows]
            )
            mix = count * gram
            tt_s[2 * s + i] = jnp.transpose(mix).astype(BF)
            upd = msg[rows].astype(F32) + nn(mix.astype(BF), m2[rows])
            upd_s[pl.ds(pl.multiple_of(s * ES + BLK * i, BLK), BLK), :] = upd.astype(BF)
        return carry

    lax.fori_loop(0, NG, forward, 0)

    agg = nn(oht_s[ATOMS : 2 * ATOMS, :], upd_s[...]).astype(BF)
    aggb_s[...] = agg
    z = nn(agg, wo_ref[...])
    sig = 0.5 + 0.5 * jnp.tanh(0.5 * z)
    out = z * sig
    we = we_ref[...].astype(F32)
    x = h_s[...].astype(F32) + out
    atom_energy = jnp.sum(x * we, axis=1, keepdims=True)
    member = jnp.where(
        lax.broadcasted_iota(jnp.int32, (ATOMS, 128), 1).astype(F32) == gid_col, 1.0, 0.0
    )
    energy_ref[...] = jnp.sum(member * atom_energy, axis=0, keepdims=True)
    cot = jnp.sum(member * ecot_ref[...], axis=1, keepdims=True)
    cot_s[...] = jnp.broadcast_to(cot, (ATOMS, 128))
    ge_s[...] = jnp.sum(x * cot, axis=0, keepdims=True)
    dz = (cot * we * (sig + out * (1.0 - sig))).astype(BF)
    dzb_s[...] = dz
    ac_s[...] = nt(dz, wo_ref[...]).astype(BF)

    def backward(s, carry):
        lanes = pl.ds(pl.multiple_of(s * ES, ES), ES)
        edges = pl.ds(pl.multiple_of(s * ES, ES), ES)
        geo = geo_s[s]
        cols = jnp.transpose(geo)
        ug = nn(ohd_s[s], ac_s[...])
        ugb = ug.astype(BF)
        m2 = m2_s[s]
        halves, turns = [], []
        for i in range(2):
            rows = slice(BLK * i, BLK * (i + 1))
            halves.append(nn(tt_s[2 * s + i], ugb[rows]).astype(BF))
            dgram = n_s[2 * s + i] * nt(ugb[rows], m2[rows])
            both = dgram + jnp.transpose(dgram)
            turns.append(
                lax.dot_general(
                    geo[:, rows], both, (((1,), (0,)), ((), ())), precision=HI, preferred_element_type=F32
                )
            )
        dm2 = jnp.concatenate(halves, axis=0)
        dm2_s[edges, :] = dm2
        dmsg = ug + nt(dm2, wt_ref[...])
        dpre_s[edges, :] = (dmsg * f_s[s].astype(F32)).astype(BF)
        drad = (dmsg * sg_s[s].astype(F32)).astype(BF)
        drad_s[edges, :] = drad
        t = (cols[:, 3:4] - centers) * inv_width
        slope = nt(drad, wr_ref[...]) * jnp.exp(-(t * t)) * (t * (-2.0 * inv_width))
        ddist = jnp.sum(jnp.transpose(slope), axis=0, keepdims=True)
        unit = geo[4:7]
        du = jnp.concatenate(turns, axis=1)[4:7]
        along = du * unit
        along = along[0:1] + along[1:2] + along[2:3]
        dv = geo[7:8] * (du - unit * along) + unit * ddist
        top = dv.astype(BF).astype(F32)
        dv_s[:, lanes] = jnp.concatenate(
            [top, dv - top, jnp.zeros((10, ES), F32)], axis=0
        ).astype(BF)
        return carry

    lax.fori_loop(0, NG, backward, 0)

    own = pl.multiple_of(me * AT, AT)
    ohs_own = oht_s[pl.ds(own, AT), :]
    ohd_own = oht_s[pl.ds(ATOMS + own, AT), :]
    dpre = dpre_s[...]
    s_src = nn(ohs_own, dpre).astype(BF)
    s_dst = nn(ohd_own, dpre).astype(BF)
    node_ref[...] = (
        cot_s[pl.ds(own, AT), 0:1] * we + nt(s_src, ws_ref[...]) + nt(s_dst, wd_ref[...])
    )
    pos = nt(dv_s[...], ohd_own) - nt(dv_s[...], ohs_own)
    pos_out_ref[...] = pos[0:3] + pos[3:6]

    group = lax.div(me, 4)
    block = pl.ds(pl.multiple_of(lax.rem(me, 4) * 128, 128), 128)
    side = pl.ds(pl.multiple_of(group * ATOMS, ATOMS), ATOMS)
    rows_t = tn(h_s[:, block], oht_s[side, :]).astype(BF)
    a_s[...] = nn(rows_t, dpre)

    @pl.when(group == 0)
    def _():
        for_trip = [msg_s[s, :, block] for s in range(NG)]
        b_s[...] = tn(jnp.concatenate(for_trip, axis=0), dm2_s[...])

    @pl.when(group == 1)
    def _():
        b_s[...] = tn(aggb_s[:, block], dzb_s[...])

    r_s[...] = nn(bt_s[pl.ds(pl.multiple_of(me * 16, 16), 16), :], drad_s[...])
    ge = ge_s[:, block]
    for d in range(32):
        rows, cols = 16 * (d // 4), slice(128 * (d % 4), 128 * (d % 4) + 128)
        two = 2 * (d // 4)
        pay_ref[d] = jnp.concatenate(
            [
                a_s[rows : rows + 16, cols],
                b_s[rows : rows + 16, cols],
                r_s[two : two + 2, cols],
                ge,
                jnp.zeros((5, 128), F32),
            ],
            axis=0,
        ).astype(BF)


def batch(me, gat, ws, wd, wr, wt, wo, we, ecot):
    vm = pl.BlockSpec(memory_space=pltpu.VMEM)
    sm = pl.BlockSpec(memory_space=pltpu.SMEM)
    V = pltpu.VMEM
    return pl.pallas_call(
        main_kernel,
        out_shape=(
            jax.ShapeDtypeStruct((1, 128), F32),
            jax.ShapeDtypeStruct((3, AT), F32),
            jax.ShapeDtypeStruct((AT, D), F32),
            jax.ShapeDtypeStruct((32, CH, 128), BF),
        ),
        in_specs=[sm] + [vm] * 8,
        out_specs=(vm, vm, vm, vm),
        scratch_shapes=[
            V((ATOMS, D), BF),
            V((2 * ATOMS, D), BF),
            V((16, ATOMS), BF),
            V((2 * ATOMS, EDGES), BF),
            V((NG, ES, ATOMS), BF),
            V((NG, 8, ES), F32),
            V((NG, ES, D), BF),
            V((NG, ES, D), BF),
            V((NG, ES, D), BF),
            V((NG, ES, D), BF),
            V((2 * NG, BLK, BLK), F32),
            V((2 * NG, BLK, BLK), BF),
            V((EDGES, D), BF),
            V((ATOMS, D), BF),
            V((ATOMS, D), BF),
            V((ATOMS, D), BF),
            V((ATOMS, 128), F32),
            V((1, D), F32),
            V((K, EDGES), BF),
            V((EDGES, D), BF),
            V((EDGES, D), BF),
            V((EDGES, D), BF),
            V((16, EDGES), BF),
            V((BLK, D), F32),
            V((BLK, D), F32),
            V((16, D), F32),
        ],
        compiler_params=pltpu.CompilerParams(vmem_limit_bytes=50 * 1024 * 1024),
        name="batch",
    )(me, gat, ws, wd, wr, wt, wo, we, ecot)


def sum_kernel(in_ref, out_ref):
    total = in_ref[0].astype(F32)
    for d in range(1, 32):
        total = total + in_ref[d].astype(F32)
    out_ref[...] = total.astype(BF)


def chunk_sum(x):
    vm = pl.BlockSpec(memory_space=pltpu.VMEM)
    return pl.pallas_call(
        sum_kernel,
        out_shape=jax.ShapeDtypeStruct((CH, 128), BF),
        in_specs=[vm],
        out_specs=vm,
        name="chunk_sum",
    )(x)


def place_kernel(me_ref, own_ref, other_ref, gs_ref, gd_ref, gr_ref, gt_ref, go_ref, ge_ref, pairs):
    z, x, y, core = me_ref[0], me_ref[1], me_ref[2], me_ref[3]

    for c, ref in ((0, own_ref), (1, other_ref)):

        def body(i, carry, c=c, ref=ref):
            kx, ky, kz = lax.div(i, 32), lax.rem(lax.div(i, 8), 4), lax.rem(i, 8)
            px = lax.rem(x - kx + 4, 4)
            py = lax.rem(y - ky + 4, 4)
            pz = lax.rem(z - kz + 8, 8)
            pc = lax.rem(core + c, 2)
            d = lax.div(pz, 4) * 16 + px * 4 + py
            g = lax.rem(pz, 4) * 2 + pc
            tile = ref[i].astype(F32)
            cols = pl.ds(pl.multiple_of(lax.rem(d, 4) * 128, 128), 128)
            high = lax.div(d, 4)
            rows = pl.ds(pl.multiple_of(lax.rem(g, 4) * 128 + high * 16, 16), 16)

            @pl.when(g < 4)
            def _():
                gs_ref[rows, cols] = tile[0:16]
                gt_ref[rows, cols] = tile[16:32]

            @pl.when(g >= 4)
            def _():
                gd_ref[rows, cols] = tile[0:16]
                go_ref[rows, cols] = tile[16:32]

            pairs[g * 8 + high, :, cols] = tile[32:40]

            @pl.when((g < 4) & (d == 0))
            def _():
                ge_ref[:, pl.ds(pl.multiple_of(lax.rem(g, 4) * 128, 128), 128)] = tile[34:35]

            return carry

        lax.fori_loop(0, 128, body, 0)
    for i in range(K // 2):
        gr_ref[2 * i : 2 * i + 2, :] = pairs[i, 0:2, :]


def place(where, own, other):
    vm = pl.BlockSpec(memory_space=pltpu.VMEM)
    sm = pl.BlockSpec(memory_space=pltpu.SMEM)
    big = jax.ShapeDtypeStruct((D, D), F32)
    return pl.pallas_call(
        place_kernel,
        out_shape=(big, big, jax.ShapeDtypeStruct((K, D), F32), big, big, jax.ShapeDtypeStruct((1, D), F32)),
        in_specs=[sm, vm, vm],
        out_specs=(vm,) * 6,
        scratch_shapes=[pltpu.VMEM((K // 2, 8, D), F32)],
        compiler_params=pltpu.CompilerParams(vmem_limit_bytes=40 * 1024 * 1024),
        name="place",
    )(where, own, other)


def moves(fn):
    pairs = []
    for zh in range(2):
        for x in range(4):
            for y in range(4):
                for zl in range(4):
                    for c in range(2):
                        z = zh * 4 + zl
                        z2, x2, y2, c2 = fn(z, x, y, c)
                        here = (zh * 16 + x * 4 + y) * 8 + zl * 2 + c
                        there = ((z2 // 4) * 16 + x2 * 4 + y2) * 8 + (z2 % 4) * 2 + c2
                        pairs.append((here, there))
    return pairs


def rotate(v, axis, k):
    if axis == "z":
        fn = lambda z, x, y, c: ((z + k) % 8, x, y, c)
    elif axis == "x":
        fn = lambda z, x, y, c: (z, (x + k) % 4, y, c)
    elif axis == "y":
        fn = lambda z, x, y, c: (z, x, (y + k) % 4, c)
    else:
        fn = lambda z, x, y, c: (z, x, y, 1 - c)
    return lax.ppermute(v, AXES, moves(fn))


def spread(v, axis, n):
    return jnp.concatenate([v] + [rotate(v, axis, k) for k in range(1, n)], axis=0)


def per_device(
    node_feats,
    positions,
    edge_src,
    edge_dst,
    edge_count,
    trip_in,
    trip_out,
    trip_count,
    graph_ids,
    w_src,
    w_dst,
    w_radial,
    w_trip,
    w_out,
    w_energy,
    energy_cot,
):
    dp, graph = lax.axis_index("dp"), lax.axis_index("graph")
    me = graph.reshape(1).astype(jnp.int32)
    piece = pack(
        me,
        node_feats[0],
        positions[0],
        edge_src,
        edge_dst,
        edge_count,
        trip_in,
        trip_out,
        trip_count,
        graph_ids,
    )
    gathered = lax.all_gather(piece, "graph", axis=0, tiled=False)
    ecot = jnp.pad(energy_cot, ((0, 0), (0, 128 - energy_cot.shape[1])))
    energy, pos_grad, node_grad, payload = batch(
        me, gathered, w_src, w_dst, w_radial, w_trip, w_out, w_energy.reshape(1, D), ecot
    )
    arrived = lax.all_to_all(payload, "dp", 0, 0, tiled=True)
    chunk = chunk_sum(arrived)
    part = spread(chunk[None], "z", 8)
    part = spread(part, "y", 4)
    part = spread(part, "x", 4)
    other = rotate(part, "core", 1)
    where = jnp.stack(
        [
            lax.div(dp, 16) * 4 + lax.div(graph, 2),
            lax.rem(lax.div(dp, 4), 4),
            lax.rem(dp, 4),
            lax.rem(graph, 2),
        ]
    ).astype(jnp.int32)
    gs, gd, gr, gt, go, ge = place(where, part, other)
    return (
        energy[:, 0 : energy_cot.shape[1]],
        pos_grad[None],
        node_grad[None],
        gs,
        gd,
        gr,
        gt,
        go,
        ge.reshape(D),
    )


def solution(mesh):
    placed = (
        P("dp", "graph", None),
        P("dp", None, "graph"),
        P("dp", "graph"),
        P("dp", "graph"),
        P("dp", "graph"),
        P("dp", "graph"),
        P("dp", "graph"),
        P("dp", "graph"),
        P("dp", "graph"),
        P(),
        P(),
        P(),
        P(),
        P(),
        P(),
        P("dp", None),
    )
    return jax.shard_map(
        per_device,
        mesh=mesh,
        in_specs=placed,
        out_specs=(
            P("dp", None),
            P("dp", None, "graph"),
            P("dp", "graph", None),
            P(),
            P(),
            P(),
            P(),
            P(),
            P(),
        ),
        check_vma=False,
    )
```

time: 591 us -> 155 us (0.26)
  waiting for transfers between devices: 269 us -> 22.9 us
  blocking collectives: 147 us -> 42.8 us
  other arithmetic: 66 us -> 0.08 us
  local copies, waits for them, and re-layouts: 71.9 us -> 9.31 us
  Pallas kernels: 0 us -> 48.3 us
  starting transfers between devices: 0.39 us -> 28.6 us
  matrix products: 20.6 us -> 0 us
  between operations: 16.2 us -> 2.06 us
    psum x1 -> x0, waiting for transfers between devices: 184 us -> none  [per_device(): lax.psum((grads[0], grads[1], grads[2], grads[3], grads[4], grads[5]), ('...]
    psum x2 -> x0, blocking collectives: 95.5 us -> none  [the longest x1 78 us: per_device(): lax.psum((grads[0], grads[1], grads[2], grads[3], grads[4], grads[5]), ('...]
    reduce_scatter x3 -> x0, waiting for transfers between devices: 84.9 us -> none  [the longest x1 38 us: per_device(): lax.psum_scatter(node_part, 'graph', scatter_dimension=0, tiled=True)]
    gather x11 -> x0, local copies, waits for them, and re-layouts: 57.8 us -> none  [the longest x2 25.9 us: edge_forward(): jnp.take_along_axis(unit, jnp.broadcast_to(outgoing[None], (3, blocks, TP...]
    pallas_call x0 -> x4, Pallas kernels: none -> 48.3 us  [the longest x1 31.2 us: batch(): pl.pallas_call(main_kernel, out_shape=(jax.ShapeDtypeStruct((1, 128), F32...]
    unnamed x11 -> x0, other arithmetic: 46.7 us -> none
    all_gather x3 -> x1, blocking collectives: 51 us -> 18.3 us  [per_device(): gathered = lax.all_gather(piece, 'graph', axis=0, tiled=False)]
    ppermute x0 -> x14, starting transfers between devices: none -> 28.6 us  [rotate(): return lax.ppermute(v, AXES, moves(fn))]
  transfers between devices with their start and end apart: 4 -> 14, of which waited for: 4 -> 8; matrix products, arithmetic and copies ran while one was open for 4% -> 1% of each run, Pallas kernels for 0% -> 0%
where the time goes in v1:
time: 155 us; the launch traced here: 154 us
  Pallas kernels  48.3 us (31%)
  blocking collectives  42.8 us (28%)
  starting transfers between devices  28.6 us (18%)
  waiting for transfers between devices  22.9 us (15%)
  local copies, waits for them, and re-layouts  9.31 us (6%)
  between operations  2.06 us (1%)
    pallas_call x1, Pallas kernels, batch(): pl.pallas_call(main_kernel, out_shape=(jax.ShapeDtypeStruct((1, 128), F32...  31.2 us
    ppermute x14, starting transfers between devices, rotate(): return lax.ppermute(v, AXES, moves(fn))  28.6 us
    all_to_all x1, blocking collectives, per_device(): arrived = lax.all_to_all(payload, 'dp', 0, 0, tiled=True)  24.6 us
    ppermute x14, waiting for transfers between devices, rotate(): return lax.ppermute(v, AXES, moves(fn))  22.9 us
    all_gather x1, blocking collectives, per_device(): gathered = lax.all_gather(piece, 'graph', axis=0, tiled=False)  18.3 us
    pallas_call x1, Pallas kernels, place(): pl.pallas_call(place_kernel, out_shape=(big, big, jax.ShapeDtypeStruct((K...  13.9 us
    unnamed x24, local copies, waits for them, and re-layouts  7.88 us
  transfers between devices with their start and end apart: 14, of which 8 were waited for; matrix products, arithmetic and copies ran while one was open for 1% of the time, Pallas kernels for 0%

profile of v1, /device:TPU:1, one launch (start us, length us, event | category | flops | bytes accessed | tf_op | source)
XLA Modules:
  0.0 154.1 jit_solution(1173152410313537621)
XLA Ops:
  1.9 1.3 copy.28
  3.2 0.7 reshape.28.we_ref
  3.9 1.6 %pack.1 = bf16[80,512]{1,0:T(8,128)(2,1)} custom-call(s32[1]{0:T(128)} %bitcast.me_ref, bf16[64,512]{1,0:T(8,128)(2,1)} %bitcast.20, f32[3,64]{1,0:T(4,128)} %bitcast.28, s32[1,256]{1,0:T(1,128)} %src_ref.1, s32[1,256]{1,0:T(1,128)} %dst_ref.1, s32[1,1]{1,0:T(1,128)S(6)} %copy.59.ec_ref, s32[1,1024]{1,0:T(1,128)} %tin_ref.1, s32[1,1024]{1,0:T(1,128)} %tout_ref.1, ...), custom_call_target="tpu_custom_call" | custom-call | tf_op jit(solution)/shard_map/pack/pallas_call | solution.py:74
  5.5 18.3 %all-gather = bf16[640,512]{1,0:T(8,128)(2,1)S(1)} all-gather(bf16[80,512]{1,0:T(8,128)(2,1)} %pack.1), channel_id=2, replica_groups=mesh['dp'=32,'graph'=8] {'graph'}, dimensions={0}, use_global_device_ids=true | all-gather | bytes 737280 | tf_op jit(solution)/shard_map/all_gather | solution.py:503
  23.8 0.7 pad.4.ecot_ref
  24.4 0.0 copy-start
  24.4 1.0 copy-done
  25.5 0.0 copy-start.1
  25.5 1.0 copy-done.1
  26.5 0.0 copy-start.2
  26.5 1.0 copy-done.2
  27.5 0.0 copy-start.3
  27.5 1.0 copy-done.3
  28.6 0.0 copy-start.4
  28.6 0.9 copy-done.4
  29.5 31.2 %batch.1 = (f32[1,128]{1,0:T(1,128)}, f32[3,64]{1,0:T(4,128)S(1)}, f32[64,512]{1,0:T(8,128)}, bf16[32,40,128]{2,1,0:T(8,128)(2,1)S(1)}) custom-call(s32[1]{0:T(128)} %bitcast.me_ref, bf16[8,80,512]{2,1,0:T(8,128)(2,1)S(1)} %bitcast.18, bf16[512,512]{1,0:T(8,128)(2,1)S(1)} %copy-done, bf16[512,512]{1,0:T(8,128)(2,1)S(1)} %copy-done.1, ...), custom_call_target="tpu_custom_call" | custom-call | tf_op jit(solution)/shard_map/batch/pallas_call | solution.py:323
  60.7 24.6 %all_to_all.5.in_ref = bf16[32,40,128]{2,1,0:T(8,128)(2,1)} all-to-all(bf16[32,40,128]{2,1,0:T(8,128)(2,1)S(1)} %get-tuple-element.22), channel_id=1, replica_groups=mesh['dp'=32,'graph'=8] {'dp'}, dimensions={0} | all-to-all | bytes 655360 | tf_op jit(solution)/shard_map/all_to_all | solution.py:508
  85.2 1.6 %chunk_sum.1 = bf16[40,128]{1,0:T(8,128)(2,1)} custom-call(bf16[32,40,128]{2,1,0:T(8,128)(2,1)} %all_to_all.5.in_ref), custom_call_target="tpu_custom_call" | custom-call | tf_op jit(solution)/shard_map/chunk_sum/pallas_call | solution.py:375
  86.9 0.0 collective-permute-start.6
  86.9 1.5 collective-permute-start.5
  88.4 4.4 %collective-permute-start.4 = (bf16[1,40,128]{2,1,0:T(8,128)(2,1)}, bf16[1,40,128]{2,1,0:T(8,128)(2,1)S(1)}, u32[]{:S(2)}, u32[]{:S(2)}) collective-permute-start(bf16[1,40,128]{2,1,0:T(8,128)(2,1)} %bitcast.23), channel_id=1, source_target_pairs={{0,130},{1,131},{2,132},{3,133},{4,134},{5,135},{6,0},{7,1},{8,138... | collective-permute-start | bytes 30728 | tf_op jit(solution)/shard_map/ppermute | solution.py:464
  92.7 0.7 collective-permute-start.3
  93.5 1.2 collective-permute-start
  94.7 0.7 constant_dynamic-update-slice_fusion.18
  95.4 2.0 %collective-permute-done = bf16[1,40,128]{2,1,0:T(8,128)(2,1)S(1)} collective-permute-done((bf16[1,40,128]{2,1,0:T(8,128)(2,1)}, bf16[1,40,128]{2,1,0:T(8,128)(2,1)S(1)}, u32[]{:S(2)}, u32[]{:S(2)}) %collective-permute-start) | collective-permute-done | bytes 10272 | tf_op jit(solution)/shard_map/ppermute | solution.py:464
  97.4 1.2 collective-permute-start.1
  98.6 3.7 %collective-permute-done.1 = bf16[1,40,128]{2,1,0:T(8,128)(2,1)S(1)} collective-permute-done((bf16[1,40,128]{2,1,0:T(8,128)(2,1)}, bf16[1,40,128]{2,1,0:T(8,128)(2,1)S(1)}, u32[]{:S(2)}, u32[]{:S(2)}) %collective-permute-start.1) | collective-permute-done | bytes 10272 | tf_op jit(solution)/shard_map/ppermute | solution.py:464
  102.3 1.2 collective-permute-start.2
  103.5 4.5 %collective-permute-done.2 = bf16[1,40,128]{2,1,0:T(8,128)(2,1)S(1)} collective-permute-done((bf16[1,40,128]{2,1,0:T(8,128)(2,1)}, bf16[1,40,128]{2,1,0:T(8,128)(2,1)S(1)}, u32[]{:S(2)}, u32[]{:S(2)}) %collective-permute-start.2) | collective-permute-done | bytes 10272 | tf_op jit(solution)/shard_map/ppermute | solution.py:464
  108.0 0.0 collective-permute-done.3
  108.0 0.0 collective-permute-done.4
  108.1 0.0 collective-permute-done.5
  108.1 0.0 collective-permute-done.6
  108.1 1.7 %collective-permute-start.7 = (bf16[8,40,128]{2,1,0:T(8,128)(2,1)S(1)}, bf16[8,40,128]{2,1,0:T(8,128)(2,1)S(1)}, u32[]{:S(2)}, u32[]{:S(2)}) collective-permute-start(bf16[8,40,128]{2,1,0:T(8,128)(2,1)S(1)} %get-tuple-element.46), channel_id=1, source_target_pairs={{0,8},{1,9},{2,10},{3,11},{4,12},{5,13},{6,14},{7,15},{8,16},{9,17... | collective-permute-start | bytes 245768 | tf_op jit(solution)/shard_map/ppermute | solution.py:464
  109.8 1.0 collective-permute-start.9
  110.9 1.6 %collective-permute-start.8 = (bf16[8,40,128]{2,1,0:T(8,128)(2,1)S(1)}, bf16[8,40,128]{2,1,0:T(8,128)(2,1)S(1)}, u32[]{:S(2)}, u32[]{:S(2)}) collective-permute-start(bf16[8,40,128]{2,1,0:T(8,128)(2,1)S(1)} %get-tuple-element.46), channel_id=1, source_target_pairs={{0,16},{1,17},{2,18},{3,19},{4,20},{5,21},{6,22},{7,23},{8,24},{9,... | collective-permute-start | bytes 245768 | tf_op jit(solution)/shard_map/ppermute | solution.py:464
  112.5 0.2 collective-permute-done.7
  112.7 2.9 %collective-permute-done.8 = bf16[8,40,128]{2,1,0:T(8,128)(2,1)S(1)} collective-permute-done((bf16[8,40,128]{2,1,0:T(8,128)(2,1)S(1)}, bf16[8,40,128]{2,1,0:T(8,128)(2,1)S(1)}, u32[]{:S(2)}, u32[]{:S(2)}) %collective-permute-start.8) | collective-permute-done | bytes 81952 | tf_op jit(solution)/shard_map/ppermute | solution.py:464
  115.7 0.0 collective-permute-done.9
  115.8 0.4 collective-permute-start.10
  116.1 3.6 %collective-permute-start.11 = (bf16[32,40,128]{2,1,0:T(8,128)(2,1)S(1)}, bf16[32,40,128]{2,1,0:T(8,128)(2,1)S(1)}, u32[]{:S(2)}, u32[]{:S(2)}) collective-permute-start(bf16[32,40,128]{2,1,0:T(8,128)(2,1)S(1)} %get-tuple-element.38), channel_id=1, source_target_pairs={{0,64},{1,65},{2,66},{3,67},{4,68},{5,69},{6,70},{7,71},{8,72},{9,... | collective-permute-start | bytes 983048 | tf_op jit(solution)/shard_map/ppermute | solution.py:464
  119.7 0.4 collective-permute-start.12
  120.2 3.2 %collective-permute-done.10 = bf16[32,40,128]{2,1,0:T(8,128)(2,1)S(1)} collective-permute-done((bf16[32,40,128]{2,1,0:T(8,128)(2,1)S(1)}, bf16[32,40,128]{2,1,0:T(8,128)(2,1)S(1)}, u32[]{:S(2)}, u32[]{:S(2)}) %collective-permute-start.10) | collective-permute-done | bytes 327712 | tf_op jit(solution)/shard_map/ppermute | solution.py:464
  123.3 0.1 constant_dynamic-update-slice_fusion.21
  123.4 4.3 %collective-permute-done.11 = bf16[32,40,128]{2,1,0:T(8,128)(2,1)S(1)} collective-permute-done((bf16[32,40,128]{2,1,0:T(8,128)(2,1)S(1)}, bf16[32,40,128]{2,1,0:T(8,128)(2,1)S(1)}, u32[]{:S(2)}, u32[]{:S(2)}) %collective-permute-start.11) | collective-permute-done | bytes 327712 | tf_op jit(solution)/shard_map/ppermute | solution.py:464
  127.7 0.1 constant_dynamic-update-slice_fusion.20
  127.8 0.0 collective-permute-done.12
  127.8 0.1 constant_dynamic-update-slice_fusion.19.own_ref
  127.8 9.7 %collective-permute-start.13 = (bf16[128,40,128]{2,1,0:T(8,128)(2,1)S(1)}, bf16[128,40,128]{2,1,0:T(8,128)(2,1)S(1)}, u32[]{:S(2)}, u32[]{:S(2)}) collective-permute-start(bf16[128,40,128]{2,1,0:T(8,128)(2,1)S(1)} %constant_dynamic-update-slice_fusion.19.own_ref), channel_id=1, source_target_pairs={{0,1},{1,0},{2,3},{3,2},{4,5},{5,4},{6,7},{7,6},{8,9},{9,8},{10,11... | collective-permute-start | bytes 3932168 | tf_op jit(solution)/shard_map/ppermute | solution.py:464
  137.5 0.6 copy.25
  138.1 0.1 pad_add_fusion.me_ref
  138.2 2.0 %collective-permute-done.13.other_ref = bf16[128,40,128]{2,1,0:T(8,128)(2,1)S(1)} collective-permute-done((bf16[128,40,128]{2,1,0:T(8,128)(2,1)S(1)}, bf16[128,40,128]{2,1,0:T(8,128)(2,1)S(1)}, u32[]{:S(2)}, u32[]{:S(2)}) %collective-permute-start.13) | collective-permute-done | bytes 1310752 | tf_op jit(solution)/shard_map/ppermute | solution.py:464
  140.2 13.9 %place.1 = (f32[512,512]{1,0:T(8,128)}, f32[512,512]{1,0:T(8,128)}, f32[128,512]{1,0:T(8,128)}, f32[512,512]{1,0:T(8,128)}, f32[512,512]{1,0:T(8,128)}, /*index=5*/f32[1,512]{1,0:T(1,128)}) custom-call(s32[4]{0:T(128)S(1)} %pad_add_fusion.me_ref, bf16[128,40,128]{2,1,0:T(8,128)(2,1)S(1)} %constant_dynamic-update-slice_fusion.19.own_ref, ...), custom_call_target="tpu_custom_call" | custom-call | tf_op jit(solution)/shard_map/place/pallas_call | solution.py:429
  (10 shorter events, 0.2 us)
Async XLA Ops:
  24.4 1.0 copy-start
  25.5 1.0 copy-start.1
  26.5 1.0 copy-start.2
  27.5 1.0 copy-start.3
  28.6 0.9 copy-start.4
  86.9 21.2 %collective-permute-start.6 = (bf16[1,40,128]{2,1,0:T(8,128)(2,1)}, bf16[1,40,128]{2,1,0:T(8,128)(2,1)S(1)}, u32[]{:S(2)}, u32[]{:S(2)}) collective-permute-start(bf16[1,40,128]{2,1,0:T(8,128)(2,1)} %bitcast.21), channel_id=1, source_target_pairs={{0,134},{1,135},{2,0},{3,1},{4,2},{5,3},{6,4},{7,5},{8,142},{9,143... | collective-permute-start | bytes 30728 | tf_op jit(solution)/shard_map/ppermute | solution.py:464
  86.9 21.2 %collective-permute-start.5 = (bf16[1,40,128]{2,1,0:T(8,128)(2,1)}, bf16[1,40,128]{2,1,0:T(8,128)(2,1)S(1)}, u32[]{:S(2)}, u32[]{:S(2)}) collective-permute-start(bf16[1,40,128]{2,1,0:T(8,128)(2,1)} %bitcast.22), channel_id=1, source_target_pairs={{0,132},{1,133},{2,134},{3,135},{4,0},{5,1},{6,2},{7,3},{8,140},{9... | collective-permute-start | bytes 30728 | tf_op jit(solution)/shard_map/ppermute | solution.py:464
  88.4 19.7 %collective-permute-start.4 = (bf16[1,40,128]{2,1,0:T(8,128)(2,1)}, bf16[1,40,128]{2,1,0:T(8,128)(2,1)S(1)}, u32[]{:S(2)}, u32[]{:S(2)}) collective-permute-start(bf16[1,40,128]{2,1,0:T(8,128)(2,1)} %bitcast.23), channel_id=1, source_target_pairs={{0,130},{1,131},{2,132},{3,133},{4,134},{5,135},{6,0},{7,1},{8,138... | collective-permute-start | bytes 30728 | tf_op jit(solution)/shard_map/ppermute | solution.py:464
  92.7 15.3 %collective-permute-start.3 = (bf16[1,40,128]{2,1,0:T(8,128)(2,1)}, bf16[1,40,128]{2,1,0:T(8,128)(2,1)S(1)}, u32[]{:S(2)}, u32[]{:S(2)}) collective-permute-start(bf16[1,40,128]{2,1,0:T(8,128)(2,1)} %bitcast.24), channel_id=1, source_target_pairs={{0,128},{1,129},{2,130},{3,131},{4,132},{5,133},{6,134},{7,135},{8... | collective-permute-start | bytes 30728 | tf_op jit(solution)/shard_map/ppermute | solution.py:464
  93.5 3.9 %collective-permute-start = (bf16[1,40,128]{2,1,0:T(8,128)(2,1)}, bf16[1,40,128]{2,1,0:T(8,128)(2,1)S(1)}, u32[]{:S(2)}, u32[]{:S(2)}) collective-permute-start(bf16[1,40,128]{2,1,0:T(8,128)(2,1)} %bitcast.25), channel_id=1, source_target_pairs={{0,2},{1,3},{2,4},{3,5},{4,6},{5,7},{6,128},{7,129},{8,10},{9,11},... | collective-permute-start | bytes 30728 | tf_op jit(solution)/shard_map/ppermute | solution.py:464
  97.4 4.8 %collective-permute-start.1 = (bf16[1,40,128]{2,1,0:T(8,128)(2,1)}, bf16[1,40,128]{2,1,0:T(8,128)(2,1)S(1)}, u32[]{:S(2)}, u32[]{:S(2)}) collective-permute-start(bf16[1,40,128]{2,1,0:T(8,128)(2,1)} %bitcast.26), channel_id=1, source_target_pairs={{0,4},{1,5},{2,6},{3,7},{4,128},{5,129},{6,130},{7,131},{8,12},{9,... | collective-permute-start | bytes 30728 | tf_op jit(solution)/shard_map/ppermute | solution.py:464
  102.3 5.7 %collective-permute-start.2 = (bf16[1,40,128]{2,1,0:T(8,128)(2,1)}, bf16[1,40,128]{2,1,0:T(8,128)(2,1)S(1)}, u32[]{:S(2)}, u32[]{:S(2)}) collective-permute-start(bf16[1,40,128]{2,1,0:T(8,128)(2,1)} %bitcast.27), channel_id=1, source_target_pairs={{0,6},{1,7},{2,128},{3,129},{4,130},{5,131},{6,132},{7,133},{8,14}... | collective-permute-start | bytes 30728 | tf_op jit(solution)/shard_map/ppermute | solution.py:464
  108.1 4.6 %collective-permute-start.7 = (bf16[8,40,128]{2,1,0:T(8,128)(2,1)S(1)}, bf16[8,40,128]{2,1,0:T(8,128)(2,1)S(1)}, u32[]{:S(2)}, u32[]{:S(2)}) collective-permute-start(bf16[8,40,128]{2,1,0:T(8,128)(2,1)S(1)} %get-tuple-element.46), channel_id=1, source_target_pairs={{0,8},{1,9},{2,10},{3,11},{4,12},{5,13},{6,14},{7,15},{8,16},{9,17... | collective-permute-start | bytes 245768 | tf_op jit(solution)/shard_map/ppermute | solution.py:464
  109.8 5.9 %collective-permute-start.9 = (bf16[8,40,128]{2,1,0:T(8,128)(2,1)S(1)}, bf16[8,40,128]{2,1,0:T(8,128)(2,1)S(1)}, u32[]{:S(2)}, u32[]{:S(2)}) collective-permute-start(bf16[8,40,128]{2,1,0:T(8,128)(2,1)S(1)} %get-tuple-element.46), channel_id=1, source_target_pairs={{0,24},{1,25},{2,26},{3,27},{4,28},{5,29},{6,30},{7,31},{8,0},{9,1... | collective-permute-start | bytes 245768 | tf_op jit(solution)/shard_map/ppermute | solution.py:464
  110.9 4.8 %collective-permute-start.8 = (bf16[8,40,128]{2,1,0:T(8,128)(2,1)S(1)}, bf16[8,40,128]{2,1,0:T(8,128)(2,1)S(1)}, u32[]{:S(2)}, u32[]{:S(2)}) collective-permute-start(bf16[8,40,128]{2,1,0:T(8,128)(2,1)S(1)} %get-tuple-element.46), channel_id=1, source_target_pairs={{0,16},{1,17},{2,18},{3,19},{4,20},{5,21},{6,22},{7,23},{8,24},{9,... | collective-permute-start | bytes 245768 | tf_op jit(solution)/shard_map/ppermute | solution.py:464
  115.8 7.6 %collective-permute-start.10 = (bf16[32,40,128]{2,1,0:T(8,128)(2,1)S(1)}, bf16[32,40,128]{2,1,0:T(8,128)(2,1)S(1)}, u32[]{:S(2)}, u32[]{:S(2)}) collective-permute-start(bf16[32,40,128]{2,1,0:T(8,128)(2,1)S(1)} %get-tuple-element.38), channel_id=1, source_target_pairs={{0,32},{1,33},{2,34},{3,35},{4,36},{5,37},{6,38},{7,39},{8,40},{9,... | collective-permute-start | bytes 983048 | tf_op jit(solution)/shard_map/ppermute | solution.py:464
  116.1 11.6 %collective-permute-start.11 = (bf16[32,40,128]{2,1,0:T(8,128)(2,1)S(1)}, bf16[32,40,128]{2,1,0:T(8,128)(2,1)S(1)}, u32[]{:S(2)}, u32[]{:S(2)}) collective-permute-start(bf16[32,40,128]{2,1,0:T(8,128)(2,1)S(1)} %get-tuple-element.38), channel_id=1, source_target_pairs={{0,64},{1,65},{2,66},{3,67},{4,68},{5,69},{6,70},{7,71},{8,72},{9,... | collective-permute-start | bytes 983048 | tf_op jit(solution)/shard_map/ppermute | solution.py:464
  119.7 8.0 %collective-permute-start.12 = (bf16[32,40,128]{2,1,0:T(8,128)(2,1)S(1)}, bf16[32,40,128]{2,1,0:T(8,128)(2,1)S(1)}, u32[]{:S(2)}, u32[]{:S(2)}) collective-permute-start(bf16[32,40,128]{2,1,0:T(8,128)(2,1)S(1)} %get-tuple-element.38), channel_id=1, source_target_pairs={{0,96},{1,97},{2,98},{3,99},{4,100},{5,101},{6,102},{7,103},{8,104... | collective-permute-start | bytes 983048 | tf_op jit(solution)/shard_map/ppermute | solution.py:464
  127.8 12.4 %collective-permute-start.13 = (bf16[128,40,128]{2,1,0:T(8,128)(2,1)S(1)}, bf16[128,40,128]{2,1,0:T(8,128)(2,1)S(1)}, u32[]{:S(2)}, u32[]{:S(2)}) collective-permute-start(bf16[128,40,128]{2,1,0:T(8,128)(2,1)S(1)} %constant_dynamic-update-slice_fusion.19.own_ref), channel_id=1, source_target_pairs={{0,1},{1,0},{2,3},{3,2},{4,5},{5,4},{6,7},{7,6},{8,9},{9,8},{10,11... | collective-permute-start | bytes 3932168 | tf_op jit(solution)/shard_map/ppermute | solution.py:464

commit v2 on v1

--- a/solution.py
+++ b/solution.py
@@ -17,7 +17,7 @@
 BLK = 128
 TPB = 512
 PIECE = 80
-CH = 40
+CH = 80
 AXES = ("dp", "graph")
 HI = lax.Precision.HIGHEST
 
@@ -34,7 +34,9 @@
     return lax.dot_general(a, b, (((0,), (0,)), ((), ())), preferred_element_type=F32)
 
 
-def pack_kernel(me_ref, h_ref, pos_ref, src_ref, dst_ref, ec_ref, tin_ref, tout_ref, tc_ref, gid_ref, out_ref, meta):
+def pack_kernel(me_ref, h_ref, pos_ref, src_ref, dst_ref, ec_ref, tin_ref, tout_ref, tc_ref, gid_ref, out_ref, meta, pos_v, sem):
+    fetch = pltpu.make_async_copy(pos_ref, pos_v, sem)
+    fetch.start()
     odd = lax.rem(me_ref[0], 2)
     out_ref[0:AT, :] = h_ref[...]
 
@@ -51,7 +53,8 @@
         v = ref[...].astype(F32)
         meta[r : r + 1, :] = v[:, 0:TPB]
         meta[r + 1 : r + 2, :] = v[:, TPB : 2 * TPB]
-    p = pos_ref[...]
+    fetch.wait()
+    p = jnp.concatenate([pos_v[i] for i in range(3)], axis=0)
     p1 = p.astype(BF).astype(F32)
     p2 = (p - p1).astype(BF).astype(F32)
     p3 = (p - p1) - p2
@@ -74,9 +77,9 @@
     return pl.pallas_call(
         pack_kernel,
         out_shape=jax.ShapeDtypeStruct((PIECE, D), BF),
-        in_specs=[sm, vm, vm, vm, vm, sm, vm, vm, sm, vm],
+        in_specs=[sm, vm, pl.BlockSpec(memory_space=pl.ANY), vm, vm, sm, vm, vm, sm, vm],
         out_specs=vm,
-        scratch_shapes=[pltpu.VMEM((16, D), F32)],
+        scratch_shapes=[pltpu.VMEM((16, D), F32), pltpu.VMEM((3, 1, AT), F32), pltpu.SemaphoreType.DMA],
         name="pack",
     )(me, h, pos, src, dst, ec, tin, tout, tc, gid)
 
@@ -84,11 +87,11 @@
 def main_kernel(
     me_ref,
     gat_ref,
-    ws_ref,
-    wd_ref,
-    wr_ref,
-    wt_ref,
-    wo_ref,
+    ws_hbm,
+    wd_hbm,
+    wr_hbm,
+    wt_hbm,
+    wo_hbm,
     we_ref,
     ecot_ref,
     energy_ref,
@@ -121,22 +124,40 @@
     a_s,
     b_s,
     r_s,
+    ws_ref,
+    wd_ref,
+    wr_ref,
+    wt_ref,
+    wo_ref,
+    sems,
 ):
-    me = me_ref[0]
+    loads = [
+        pltpu.make_async_copy(far, near, sems.at[i])
+        for i, (far, near) in enumerate(
+            ((ws_hbm, ws_ref), (wd_hbm, wd_ref), (wr_hbm, wr_ref), (wt_hbm, wt_ref), (wo_hbm, wo_ref))
+        )
+    ]
+    for load in loads:
+        load.start()
+    me, my_u, my_v = me_ref[0], me_ref[1], me_ref[2]
     gid_rows = []
     for j in range(4):
-        first, second = gat_ref[2 * j, AT:PIECE, 0:128], gat_ref[2 * j + 1, AT:PIECE, 0:128]
+        first, second = gat_ref[me ^ (2 * j), AT:PIECE, 0:128], gat_ref[me ^ (2 * j + 1), AT:PIECE, 0:128]
         both = first.astype(F32) + second.astype(F32)
         posp_s[:, 128 * j : 128 * (j + 1)] = both.astype(BF)
         gid_rows.append(both[15:16, :])
     for s in range(NG):
-        h_s[AT * s : AT * (s + 1), :] = gat_ref[s, 0:AT, :]
+        h_s[AT * s : AT * (s + 1), :] = gat_ref[me ^ s, 0:AT, :]
     gid_row = jnp.concatenate(gid_rows, axis=1)
     gid_col = jnp.transpose(jnp.broadcast_to(gid_row, (8, ATOMS)))[:, 0:1]
     h = h_s[...]
+    loads[0].wait()
     ab_s[0:ATOMS, :] = nn(h, ws_ref[...]).astype(BF)
+    loads[1].wait()
     ab_s[ATOMS : 2 * ATOMS, :] = nn(h, wd_ref[...]).astype(BF)
 
+    for load in loads[2:]:
+        load.wait()
     step = 16.0 / K
     inv_width = K / 24.0
     sub_a = lax.broadcasted_iota(jnp.int32, (ATOMS, ES), 0).astype(F32)
@@ -150,7 +171,7 @@
         return jnp.where(cond, 1.0, 0.0).astype(BF)
 
     def forward(s, carry):
-        meta = gat_ref[s, AT:PIECE, :].astype(F32)
+        meta = gat_ref[lax.bitwise_xor(me, s), AT:PIECE, :].astype(F32)
         src = 2.0 * meta[0:1, 0:ES] + meta[0:1, ES : 2 * ES]
         dst = 2.0 * meta[1:2, 0:ES] + meta[1:2, ES : 2 * ES]
         ec = meta[15:16, 128:256]
@@ -221,7 +242,7 @@
     x = h_s[...].astype(F32) + out
     atom_energy = jnp.sum(x * we, axis=1, keepdims=True)
     member = jnp.where(
-        lax.broadcasted_iota(jnp.int32, (ATOMS, 128), 1).astype(F32) == gid_col, 1.0, 0.0
+        lax.broadcasted_iota(jnp.int32, (ATOMS, 16), 1).astype(F32) == gid_col, 1.0, 0.0
     )
     energy_ref[...] = jnp.sum(member * atom_energy, axis=0, keepdims=True)
     cot = jnp.sum(member * ecot_ref[...], axis=1, keepdims=True)
@@ -282,7 +303,9 @@
         cot_s[pl.ds(own, AT), 0:1] * we + nt(s_src, ws_ref[...]) + nt(s_dst, wd_ref[...])
     )
     pos = nt(dv_s[...], ohd_own) - nt(dv_s[...], ohs_own)
-    pos_out_ref[...] = pos[0:3] + pos[3:6]
+    pos = pos[0:3] + pos[3:6]
+    for i in range(3):
+        pos_out_ref[i] = pos[i : i + 1]
 
     group = lax.div(me, 4)
     block = pl.ds(pl.multiple_of(lax.rem(me, 4) * 128, 128), 128)
@@ -301,19 +324,20 @@
 
     r_s[...] = nn(bt_s[pl.ds(pl.multiple_of(me * 16, 16), 16), :], drad_s[...])
     ge = ge_s[:, block]
-    for d in range(32):
-        rows, cols = 16 * (d // 4), slice(128 * (d % 4), 128 * (d % 4) + 128)
-        two = 2 * (d // 4)
-        pay_ref[d] = jnp.concatenate(
-            [
-                a_s[rows : rows + 16, cols],
-                b_s[rows : rows + 16, cols],
-                r_s[two : two + 2, cols],
-                ge,
-                jnp.zeros((5, 128), F32),
-            ],
-            axis=0,
-        ).astype(BF)
+    for u in range(4):
+        for v in range(4):
+            cols = slice(128 * v, 128 * v + 128)
+            chunk = jnp.concatenate(
+                [
+                    a_s[32 * u : 32 * u + 32, cols],
+                    b_s[32 * u : 32 * u + 32, cols],
+                    r_s[4 * u : 4 * u + 4, cols],
+                    ge,
+                    jnp.zeros((CH - 69, 128), F32),
+                ],
+                axis=0,
+            )
+            pay_ref[lax.rem(u - my_u + 4, 4), lax.rem(v - my_v + 4, 4)] = chunk.astype(BF)
 
 
 def batch(me, gat, ws, wd, wr, wt, wo, we, ecot):
@@ -323,12 +347,12 @@
     return pl.pallas_call(
         main_kernel,
         out_shape=(
-            jax.ShapeDtypeStruct((1, 128), F32),
-            jax.ShapeDtypeStruct((3, AT), F32),
+            jax.ShapeDtypeStruct((1, 16), F32),
+            jax.ShapeDtypeStruct((3, 1, AT), F32),
             jax.ShapeDtypeStruct((AT, D), F32),
-            jax.ShapeDtypeStruct((32, CH, 128), BF),
+            jax.ShapeDtypeStruct((4, 4, CH, 128), BF),
         ),
-        in_specs=[sm] + [vm] * 8,
+        in_specs=[sm, vm] + [pl.BlockSpec(memory_space=pl.ANY)] * 5 + [vm] * 2,
         out_specs=(vm, vm, vm, vm),
         scratch_shapes=[
             V((ATOMS, D), BF),
@@ -357,81 +381,76 @@
             V((BLK, D), F32),
             V((BLK, D), F32),
             V((16, D), F32),
+            V((D, D), BF),
+            V((D, D), BF),
+            V((K, D), BF),
+            V((D, D), BF),
+            V((D, D), BF),
+            pltpu.SemaphoreType.DMA((5,)),
         ],
         compiler_params=pltpu.CompilerParams(vmem_limit_bytes=50 * 1024 * 1024),
         name="batch",
     )(me, gat, ws, wd, wr, wt, wo, we, ecot)
 
 
-def sum_kernel(in_ref, out_ref):
-    total = in_ref[0].astype(F32)
-    for d in range(1, 32):
-        total = total + in_ref[d].astype(F32)
-    out_ref[...] = total.astype(BF)
-
-
-def chunk_sum(x):
-    vm = pl.BlockSpec(memory_space=pltpu.VMEM)
-    return pl.pallas_call(
-        sum_kernel,
-        out_shape=jax.ShapeDtypeStruct((CH, 128), BF),
-        in_specs=[vm],
-        out_specs=vm,
-        name="chunk_sum",
-    )(x)
-
-
-def place_kernel(me_ref, own_ref, other_ref, gs_ref, gd_ref, gr_ref, gt_ref, go_ref, ge_ref, pairs):
-    z, x, y, core = me_ref[0], me_ref[1], me_ref[2], me_ref[3]
-
+def place_kernel(me_ref, own_ref, other_ref, gs_ref, gd_ref, gr_ref, gt_ref, go_ref, ge_ref, first, second, low, sems):
+    x, y, zl, core = me_ref[0], me_ref[1], me_ref[2], me_ref[3]
     for c, ref in ((0, own_ref), (1, other_ref)):
-
-        def body(i, carry, c=c, ref=ref):
-            kx, ky, kz = lax.div(i, 32), lax.rem(lax.div(i, 8), 4), lax.rem(i, 8)
-            px = lax.rem(x - kx + 4, 4)
-            py = lax.rem(y - ky + 4, 4)
-            pz = lax.rem(z - kz + 8, 8)
-            pc = lax.rem(core + c, 2)
-            d = lax.div(pz, 4) * 16 + px * 4 + py
-            g = lax.rem(pz, 4) * 2 + pc
-            tile = ref[i].astype(F32)
-            cols = pl.ds(pl.multiple_of(lax.rem(d, 4) * 128, 128), 128)
-            high = lax.div(d, 4)
-            rows = pl.ds(pl.multiple_of(lax.rem(g, 4) * 128 + high * 16, 16), 16)
-
-            @pl.when(g < 4)
-            def _():
-                gs_ref[rows, cols] = tile[0:16]
-                gt_ref[rows, cols] = tile[16:32]
-
-            @pl.when(g >= 4)
-            def _():
-                gd_ref[rows, cols] = tile[0:16]
-                go_ref[rows, cols] = tile[16:32]
-
-            pairs[g * 8 + high, :, cols] = tile[32:40]
-
-            @pl.when((g < 4) & (d == 0))
-            def _():
-                ge_ref[:, pl.ds(pl.multiple_of(lax.rem(g, 4) * 128, 128), 128)] = tile[34:35]
-
+        pc = core ^ c
+        my_u = jnp.where(pc == 0, x, y)
+        my_v = jnp.where(pc == 0, y, x)
+
+        def body(i, carry, pc=pc, my_u=my_u, my_v=my_v, ref=ref):
+            u = lax.rem(my_u - lax.div(i, 4) + 4, 4)
+            v = lax.rem(my_v - lax.rem(i, 4) + 4, 4)
+            cols = pl.ds(pl.multiple_of(v * 128, 128), 128)
+            for kz in range(4):
+                g = (zl ^ kz) * 2 + pc
+                tile = ref[4 * i + kz].astype(F32)
+                rows = pl.ds(pl.multiple_of(g * 128 + u * 32, 32), 32)
+                first[rows, cols] = tile[0:32]
+                second[rows, cols] = tile[32:64]
+                low[g * 4 + u, :, cols] = tile[64:72]
             return carry
 
-        lax.fori_loop(0, 128, body, 0)
-    for i in range(K // 2):
-        gr_ref[2 * i : 2 * i + 2, :] = pairs[i, 0:2, :]
+        lax.fori_loop(0, 16, body, 0)
+    copies = [
+        pltpu.make_async_copy(near, far, sems.at[i])
+        for i, (near, far) in enumerate(
+            (
+                (first.at[0:D], gs_ref),
+                (first.at[D : 2 * D], gd_ref),
+                (second.at[0:D], gt_ref),
+                (second.at[D : 2 * D], go_ref),
+            )
+        )
+    ]
+    for copy in copies:
+        copy.start()
+    for i in range(K // 4):
+        gr_ref[4 * i : 4 * i + 4, :] = low[i, 0:4, :]
+    for g in range(4):
+        ge_ref[:, 128 * g : 128 * (g + 1)] = low[4 * g, 4:5, 0:128]
+    for copy in copies:
+        copy.wait()
 
 
 def place(where, own, other):
     vm = pl.BlockSpec(memory_space=pltpu.VMEM)
     sm = pl.BlockSpec(memory_space=pltpu.SMEM)
+    far = pl.BlockSpec(memory_space=pl.ANY)
     big = jax.ShapeDtypeStruct((D, D), F32)
     return pl.pallas_call(
         place_kernel,
         out_shape=(big, big, jax.ShapeDtypeStruct((K, D), F32), big, big, jax.ShapeDtypeStruct((1, D), F32)),
         in_specs=[sm, vm, vm],
-        out_specs=(vm,) * 6,
-        scratch_shapes=[pltpu.VMEM((K // 2, 8, D), F32)],
+        out_specs=(far, far, vm, far, far, vm),
+        scratch_shapes=[
+            pltpu.VMEM((2 * D, D), F32),
+            pltpu.VMEM((2 * D, D), F32),
+            pltpu.VMEM((K // 4, 8, D), F32),
+            pltpu.SemaphoreType.DMA((4,)),
+        ],
         compiler_params=pltpu.CompilerParams(vmem_limit_bytes=40 * 1024 * 1024),
         name="place",
     )(where, own, other)
@@ -444,28 +463,34 @@
             for y in range(4):
                 for zl in range(4):
                     for c in range(2):
-                        z = zh * 4 + zl
-                        z2, x2, y2, c2 = fn(z, x, y, c)
+                        u, v = (x, y) if c == 0 else (y, x)
+                        zh2, u2, v2, zl2, c2 = fn(zh, u, v, zl, c)
+                        x2, y2 = (u2, v2) if c == 0 else (v2, u2)
                         here = (zh * 16 + x * 4 + y) * 8 + zl * 2 + c
-                        there = ((z2 // 4) * 16 + x2 * 4 + y2) * 8 + (z2 % 4) * 2 + c2
+                        there = (zh2 * 16 + x2 * 4 + y2) * 8 + zl2 * 2 + c2
                         pairs.append((here, there))
     return pairs
 
 
-def rotate(v, axis, k):
-    if axis == "z":
-        fn = lambda z, x, y, c: ((z + k) % 8, x, y, c)
-    elif axis == "x":
-        fn = lambda z, x, y, c: (z, (x + k) % 4, y, c)
-    elif axis == "y":
-        fn = lambda z, x, y, c: (z, x, (y + k) % 4, c)
-    else:
-        fn = lambda z, x, y, c: (z, x, y, 1 - c)
-    return lax.ppermute(v, AXES, moves(fn))
-
-
-def spread(v, axis, n):
-    return jnp.concatenate([v] + [rotate(v, axis, k) for k in range(1, n)], axis=0)
+def shift(value, zh=0, u=0, v=0, zl=0, c=0):
+    def fn(zh_, u_, v_, zl_, c_):
+        return zh_ ^ zh, (u_ + u) % 4, (v_ + v) % 4, zl_ ^ zl, c_ ^ c
+
+    return lax.ppermute(value, AXES, moves(fn))
+
+
+def join(*parts):
+    return jnp.concatenate(parts, axis=0)
+
+
+ORDER = (1, 3, 2)
+
+
+def total(parts):
+    result = parts[0].astype(F32)
+    for part in parts[1:]:
+        result = result + part.astype(F32)
+    return result
 
 
 def per_device(
@@ -487,11 +512,14 @@
     energy_cot,
 ):
     dp, graph = lax.axis_index("dp"), lax.axis_index("graph")
-    me = graph.reshape(1).astype(jnp.int32)
+    x, y = lax.rem(lax.div(dp, 4), 4), lax.rem(dp, 4)
+    zl, core = lax.div(graph, 2), lax.rem(graph, 2)
+    u, v = jnp.where(core == 0, x, y), jnp.where(core == 0, y, x)
+    me = jnp.stack([graph, u, v]).astype(jnp.int32)
     piece = pack(
         me,
         node_feats[0],
-        positions[0],
+        jnp.swapaxes(positions, 0, 1),
         edge_src,
         edge_dst,
         edge_count,
@@ -499,38 +527,24 @@
         trip_out,
         trip_count,
         graph_ids,
+    )[None]
+    pair = join(piece, shift(piece, c=1))
+    gathered = join(pair, *[shift(pair, zl=k) for k in (1, 2, 3)])
+    energy, pos_grad, node_grad, payload = batch(
+        me, gathered, w_src, w_dst, w_radial, w_trip, w_out, w_energy.reshape(1, D), energy_cot
     )
-    gathered = lax.all_gather(piece, "graph", axis=0, tiled=False)
-    ecot = jnp.pad(energy_cot, ((0, 0), (0, 128 - energy_cot.shape[1])))
-    energy, pos_grad, node_grad, payload = batch(
-        me, gathered, w_src, w_dst, w_radial, w_trip, w_out, w_energy.reshape(1, D), ecot
-    )
-    arrived = lax.all_to_all(payload, "dp", 0, 0, tiled=True)
-    chunk = chunk_sum(arrived)
-    part = spread(chunk[None], "z", 8)
-    part = spread(part, "y", 4)
-    part = spread(part, "x", 4)
-    other = rotate(part, "core", 1)
-    where = jnp.stack(
-        [
-            lax.div(dp, 16) * 4 + lax.div(graph, 2),
-            lax.rem(lax.div(dp, 4), 4),
-            lax.rem(dp, 4),
-            lax.rem(graph, 2),
-        ]
-    ).astype(jnp.int32)
+    part = total([payload[0]] + [shift(payload[k], u=k) for k in ORDER]).astype(BF)
+    part = total([part[0]] + [shift(part[k], v=k) for k in ORDER]).astype(BF)
+    part = (part.astype(F32) + shift(part, zh=1).astype(F32)).astype(BF)[None]
+    part = join(part, *[shift(part, zl=k) for k in (1, 2, 3)])
+    back = [shift(part, v=k) for k in ORDER]
+    part = join(part, back[0], back[2], back[1])
+    back = [shift(part, u=k) for k in ORDER]
+    part = join(part, back[0], back[2], back[1])
+    other = shift(part, c=1)
+    where = jnp.stack([x, y, zl, core]).astype(jnp.int32)
     gs, gd, gr, gt, go, ge = place(where, part, other)
-    return (
-        energy[:, 0 : energy_cot.shape[1]],
-        pos_grad[None],
-        node_grad[None],
-        gs,
-        gd,
-        gr,
-        gt,
-        go,
-        ge.reshape(D),
-    )
+    return (energy, jnp.swapaxes(pos_grad, 0, 1), node_grad[None], gs, gd, gr, gt, go, ge.reshape(D))
 
 
 def solution(mesh):

time: 155 us -> 127 us (0.82)
  blocking collectives: 42.8 us -> 0 us
  waiting for transfers between devices: 22.9 us -> 40.2 us
  starting transfers between devices: 28.6 us -> 40.9 us
  Pallas kernels: 48.3 us -> 38.8 us
  local copies, waits for them, and re-layouts: 9.31 us -> 2.98 us
  other arithmetic: 0.08 us -> 1.66 us
    all_to_all x1 -> x0, blocking collectives: 24.6 us -> none  [per_device(): arrived = lax.all_to_all(payload, 'dp', 0, 0, tiled=True)]
    all_gather x1 -> x0, blocking collectives: 18.3 us -> none  [per_device(): gathered = lax.all_gather(piece, 'graph', axis=0, tiled=False)]
    ppermute x14 -> x21, waiting for transfers between devices: 22.9 us -> 40.2 us  [shift(): return lax.ppermute(value, AXES, moves(fn))]
    ppermute x14 -> x21, starting transfers between devices: 28.6 us -> 40.9 us  [shift(): return lax.ppermute(value, AXES, moves(fn))]
    pallas_call x1, Pallas kernels: 13.9 us -> 4.28 us  [place(): pl.pallas_call(place_kernel, out_shape=(big, big, jax.ShapeDtypeStruct((K...]
    unnamed x24 -> x26, local copies, waits for them, and re-layouts: 7.88 us -> 2.18 us
    pallas_call x2 -> x1, Pallas kernels: 32.8 us -> 32.2 us  [batch(): pl.pallas_call(main_kernel, out_shape=(jax.ShapeDtypeStruct((1, 16), F32)...]
  transfers between devices with their start and end apart: 14 -> 21, of which waited for: 8 -> 14; matrix products, arithmetic and copies ran while one was open for 1% -> 1% of each run, Pallas kernels for 0% -> 0%
where the time goes in v2:
time: 127 us
  starting transfers between devices  40.9 us (32%)
  waiting for transfers between devices  40.2 us (32%)
  Pallas kernels  38.8 us (31%)
  local copies, waits for them, and re-layouts  2.98 us (2%)
  between operations  2.5 us (2%)
  other arithmetic  1.66 us (1%)
    ppermute x21, starting transfers between devices, shift(): return lax.ppermute(value, AXES, moves(fn))  40.9 us
    ppermute x21, waiting for transfers between devices, shift(): return lax.ppermute(value, AXES, moves(fn))  40.2 us
    pallas_call x1, Pallas kernels, batch(): pl.pallas_call(main_kernel, out_shape=(jax.ShapeDtypeStruct((1, 16), F32)...  32.2 us
    pallas_call x1, Pallas kernels, place(): pl.pallas_call(place_kernel, out_shape=(big, big, jax.ShapeDtypeStruct((K...  4.28 us
  transfers between devices with their start and end apart: 21, of which 14 were waited for; matrix products, arithmetic and copies ran while one was open for 1% of the time, Pallas kernels for 0%

profile of v2, /device:TPU:1, one launch (start us, length us, event | category | flops | bytes accessed | tf_op | source)
XLA Modules:
  0.0 127.0 jit_solution(10084206667559225902)
XLA Ops:
  0.6 0.0 copy-start.6
  0.7 0.0 copy-start.2
  0.7 0.0 copy-start.4
  0.7 0.0 copy-start.1
  0.7 0.0 copy-start
  2.1 0.6 pad_add_fusion.me_ref
  2.7 0.0 copy-start.5
  2.7 2.3 %pack.1 = bf16[80,512]{1,0:T(8,128)(2,1)} custom-call(s32[3]{0:T(128)} %pad_add_fusion.me_ref, bf16[64,512]{1,0:T(8,128)(2,1)} %bitcast.39, f32[3,1,64]{2,1,0:T(1,128)} %bitcast.40, s32[1,256]{1,0:T(1,128)} %src_ref.1, s32[1,256]{1,0:T(1,128)} %dst_ref.1, s32[1,1]{1,0:T(1,128)S(6)} %copy.44.ec_ref, s32[1,1024]{1,0:T(1,128)} %tin_ref.1, s32[1,1024]{1,0:T(1,128)} %tout_ref.1, ...), custom_call_target="tpu_custom_call" | custom-call | tf_op jit(solution)/shard_map/pack/pallas_call | solution.py:77
  5.0 3.3 %collective-permute-start = (bf16[1,80,512]{2,1,0:T(8,128)(2,1)}, bf16[1,80,512]{2,1,0:T(8,128)(2,1)S(1)}, u32[]{:S(2)}, u32[]{:S(2)}) collective-permute-start(bf16[1,80,512]{2,1,0:T(8,128)(2,1)} %bitcast.37), channel_id=1, source_target_pairs={{0,1},{1,0},{2,3},{3,2},{4,5},{5,4},{6,7},{7,6},{8,9},{9,8},{10,11... | collective-permute-start | bytes 245768 | tf_op jit(solution)/shard_map/ppermute | solution.py:479
  8.4 1.1 collective-permute-done
  9.5 0.9 pad_maximum_fusion
  10.4 0.1 collective-permute-start.1
  10.5 0.9 constant_dynamic-update-slice_fusion.4
  11.4 0.7 reshape.28.we_ref
  12.1 2.6 %collective-permute-start.3 = (bf16[2,80,512]{2,1,0:T(8,128)(2,1)S(1)}, bf16[2,80,512]{2,1,0:T(8,128)(2,1)S(1)}, u32[]{:S(2)}, u32[]{:S(2)}) collective-permute-start(bf16[2,80,512]{2,1,0:T(8,128)(2,1)S(1)} %pad_maximum_fusion), channel_id=1, source_target_pairs={{0,6},{1,7},{2,4},{3,5},{4,2},{5,3},{6,0},{7,1},{8,14},{9,15},{10,... | collective-permute-start | bytes 491528 | tf_op jit(solution)/shard_map/ppermute | solution.py:479
  14.7 0.3 collective-permute-start.2
  15.0 1.0 collective-permute-done.1
  15.9 13.5 %collective-permute-done.2 = bf16[2,80,512]{2,1,0:T(8,128)(2,1)S(1)} collective-permute-done((bf16[2,80,512]{2,1,0:T(8,128)(2,1)S(1)}, bf16[2,80,512]{2,1,0:T(8,128)(2,1)S(1)}, u32[]{:S(2)}, u32[]{:S(2)}) %collective-permute-start.2) | collective-permute-done | bytes 163872 | tf_op jit(solution)/shard_map/ppermute | solution.py:479
  29.4 0.0 collective-permute-done.3
  29.5 0.0 copy-done.6
  29.5 0.0 copy-done.2
  29.5 0.0 copy-done.4
  29.5 0.0 copy-done.1
  29.5 0.0 copy-done
  29.5 0.0 copy-done.5
  29.5 0.0 copy-start.3
  29.5 1.0 copy-done.3
  30.6 32.2 %batch.1 = (f32[1,16]{1,0:T(1,128)}, f32[3,1,64]{2,1,0:T(1,128)}, f32[64,512]{1,0:T(8,128)}, bf16[4,4,80,128]{3,2,1,0:T(8,128)(2,1)S(1)}) custom-call(s32[3]{0:T(128)S(1)} %copy-done.5, bf16[8,80,512]{2,1,0:T(8,128)(2,1)S(1)} %constant_dynamic-update-slice_fusion.gat_ref, bf16[512,512]{1,0:T(8,128)(2,1)S(1)} %copy-done, bf16[512,512]{1,0:T(8,128)(2,1)S(1)} %copy-done.1, ...), custom_call_target="tpu_custom_call" | custom-call | tf_op jit(solution)/shard_map/batch/pallas_call | solution.py:347
  62.8 1.4 %collective-permute-start.4 = (bf16[4,80,128]{2,1,0:T(8,128)(2,1)S(1)}, bf16[4,80,128]{2,1,0:T(8,128)(2,1)S(1)}, u32[]{:S(2)}, u32[]{:S(2)}) collective-permute-start(bf16[4,80,128]{2,1,0:T(8,128)(2,1)S(1)} %get-tuple-element.31), channel_id=1, source_target_pairs={{0,32},{1,9},{2,34},{3,11},{4,36},{5,13},{6,38},{7,15},{8,40},{9,1... | collective-permute-start | bytes 245768 | tf_op jit(solution)/shard_map/ppermute | solution.py:479
  64.3 2.6 %collective-permute-start.6 = (bf16[4,80,128]{2,1,0:T(8,128)(2,1)S(1)}, bf16[4,80,128]{2,1,0:T(8,128)(2,1)S(1)}, u32[]{:S(2)}, u32[]{:S(2)}) collective-permute-start(bf16[4,80,128]{2,1,0:T(8,128)(2,1)S(1)} %get-tuple-element.32), channel_id=1, source_target_pairs={{0,64},{1,17},{2,66},{3,19},{4,68},{5,21},{6,70},{7,23},{8,72},{9,... | collective-permute-start | bytes 245768 | tf_op jit(solution)/shard_map/ppermute | solution.py:479
  66.9 1.1 collective-permute-start.5
  68.0 0.0 collective-permute-done.4
  68.0 1.6 %collective-permute-done.6 = bf16[4,80,128]{2,1,0:T(8,128)(2,1)S(1)} collective-permute-done((bf16[4,80,128]{2,1,0:T(8,128)(2,1)S(1)}, bf16[4,80,128]{2,1,0:T(8,128)(2,1)S(1)}, u32[]{:S(2)}, u32[]{:S(2)}) %collective-permute-start.6) | collective-permute-done | bytes 81952 | tf_op jit(solution)/shard_map/ppermute | solution.py:479
  69.6 0.9 collective-permute-done.5
  70.5 1.5 %collective-permute-start.7 = (bf16[80,128]{1,0:T(8,128)(2,1)S(1)}, bf16[80,128]{1,0:T(8,128)(2,1)S(1)}, u32[]{:S(2)}, u32[]{:S(2)}) collective-permute-start(bf16[80,128]{1,0:T(8,128)(2,1)S(1)} %get-tuple-element.40), channel_id=1, source_target_pairs={{0,8},{1,33},{2,10},{3,35},{4,12},{5,37},{6,14},{7,39},{8,16},{9,4... | collective-permute-start | bytes 61448 | tf_op jit(solution)/shard_map/ppermute | solution.py:479
  72.0 2.1 %collective-permute-start.9 = (bf16[80,128]{1,0:T(8,128)(2,1)S(1)}, bf16[80,128]{1,0:T(8,128)(2,1)S(1)}, u32[]{:S(2)}, u32[]{:S(2)}) collective-permute-start(bf16[80,128]{1,0:T(8,128)(2,1)S(1)} %get-tuple-element.41), channel_id=1, source_target_pairs={{0,16},{1,65},{2,18},{3,67},{4,20},{5,69},{6,22},{7,71},{8,24},{9,... | collective-permute-start | bytes 61448 | tf_op jit(solution)/shard_map/ppermute | solution.py:479
  74.2 1.5 %collective-permute-start.8 = (bf16[80,128]{1,0:T(8,128)(2,1)S(1)}, bf16[80,128]{1,0:T(8,128)(2,1)S(1)}, u32[]{:S(2)}, u32[]{:S(2)}) collective-permute-start(bf16[80,128]{1,0:T(8,128)(2,1)S(1)} %get-tuple-element.42), channel_id=1, source_target_pairs={{0,24},{1,97},{2,26},{3,99},{4,28},{5,101},{6,30},{7,103},{8,0},{9... | collective-permute-start | bytes 61448 | tf_op jit(solution)/shard_map/ppermute | solution.py:479
  75.6 0.0 collective-permute-done.7
  75.6 0.5 collective-permute-done.9
  76.2 0.6 collective-permute-done.8
  76.8 5.0 %collective-permute-start.10 = (bf16[80,128]{1,0:T(8,128)(2,1)S(1)}, bf16[80,128]{1,0:T(8,128)(2,1)S(1)}, u32[]{:S(2)}, u32[]{:S(2)}) collective-permute-start(bf16[80,128]{1,0:T(8,128)(2,1)S(1)} %fusion.5), channel_id=1, source_target_pairs={{0,128},{1,129},{2,130},{3,131},{4,132},{5,133},{6,134},{7,135},{8... | collective-permute-start | bytes 61448 | tf_op jit(solution)/shard_map/ppermute | solution.py:479
  81.8 1.6 %collective-permute-done.10 = bf16[80,128]{1,0:T(8,128)(2,1)S(1)} collective-permute-done((bf16[80,128]{1,0:T(8,128)(2,1)S(1)}, bf16[80,128]{1,0:T(8,128)(2,1)S(1)}, u32[]{:S(2)}, u32[]{:S(2)}) %collective-permute-start.10) | collective-permute-done | bytes 20512 | tf_op jit(solution)/shard_map/ppermute | solution.py:479
  83.5 2.6 %collective-permute-start.13 = (bf16[1,80,128]{2,1,0:T(8,128)(2,1)S(1)}, bf16[1,80,128]{2,1,0:T(8,128)(2,1)S(1)}, u32[]{:S(2)}, u32[]{:S(2)}) collective-permute-start(bf16[1,80,128]{2,1,0:T(8,128)(2,1)S(1)} %get-tuple-element.30), channel_id=1, source_target_pairs={{0,6},{1,7},{2,4},{3,5},{4,2},{5,3},{6,0},{7,1},{8,14},{9,15},{10,... | collective-permute-start | bytes 61448 | tf_op jit(solution)/shard_map/ppermute | solution.py:479
  86.1 0.0 collective-permute-start.12
  86.1 1.0 collective-permute-start.11
  87.1 1.2 collective-permute-done.13
  88.3 1.5 %collective-permute-done.12 = bf16[1,80,128]{2,1,0:T(8,128)(2,1)S(1)} collective-permute-done((bf16[1,80,128]{2,1,0:T(8,128)(2,1)S(1)}, bf16[1,80,128]{2,1,0:T(8,128)(2,1)S(1)}, u32[]{:S(2)}, u32[]{:S(2)}) %collective-permute-start.12) | collective-permute-done | bytes 20512 | tf_op jit(solution)/shard_map/ppermute | solution.py:479
  89.7 0.0 collective-permute-done.11
  89.8 2.4 %collective-permute-start.16 = (bf16[4,80,128]{2,1,0:T(8,128)(2,1)S(1)}, bf16[4,80,128]{2,1,0:T(8,128)(2,1)S(1)}, u32[]{:S(2)}, u32[]{:S(2)}) collective-permute-start(bf16[4,80,128]{2,1,0:T(8,128)(2,1)S(1)} %pad_maximum_fusion.1), channel_id=1, source_target_pairs={{0,24},{1,97},{2,26},{3,99},{4,28},{5,101},{6,30},{7,103},{8,0},{9... | collective-permute-start | bytes 245768 | tf_op jit(solution)/shard_map/ppermute | solution.py:479
  92.2 0.0 collective-permute-start.15
  92.2 0.7 collective-permute-start.14
  92.9 4.7 %collective-permute-done.14 = bf16[4,80,128]{2,1,0:T(8,128)(2,1)S(1)} collective-permute-done((bf16[4,80,128]{2,1,0:T(8,128)(2,1)S(1)}, bf16[4,80,128]{2,1,0:T(8,128)(2,1)S(1)}, u32[]{:S(2)}, u32[]{:S(2)}) %collective-permute-start.14) | collective-permute-done | bytes 81952 | tf_op jit(solution)/shard_map/ppermute | solution.py:479
  97.6 0.0 collective-permute-done.15
  97.7 0.0 collective-permute-done.16
  97.7 0.1 collective-permute-start.17
  97.8 3.0 %collective-permute-start.18 = (bf16[16,80,128]{2,1,0:T(8,128)(2,1)S(1)}, bf16[16,80,128]{2,1,0:T(8,128)(2,1)S(1)}, u32[]{:S(2)}, u32[]{:S(2)}) collective-permute-start(bf16[16,80,128]{2,1,0:T(8,128)(2,1)S(1)} %get-tuple-element.34), channel_id=1, source_target_pairs={{0,64},{1,17},{2,66},{3,19},{4,68},{5,21},{6,70},{7,23},{8,72},{9,... | collective-permute-start | bytes 983048 | tf_op jit(solution)/shard_map/ppermute | solution.py:479
  100.8 0.3 collective-permute-start.19
  101.1 5.6 %collective-permute-done.17 = bf16[16,80,128]{2,1,0:T(8,128)(2,1)S(1)} collective-permute-done((bf16[16,80,128]{2,1,0:T(8,128)(2,1)S(1)}, bf16[16,80,128]{2,1,0:T(8,128)(2,1)S(1)}, u32[]{:S(2)}, u32[]{:S(2)}) %collective-permute-start.17) | collective-permute-done | bytes 327712 | tf_op jit(solution)/shard_map/ppermute | solution.py:479
  106.7 3.8 %collective-permute-done.18 = bf16[16,80,128]{2,1,0:T(8,128)(2,1)S(1)} collective-permute-done((bf16[16,80,128]{2,1,0:T(8,128)(2,1)S(1)}, bf16[16,80,128]{2,1,0:T(8,128)(2,1)S(1)}, u32[]{:S(2)}, u32[]{:S(2)}) %collective-permute-start.18) | collective-permute-done | bytes 327712 | tf_op jit(solution)/shard_map/ppermute | solution.py:479
  110.6 0.0 collective-permute-done.19
  110.7 9.3 %collective-permute-start.20 = (bf16[64,80,128]{2,1,0:T(8,128)(2,1)S(1)}, bf16[64,80,128]{2,1,0:T(8,128)(2,1)S(1)}, u32[]{:S(2)}, u32[]{:S(2)}) collective-permute-start(bf16[64,80,128]{2,1,0:T(8,128)(2,1)S(1)} %constant_dynamic-update-slice_fusion.12.own_ref), channel_id=1, source_target_pairs={{0,1},{1,0},{2,3},{3,2},{4,5},{5,4},{6,7},{7,6},{8,9},{9,8},{10,11... | collective-permute-start | bytes 3932168 | tf_op jit(solution)/shard_map/ppermute | solution.py:479
  119.9 0.1 pad_add_fusion.1.me_ref
  120.0 2.6 %collective-permute-done.20.other_ref = bf16[64,80,128]{2,1,0:T(8,128)(2,1)S(1)} collective-permute-done((bf16[64,80,128]{2,1,0:T(8,128)(2,1)S(1)}, bf16[64,80,128]{2,1,0:T(8,128)(2,1)S(1)}, u32[]{:S(2)}, u32[]{:S(2)}) %collective-permute-start.20) | collective-permute-done | bytes 1310752 | tf_op jit(solution)/shard_map/ppermute | solution.py:479
  122.6 4.3 %place.1 = (f32[512,512]{1,0:T(8,128)}, f32[512,512]{1,0:T(8,128)}, f32[128,512]{1,0:T(8,128)}, f32[512,512]{1,0:T(8,128)}, f32[512,512]{1,0:T(8,128)}, /*index=5*/f32[1,512]{1,0:T(1,128)}) custom-call(s32[4]{0:T(128)S(1)} %pad_add_fusion.1.me_ref, bf16[64,80,128]{2,1,0:T(8,128)(2,1)S(1)} %constant_dynamic-update-slice_fusion.12.own_ref, ...), custom_call_target="tpu_custom_call" | custom-call | tf_op jit(solution)/shard_map/place/pallas_call | solution.py:443
  (20 shorter events, 0.4 us)
Async XLA Ops:
  0.6 28.8 %copy-start.6 = (f32[1,16]{1,0:T(1,128)S(1)}, f32[1,16]{1,0:T(1,128)}, u32[]{:S(2)}) copy-start(f32[1,16]{1,0:T(1,128)} %ecot_ref.1) | copy-start | bytes 196
  0.7 28.8 %copy-start.2 = (bf16[512,512]{1,0:T(8,128)(2,1)S(1)}, bf16[512,512]{1,0:T(8,128)(2,1)}, u32[]{:S(2)}) copy-start(bf16[512,512]{1,0:T(8,128)(2,1)} %wt_hbm.1) | copy-start | bytes 1572868
  0.7 28.8 %copy-start.4 = (bf16[128,512]{1,0:T(8,128)(2,1)S(1)}, bf16[128,512]{1,0:T(8,128)(2,1)}, u32[]{:S(2)}) copy-start(bf16[128,512]{1,0:T(8,128)(2,1)} %wr_hbm.1) | copy-start | bytes 393220
  0.7 28.8 %copy-start.1 = (bf16[512,512]{1,0:T(8,128)(2,1)S(1)}, bf16[512,512]{1,0:T(8,128)(2,1)}, u32[]{:S(2)}) copy-start(bf16[512,512]{1,0:T(8,128)(2,1)} %wd_hbm.1) | copy-start | bytes 1572868
  0.7 28.8 %copy-start = (bf16[512,512]{1,0:T(8,128)(2,1)S(1)}, bf16[512,512]{1,0:T(8,128)(2,1)}, u32[]{:S(2)}) copy-start(bf16[512,512]{1,0:T(8,128)(2,1)} %ws_hbm.1) | copy-start | bytes 1572868
  2.7 26.8 %copy-start.5 = (s32[3]{0:T(128)S(1)}, s32[3]{0:T(128)}, u32[]{:S(2)}) copy-start(s32[3]{0:T(128)} %pad_add_fusion.me_ref) | copy-start | bytes 40
  5.0 4.5 %collective-permute-start = (bf16[1,80,512]{2,1,0:T(8,128)(2,1)}, bf16[1,80,512]{2,1,0:T(8,128)(2,1)S(1)}, u32[]{:S(2)}, u32[]{:S(2)}) collective-permute-start(bf16[1,80,512]{2,1,0:T(8,128)(2,1)} %bitcast.37), channel_id=1, source_target_pairs={{0,1},{1,0},{2,3},{3,2},{4,5},{5,4},{6,7},{7,6},{8,9},{9,8},{10,11... | collective-permute-start | bytes 245768 | tf_op jit(solution)/shard_map/ppermute | solution.py:479
  10.4 5.5 %collective-permute-start.1 = (bf16[2,80,512]{2,1,0:T(8,128)(2,1)S(1)}, bf16[2,80,512]{2,1,0:T(8,128)(2,1)S(1)}, u32[]{:S(2)}, u32[]{:S(2)}) collective-permute-start(bf16[2,80,512]{2,1,0:T(8,128)(2,1)S(1)} %pad_maximum_fusion), channel_id=1, source_target_pairs={{0,2},{1,3},{2,0},{3,1},{4,6},{5,7},{6,4},{7,5},{8,10},{9,11},{10,... | collective-permute-start | bytes 491528 | tf_op jit(solution)/shard_map/ppermute | solution.py:479
  12.1 17.4 %collective-permute-start.3 = (bf16[2,80,512]{2,1,0:T(8,128)(2,1)S(1)}, bf16[2,80,512]{2,1,0:T(8,128)(2,1)S(1)}, u32[]{:S(2)}, u32[]{:S(2)}) collective-permute-start(bf16[2,80,512]{2,1,0:T(8,128)(2,1)S(1)} %pad_maximum_fusion), channel_id=1, source_target_pairs={{0,6},{1,7},{2,4},{3,5},{4,2},{5,3},{6,0},{7,1},{8,14},{9,15},{10,... | collective-permute-start | bytes 491528 | tf_op jit(solution)/shard_map/ppermute | solution.py:479
  14.7 14.7 %collective-permute-start.2 = (bf16[2,80,512]{2,1,0:T(8,128)(2,1)S(1)}, bf16[2,80,512]{2,1,0:T(8,128)(2,1)S(1)}, u32[]{:S(2)}, u32[]{:S(2)}) collective-permute-start(bf16[2,80,512]{2,1,0:T(8,128)(2,1)S(1)} %pad_maximum_fusion), channel_id=1, source_target_pairs={{0,4},{1,5},{2,6},{3,7},{4,0},{5,1},{6,2},{7,3},{8,12},{9,13},{10,... | collective-permute-start | bytes 491528 | tf_op jit(solution)/shard_map/ppermute | solution.py:479
  29.5 1.0 copy-start.3
  62.8 5.1 %collective-permute-start.4 = (bf16[4,80,128]{2,1,0:T(8,128)(2,1)S(1)}, bf16[4,80,128]{2,1,0:T(8,128)(2,1)S(1)}, u32[]{:S(2)}, u32[]{:S(2)}) collective-permute-start(bf16[4,80,128]{2,1,0:T(8,128)(2,1)S(1)} %get-tuple-element.31), channel_id=1, source_target_pairs={{0,32},{1,9},{2,34},{3,11},{4,36},{5,13},{6,38},{7,15},{8,40},{9,1... | collective-permute-start | bytes 245768 | tf_op jit(solution)/shard_map/ppermute | solution.py:479
  64.3 5.3 %collective-permute-start.6 = (bf16[4,80,128]{2,1,0:T(8,128)(2,1)S(1)}, bf16[4,80,128]{2,1,0:T(8,128)(2,1)S(1)}, u32[]{:S(2)}, u32[]{:S(2)}) collective-permute-start(bf16[4,80,128]{2,1,0:T(8,128)(2,1)S(1)} %get-tuple-element.32), channel_id=1, source_target_pairs={{0,64},{1,17},{2,66},{3,19},{4,68},{5,21},{6,70},{7,23},{8,72},{9,... | collective-permute-start | bytes 245768 | tf_op jit(solution)/shard_map/ppermute | solution.py:479
  66.9 3.6 %collective-permute-start.5 = (bf16[4,80,128]{2,1,0:T(8,128)(2,1)S(1)}, bf16[4,80,128]{2,1,0:T(8,128)(2,1)S(1)}, u32[]{:S(2)}, u32[]{:S(2)}) collective-permute-start(bf16[4,80,128]{2,1,0:T(8,128)(2,1)S(1)} %get-tuple-element.33), channel_id=1, source_target_pairs={{0,96},{1,25},{2,98},{3,27},{4,100},{5,29},{6,102},{7,31},{8,104},... | collective-permute-start | bytes 245768 | tf_op jit(solution)/shard_map/ppermute | solution.py:479
  70.5 5.1 %collective-permute-start.7 = (bf16[80,128]{1,0:T(8,128)(2,1)S(1)}, bf16[80,128]{1,0:T(8,128)(2,1)S(1)}, u32[]{:S(2)}, u32[]{:S(2)}) collective-permute-start(bf16[80,128]{1,0:T(8,128)(2,1)S(1)} %get-tuple-element.40), channel_id=1, source_target_pairs={{0,8},{1,33},{2,10},{3,35},{4,12},{5,37},{6,14},{7,39},{8,16},{9,4... | collective-permute-start | bytes 61448 | tf_op jit(solution)/shard_map/ppermute | solution.py:479
  72.0 4.1 %collective-permute-start.9 = (bf16[80,128]{1,0:T(8,128)(2,1)S(1)}, bf16[80,128]{1,0:T(8,128)(2,1)S(1)}, u32[]{:S(2)}, u32[]{:S(2)}) collective-permute-start(bf16[80,128]{1,0:T(8,128)(2,1)S(1)} %get-tuple-element.41), channel_id=1, source_target_pairs={{0,16},{1,65},{2,18},{3,67},{4,20},{5,69},{6,22},{7,71},{8,24},{9,... | collective-permute-start | bytes 61448 | tf_op jit(solution)/shard_map/ppermute | solution.py:479
  74.2 2.6 %collective-permute-start.8 = (bf16[80,128]{1,0:T(8,128)(2,1)S(1)}, bf16[80,128]{1,0:T(8,128)(2,1)S(1)}, u32[]{:S(2)}, u32[]{:S(2)}) collective-permute-start(bf16[80,128]{1,0:T(8,128)(2,1)S(1)} %get-tuple-element.42), channel_id=1, source_target_pairs={{0,24},{1,97},{2,26},{3,99},{4,28},{5,101},{6,30},{7,103},{8,0},{9... | collective-permute-start | bytes 61448 | tf_op jit(solution)/shard_map/ppermute | solution.py:479
  76.8 6.6 %collective-permute-start.10 = (bf16[80,128]{1,0:T(8,128)(2,1)S(1)}, bf16[80,128]{1,0:T(8,128)(2,1)S(1)}, u32[]{:S(2)}, u32[]{:S(2)}) collective-permute-start(bf16[80,128]{1,0:T(8,128)(2,1)S(1)} %fusion.5), channel_id=1, source_target_pairs={{0,128},{1,129},{2,130},{3,131},{4,132},{5,133},{6,134},{7,135},{8... | collective-permute-start | bytes 61448 | tf_op jit(solution)/shard_map/ppermute | solution.py:479
  83.5 4.8 %collective-permute-start.13 = (bf16[1,80,128]{2,1,0:T(8,128)(2,1)S(1)}, bf16[1,80,128]{2,1,0:T(8,128)(2,1)S(1)}, u32[]{:S(2)}, u32[]{:S(2)}) collective-permute-start(bf16[1,80,128]{2,1,0:T(8,128)(2,1)S(1)} %get-tuple-element.30), channel_id=1, source_target_pairs={{0,6},{1,7},{2,4},{3,5},{4,2},{5,3},{6,0},{7,1},{8,14},{9,15},{10,... | collective-permute-start | bytes 61448 | tf_op jit(solution)/shard_map/ppermute | solution.py:479
  86.1 3.7 %collective-permute-start.12 = (bf16[1,80,128]{2,1,0:T(8,128)(2,1)S(1)}, bf16[1,80,128]{2,1,0:T(8,128)(2,1)S(1)}, u32[]{:S(2)}, u32[]{:S(2)}) collective-permute-start(bf16[1,80,128]{2,1,0:T(8,128)(2,1)S(1)} %get-tuple-element.30), channel_id=1, source_target_pairs={{0,4},{1,5},{2,6},{3,7},{4,0},{5,1},{6,2},{7,3},{8,12},{9,13},{10,... | collective-permute-start | bytes 61448 | tf_op jit(solution)/shard_map/ppermute | solution.py:479
  86.1 3.7 %collective-permute-start.11 = (bf16[1,80,128]{2,1,0:T(8,128)(2,1)S(1)}, bf16[1,80,128]{2,1,0:T(8,128)(2,1)S(1)}, u32[]{:S(2)}, u32[]{:S(2)}) collective-permute-start(bf16[1,80,128]{2,1,0:T(8,128)(2,1)S(1)} %get-tuple-element.30), channel_id=1, source_target_pairs={{0,2},{1,3},{2,0},{3,1},{4,6},{5,7},{6,4},{7,5},{8,10},{9,11},{10,... | collective-permute-start | bytes 61448 | tf_op jit(solution)/shard_map/ppermute | solution.py:479
  89.8 7.9 %collective-permute-start.16 = (bf16[4,80,128]{2,1,0:T(8,128)(2,1)S(1)}, bf16[4,80,128]{2,1,0:T(8,128)(2,1)S(1)}, u32[]{:S(2)}, u32[]{:S(2)}) collective-permute-start(bf16[4,80,128]{2,1,0:T(8,128)(2,1)S(1)} %pad_maximum_fusion.1), channel_id=1, source_target_pairs={{0,24},{1,97},{2,26},{3,99},{4,28},{5,101},{6,30},{7,103},{8,0},{9... | collective-permute-start | bytes 245768 | tf_op jit(solution)/shard_map/ppermute | solution.py:479
  92.2 5.4 %collective-permute-start.15 = (bf16[4,80,128]{2,1,0:T(8,128)(2,1)S(1)}, bf16[4,80,128]{2,1,0:T(8,128)(2,1)S(1)}, u32[]{:S(2)}, u32[]{:S(2)}) collective-permute-start(bf16[4,80,128]{2,1,0:T(8,128)(2,1)S(1)} %pad_maximum_fusion.1), channel_id=1, source_target_pairs={{0,16},{1,65},{2,18},{3,67},{4,20},{5,69},{6,22},{7,71},{8,24},{9,... | collective-permute-start | bytes 245768 | tf_op jit(solution)/shard_map/ppermute | solution.py:479
  92.2 5.4 %collective-permute-start.14 = (bf16[4,80,128]{2,1,0:T(8,128)(2,1)S(1)}, bf16[4,80,128]{2,1,0:T(8,128)(2,1)S(1)}, u32[]{:S(2)}, u32[]{:S(2)}) collective-permute-start(bf16[4,80,128]{2,1,0:T(8,128)(2,1)S(1)} %pad_maximum_fusion.1), channel_id=1, source_target_pairs={{0,8},{1,33},{2,10},{3,35},{4,12},{5,37},{6,14},{7,39},{8,16},{9,4... | collective-permute-start | bytes 245768 | tf_op jit(solution)/shard_map/ppermute | solution.py:479
  97.7 9.0 %collective-permute-start.17 = (bf16[16,80,128]{2,1,0:T(8,128)(2,1)S(1)}, bf16[16,80,128]{2,1,0:T(8,128)(2,1)S(1)}, u32[]{:S(2)}, u32[]{:S(2)}) collective-permute-start(bf16[16,80,128]{2,1,0:T(8,128)(2,1)S(1)} %get-tuple-element.34), channel_id=1, source_target_pairs={{0,32},{1,9},{2,34},{3,11},{4,36},{5,13},{6,38},{7,15},{8,40},{9,1... | collective-permute-start | bytes 983048 | tf_op jit(solution)/shard_map/ppermute | solution.py:479
  97.8 12.7 %collective-permute-start.18 = (bf16[16,80,128]{2,1,0:T(8,128)(2,1)S(1)}, bf16[16,80,128]{2,1,0:T(8,128)(2,1)S(1)}, u32[]{:S(2)}, u32[]{:S(2)}) collective-permute-start(bf16[16,80,128]{2,1,0:T(8,128)(2,1)S(1)} %get-tuple-element.34), channel_id=1, source_target_pairs={{0,64},{1,17},{2,66},{3,19},{4,68},{5,21},{6,70},{7,23},{8,72},{9,... | collective-permute-start | bytes 983048 | tf_op jit(solution)/shard_map/ppermute | solution.py:479
  100.8 9.8 %collective-permute-start.19 = (bf16[16,80,128]{2,1,0:T(8,128)(2,1)S(1)}, bf16[16,80,128]{2,1,0:T(8,128)(2,1)S(1)}, u32[]{:S(2)}, u32[]{:S(2)}) collective-permute-start(bf16[16,80,128]{2,1,0:T(8,128)(2,1)S(1)} %get-tuple-element.34), channel_id=1, source_target_pairs={{0,96},{1,25},{2,98},{3,27},{4,100},{5,29},{6,102},{7,31},{8,104},... | collective-permute-start | bytes 983048 | tf_op jit(solution)/shard_map/ppermute | solution.py:479
  110.7 12.0 %collective-permute-start.20 = (bf16[64,80,128]{2,1,0:T(8,128)(2,1)S(1)}, bf16[64,80,128]{2,1,0:T(8,128)(2,1)S(1)}, u32[]{:S(2)}, u32[]{:S(2)}) collective-permute-start(bf16[64,80,128]{2,1,0:T(8,128)(2,1)S(1)} %constant_dynamic-update-slice_fusion.12.own_ref), channel_id=1, source_target_pairs={{0,1},{1,0},{2,3},{3,2},{4,5},{5,4},{6,7},{7,6},{8,9},{9,8},{10,11... | collective-permute-start | bytes 3932168 | tf_op jit(solution)/shard_map/ppermute | solution.py:479

commit v3 on v2

--- a/solution.py
+++ b/solution.py
@@ -34,9 +34,7 @@
     return lax.dot_general(a, b, (((0,), (0,)), ((), ())), preferred_element_type=F32)
 
 
-def pack_kernel(me_ref, h_ref, pos_ref, src_ref, dst_ref, ec_ref, tin_ref, tout_ref, tc_ref, gid_ref, out_ref, meta, pos_v, sem):
-    fetch = pltpu.make_async_copy(pos_ref, pos_v, sem)
-    fetch.start()
+def pack_kernel(me_ref, h_ref, pos_ref, src_ref, dst_ref, ec_ref, tin_ref, tout_ref, tc_ref, gid_ref, out_ref, meta):
     odd = lax.rem(me_ref[0], 2)
     out_ref[0:AT, :] = h_ref[...]
 
@@ -53,8 +51,7 @@
         v = ref[...].astype(F32)
         meta[r : r + 1, :] = v[:, 0:TPB]
         meta[r + 1 : r + 2, :] = v[:, TPB : 2 * TPB]
-    fetch.wait()
-    p = jnp.concatenate([pos_v[i] for i in range(3)], axis=0)
+    p = jnp.concatenate([pos_ref[i] for i in range(3)], axis=0)
     p1 = p.astype(BF).astype(F32)
     p2 = (p - p1).astype(BF).astype(F32)
     p3 = (p - p1) - p2
@@ -77,16 +74,19 @@
     return pl.pallas_call(
         pack_kernel,
         out_shape=jax.ShapeDtypeStruct((PIECE, D), BF),
-        in_specs=[sm, vm, pl.BlockSpec(memory_space=pl.ANY), vm, vm, sm, vm, vm, sm, vm],
+        in_specs=[sm, vm, vm, vm, vm, sm, vm, vm, sm, vm],
         out_specs=vm,
-        scratch_shapes=[pltpu.VMEM((16, D), F32), pltpu.VMEM((3, 1, AT), F32), pltpu.SemaphoreType.DMA],
+        scratch_shapes=[pltpu.VMEM((16, D), F32)],
         name="pack",
     )(me, h, pos, src, dst, ec, tin, tout, tc, gid)
 
 
 def main_kernel(
     me_ref,
-    gat_ref,
+    slice_ref,
+    u_ref,
+    own_ref,
+    other_ref,
     ws_hbm,
     wd_hbm,
     wr_hbm,
@@ -99,6 +99,7 @@
     node_ref,
     pay_ref,
     h_s,
+    meta_s,
     ab_s,
     posp_s,
     oht_s,
@@ -139,76 +140,78 @@
     ]
     for load in loads:
         load.start()
-    me, my_u, my_v = me_ref[0], me_ref[1], me_ref[2]
+    me, my_slice, my_u = me_ref[0], slice_ref[0], u_ref[0]
+    for near, ref in ((0, own_ref), (1, other_ref)):
+        for kz in range(4):
+            shard = me ^ (2 * kz + near)
+            h_s[pl.ds(pl.multiple_of(shard * AT, AT), AT), :] = ref[kz, 0:AT, :]
+            meta_s[shard] = ref[kz, AT:PIECE, :].astype(F32)
     gid_rows = []
     for j in range(4):
-        first, second = gat_ref[me ^ (2 * j), AT:PIECE, 0:128], gat_ref[me ^ (2 * j + 1), AT:PIECE, 0:128]
-        both = first.astype(F32) + second.astype(F32)
+        both = meta_s[2 * j, :, 0:128] + meta_s[2 * j + 1, :, 0:128]
         posp_s[:, 128 * j : 128 * (j + 1)] = both.astype(BF)
         gid_rows.append(both[15:16, :])
-    for s in range(NG):
-        h_s[AT * s : AT * (s + 1), :] = gat_ref[me ^ s, 0:AT, :]
     gid_row = jnp.concatenate(gid_rows, axis=1)
     gid_col = jnp.transpose(jnp.broadcast_to(gid_row, (8, ATOMS)))[:, 0:1]
-    h = h_s[...]
-    loads[0].wait()
-    ab_s[0:ATOMS, :] = nn(h, ws_ref[...]).astype(BF)
-    loads[1].wait()
-    ab_s[ATOMS : 2 * ATOMS, :] = nn(h, wd_ref[...]).astype(BF)
-
-    for load in loads[2:]:
-        load.wait()
+
     step = 16.0 / K
     inv_width = K / 24.0
-    sub_a = lax.broadcasted_iota(jnp.int32, (ATOMS, ES), 0).astype(F32)
+    sub_e = lax.broadcasted_iota(jnp.int32, (BLK, ES), 0).astype(F32).astype(BF)
+    sub_t = lax.broadcasted_iota(jnp.int32, (BLK, TPB), 0).astype(F32).astype(BF)
     lane_a = lax.broadcasted_iota(jnp.int32, (ES, ATOMS), 1).astype(F32)
-    sub_b = lax.broadcasted_iota(jnp.int32, (BLK, TPB), 0).astype(F32)
     lane_e = lax.broadcasted_iota(jnp.int32, (1, ES), 1).astype(F32)
     lane_t = lax.broadcasted_iota(jnp.int32, (1, TPB), 1).astype(F32)
     centers = lax.broadcasted_iota(jnp.int32, (1, K), 1).astype(F32) * step
+    one, zero = jnp.ones((), BF), jnp.zeros((), BF)
 
     def onehot(cond):
         return jnp.where(cond, 1.0, 0.0).astype(BF)
 
-    def forward(s, carry):
-        meta = gat_ref[lax.bitwise_xor(me, s), AT:PIECE, :].astype(F32)
+    def hit(places, row):
+        wide = jnp.broadcast_to(row.astype(BF), places.shape)
+        return jnp.where(places == wide, one, zero)
+
+    def geometry(s):
+        meta = meta_s[s]
         src = 2.0 * meta[0:1, 0:ES] + meta[0:1, ES : 2 * ES]
         dst = 2.0 * meta[1:2, 0:ES] + meta[1:2, ES : 2 * ES]
         ec = meta[15:16, 128:256]
-        tc = 8.0 * meta[15:16, 256:384] + meta[15:16, 384:512]
         live = jnp.where(lane_e < jnp.concatenate([ec, ec], axis=1), 1.0, 0.0)
-        lanes = pl.ds(pl.multiple_of(s * ES, ES), ES)
-        ohts = onehot(sub_a == src)
-        ohtd = onehot(sub_a == dst)
-        oht_s[0:ATOMS, lanes] = ohts
-        oht_s[ATOMS : 2 * ATOMS, lanes] = ohtd
+        lanes = slice(s * ES, (s + 1) * ES)
+        for base, row in ((0, src), (ATOMS, dst)):
+            for j in range(4):
+                oht_s[base + BLK * j : base + BLK * (j + 1), lanes] = hit(sub_e, row - float(BLK * j))
         posp = posp_s[...]
-        ps = nn(posp, ohts)
-        pd = nn(posp, ohtd)
+        ps = nn(posp, oht_s[0:ATOMS, lanes])
+        pd = nn(posp, oht_s[ATOMS : 2 * ATOMS, lanes])
         ps = (ps[6:9] + ps[9:12]) + ps[12:15]
         pd = (pd[6:9] + pd[9:12]) + pd[12:15]
         vec = pd - ps
         sq = vec * vec
         dist = jnp.sqrt(sq[0:1] + sq[1:2] + sq[2:3] + 0.25)
         inv = 1.0 / dist
-        unit = vec * inv
-        geo = jnp.concatenate([src, dst, live, dist, unit, inv], axis=0)
-        geo_s[s] = geo
+        geo_s[s] = jnp.concatenate([src, dst, live, dist, vec * inv, inv], axis=0)
+
+    def forward(s):
+        geo = geo_s[s]
+        meta = meta_s[s]
+        unit = geo[4:7]
+        tc = 8.0 * meta[15:16, 256:384] + meta[15:16, 384:512]
         cols = jnp.transpose(geo)
         ohs = onehot(lane_a == cols[:, 0:1])
         ohd = onehot(lane_a == cols[:, 1:2])
         ohd_s[s] = ohd
         t = (cols[:, 3:4] - centers) * inv_width
-        basis = jnp.exp(-(t * t)).astype(BF)
-        bt_s[:, lanes] = jnp.transpose(basis.astype(F32)).astype(BF)
-        pre = nn(ohs, ab_s[0:ATOMS, :]) + nn(ohd, ab_s[ATOMS : 2 * ATOMS, :])
-        radial = nn(basis, wr_ref[...]) * cols[:, 2:3]
-        sig = 0.5 + 0.5 * jnp.tanh(0.5 * pre)
-        sil = pre * sig
+        basis = jnp.exp(-(t * t)) * cols[:, 2:3]
+        bt_s[:, s * ES : (s + 1) * ES] = jnp.transpose(basis).astype(BF)
+        q = nn(ohs, ab_s[0:ATOMS, :]) + nn(ohd, ab_s[ATOMS : 2 * ATOMS, :])
+        radial = nn(basis.astype(BF), wr_ref[...])
+        a = 1.0 + jnp.tanh(q)
+        sil = q * a
         msg = (sil * radial).astype(BF)
         msg_s[s] = msg
-        f_s[s] = (radial * (sig + sil * (1.0 - sig))).astype(BF)
-        sg_s[s] = (sil * cols[:, 2:3]).astype(BF)
+        f_s[s] = (radial * (a + sil * (2.0 - a))).astype(BF)
+        sg_s[s] = sil.astype(BF)
         m2 = nn(msg, wt_ref[...]).astype(BF)
         m2_s[s] = m2
         for i in range(2):
@@ -216,9 +219,7 @@
             limit = jnp.concatenate([tc] * 4, axis=1) - float(TPB * i)
             tin = meta[2 + i : 3 + i, :]
             tout = jnp.where(lane_t < limit, meta[4 + i : 5 + i, :], -1.0)
-            pick_in = onehot(sub_b == tin)
-            pick_out = onehot(sub_b == tout)
-            count = nt(pick_out, pick_in) * cols[rows, 2:3]
+            count = nt(hit(sub_t, tout), hit(sub_t, tin)) * cols[rows, 2:3]
             n_s[2 * s + i] = count
             gram = (
                 cols[rows, 4:5] * unit[0:1, rows]
@@ -228,10 +229,19 @@
             mix = count * gram
             tt_s[2 * s + i] = jnp.transpose(mix).astype(BF)
             upd = msg[rows].astype(F32) + nn(mix.astype(BF), m2[rows])
-            upd_s[pl.ds(pl.multiple_of(s * ES + BLK * i, BLK), BLK), :] = upd.astype(BF)
-        return carry
-
-    lax.fori_loop(0, NG, forward, 0)
+            upd_s[s * ES + BLK * i : s * ES + BLK * (i + 1), :] = upd.astype(BF)
+
+    for s in range(NG):
+        geometry(s)
+    h = h_s[...]
+    loads[0].wait()
+    ab_s[0:ATOMS, :] = (0.5 * nn(h, ws_ref[...])).astype(BF)
+    loads[1].wait()
+    ab_s[ATOMS : 2 * ATOMS, :] = (0.5 * nn(h, wd_ref[...])).astype(BF)
+    for load in loads[2:]:
+        load.wait()
+    for s in range(NG):
+        forward(s)
 
     agg = nn(oht_s[ATOMS : 2 * ATOMS, :], upd_s[...]).astype(BF)
     aggb_s[...] = agg
@@ -252,9 +262,8 @@
     dzb_s[...] = dz
     ac_s[...] = nt(dz, wo_ref[...]).astype(BF)
 
-    def backward(s, carry):
-        lanes = pl.ds(pl.multiple_of(s * ES, ES), ES)
-        edges = pl.ds(pl.multiple_of(s * ES, ES), ES)
+    def backward(s):
+        edges = slice(s * ES, (s + 1) * ES)
         geo = geo_s[s]
         cols = jnp.transpose(geo)
         ug = nn(ohd_s[s], ac_s[...])
@@ -267,8 +276,8 @@
             dgram = n_s[2 * s + i] * nt(ugb[rows], m2[rows])
             both = dgram + jnp.transpose(dgram)
             turns.append(
-                lax.dot_general(
-                    geo[:, rows], both, (((1,), (0,)), ((), ())), precision=HI, preferred_element_type=F32
+                jnp.concatenate(
+                    [jnp.sum(both * cols[rows, a : a + 1], axis=0, keepdims=True) for a in (4, 5, 6)], axis=0
                 )
             )
         dm2 = jnp.concatenate(halves, axis=0)
@@ -278,27 +287,25 @@
         drad = (dmsg * sg_s[s].astype(F32)).astype(BF)
         drad_s[edges, :] = drad
         t = (cols[:, 3:4] - centers) * inv_width
-        slope = nt(drad, wr_ref[...]) * jnp.exp(-(t * t)) * (t * (-2.0 * inv_width))
-        ddist = jnp.sum(jnp.transpose(slope), axis=0, keepdims=True)
+        slope = nt(drad, wr_ref[...]) * (jnp.exp(-(t * t)) * (t * (-2.0 * inv_width)))
+        ddist = jnp.sum(jnp.transpose(slope), axis=0, keepdims=True) * geo[2:3]
         unit = geo[4:7]
-        du = jnp.concatenate(turns, axis=1)[4:7]
+        du = jnp.concatenate(turns, axis=1)
         along = du * unit
         along = along[0:1] + along[1:2] + along[2:3]
         dv = geo[7:8] * (du - unit * along) + unit * ddist
         top = dv.astype(BF).astype(F32)
-        dv_s[:, lanes] = jnp.concatenate(
-            [top, dv - top, jnp.zeros((10, ES), F32)], axis=0
-        ).astype(BF)
-        return carry
-
-    lax.fori_loop(0, NG, backward, 0)
+        dv_s[:, edges] = jnp.concatenate([top, dv - top, jnp.zeros((10, ES), F32)], axis=0).astype(BF)
+
+    for s in range(NG):
+        backward(s)
 
     own = pl.multiple_of(me * AT, AT)
     ohs_own = oht_s[pl.ds(own, AT), :]
     ohd_own = oht_s[pl.ds(ATOMS + own, AT), :]
     dpre = dpre_s[...]
-    s_src = nn(ohs_own, dpre).astype(BF)
-    s_dst = nn(ohd_own, dpre).astype(BF)
+    s_src = (0.5 * nn(ohs_own, dpre)).astype(BF)
+    s_dst = (0.5 * nn(ohd_own, dpre)).astype(BF)
     node_ref[...] = (
         cot_s[pl.ds(own, AT), 0:1] * we + nt(s_src, ws_ref[...]) + nt(s_dst, wd_ref[...])
     )
@@ -307,11 +314,11 @@
     for i in range(3):
         pos_out_ref[i] = pos[i : i + 1]
 
-    group = lax.div(me, 4)
-    block = pl.ds(pl.multiple_of(lax.rem(me, 4) * 128, 128), 128)
+    group = lax.div(my_slice, 4)
+    block = pl.ds(pl.multiple_of(lax.rem(my_slice, 4) * 128, 128), 128)
     side = pl.ds(pl.multiple_of(group * ATOMS, ATOMS), ATOMS)
     rows_t = tn(h_s[:, block], oht_s[side, :]).astype(BF)
-    a_s[...] = nn(rows_t, dpre)
+    a_s[...] = 0.5 * nn(rows_t, dpre)
 
     @pl.when(group == 0)
     def _():
@@ -322,7 +329,7 @@
     def _():
         b_s[...] = tn(aggb_s[:, block], dzb_s[...])
 
-    r_s[...] = nn(bt_s[pl.ds(pl.multiple_of(me * 16, 16), 16), :], drad_s[...])
+    r_s[...] = nn(bt_s[pl.ds(pl.multiple_of(my_slice * 16, 16), 16), :], drad_s[...])
     ge = ge_s[:, block]
     for u in range(4):
         for v in range(4):
@@ -337,10 +344,10 @@
                 ],
                 axis=0,
             )
-            pay_ref[lax.rem(u - my_u + 4, 4), lax.rem(v - my_v + 4, 4)] = chunk.astype(BF)
-
-
-def batch(me, gat, ws, wd, wr, wt, wo, we, ecot):
+            pay_ref[lax.rem(u - my_u + 4, 4), v] = chunk.astype(BF)
+
+
+def batch(me, part, u, own, other, ws, wd, wr, wt, wo, we, ecot):
     vm = pl.BlockSpec(memory_space=pltpu.VMEM)
     sm = pl.BlockSpec(memory_space=pltpu.SMEM)
     V = pltpu.VMEM
@@ -352,10 +359,11 @@
             jax.ShapeDtypeStruct((AT, D), F32),
             jax.ShapeDtypeStruct((4, 4, CH, 128), BF),
         ),
-        in_specs=[sm, vm] + [pl.BlockSpec(memory_space=pl.ANY)] * 5 + [vm] * 2,
+        in_specs=[sm] * 3 + [vm] * 2 + [pl.BlockSpec(memory_space=pl.ANY)] * 5 + [vm] * 2,
         out_specs=(vm, vm, vm, vm),
         scratch_shapes=[
             V((ATOMS, D), BF),
+            V((NG, 16, D), F32),
             V((2 * ATOMS, D), BF),
             V((16, ATOMS), BF),
             V((2 * ATOMS, EDGES), BF),
@@ -390,23 +398,23 @@
         ],
         compiler_params=pltpu.CompilerParams(vmem_limit_bytes=50 * 1024 * 1024),
         name="batch",
-    )(me, gat, ws, wd, wr, wt, wo, we, ecot)
-
-
-def place_kernel(me_ref, own_ref, other_ref, gs_ref, gd_ref, gr_ref, gt_ref, go_ref, ge_ref, first, second, low, sems):
-    x, y, zl, core = me_ref[0], me_ref[1], me_ref[2], me_ref[3]
+    )(me, part, u, own, other, ws, wd, wr, wt, wo, we, ecot)
+
+
+def place_kernel(x_ref, y_ref, slice_ref, own_ref, other_ref, gs_ref, gd_ref, gr_ref, gt_ref, go_ref, ge_ref, first, second, low, sems):
+    x, y, mine = x_ref[0], y_ref[0], slice_ref[0]
+    core = mine & 1
     for c, ref in ((0, own_ref), (1, other_ref)):
         pc = core ^ c
         my_u = jnp.where(pc == 0, x, y)
-        my_v = jnp.where(pc == 0, y, x)
-
-        def body(i, carry, pc=pc, my_u=my_u, my_v=my_v, ref=ref):
+
+        def body(i, carry, c=c, my_u=my_u, ref=ref):
             u = lax.rem(my_u - lax.div(i, 4) + 4, 4)
-            v = lax.rem(my_v - lax.rem(i, 4) + 4, 4)
-            cols = pl.ds(pl.multiple_of(v * 128, 128), 128)
-            for kz in range(4):
-                g = (zl ^ kz) * 2 + pc
-                tile = ref[4 * i + kz].astype(F32)
+            kz = lax.rem(i, 4)
+            for k in range(4):
+                cols = slice(128 * k, 128 * (k + 1))
+                g = lax.bitwise_xor(mine, 2 * kz + c)
+                tile = ref[4 * i + k].astype(F32)
                 rows = pl.ds(pl.multiple_of(g * 128 + u * 32, 32), 32)
                 first[rows, cols] = tile[0:32]
                 second[rows, cols] = tile[32:64]
@@ -435,7 +443,7 @@
         copy.wait()
 
 
-def place(where, own, other):
+def place(x, y, part, own, other):
     vm = pl.BlockSpec(memory_space=pltpu.VMEM)
     sm = pl.BlockSpec(memory_space=pltpu.SMEM)
     far = pl.BlockSpec(memory_space=pl.ANY)
@@ -443,7 +451,7 @@
     return pl.pallas_call(
         place_kernel,
         out_shape=(big, big, jax.ShapeDtypeStruct((K, D), F32), big, big, jax.ShapeDtypeStruct((1, D), F32)),
-        in_specs=[sm, vm, vm],
+        in_specs=[sm] * 3 + [vm] * 2,
         out_specs=(far, far, vm, far, far, vm),
         scratch_shapes=[
             pltpu.VMEM((2 * D, D), F32),
@@ -453,7 +461,7 @@
         ],
         compiler_params=pltpu.CompilerParams(vmem_limit_bytes=40 * 1024 * 1024),
         name="place",
-    )(where, own, other)
+    )(x, y, part, own, other)
 
 
 def moves(fn):
@@ -486,11 +494,9 @@
 ORDER = (1, 3, 2)
 
 
-def total(parts):
-    result = parts[0].astype(F32)
-    for part in parts[1:]:
-        result = result + part.astype(F32)
-    return result
+def total(a, b, c, d):
+    a, b, c, d = (part.astype(F32) for part in (a, b, c, d))
+    return ((a + b) + (c + d)).astype(BF)
 
 
 def per_device(
@@ -512,10 +518,11 @@
     energy_cot,
 ):
     dp, graph = lax.axis_index("dp"), lax.axis_index("graph")
-    x, y = lax.rem(lax.div(dp, 4), 4), lax.rem(dp, 4)
-    zl, core = lax.div(graph, 2), lax.rem(graph, 2)
-    u, v = jnp.where(core == 0, x, y), jnp.where(core == 0, y, x)
-    me = jnp.stack([graph, u, v]).astype(jnp.int32)
+    zh, x, y = lax.shift_right_logical(dp, 4), lax.shift_right_logical(dp, 2) & 3, dp & 3
+    core = graph & 1
+    u = jnp.where(core == 0, x, y)
+    part = graph ^ (6 * zh)
+    me, x, y, u, part = (a.astype(jnp.int32).reshape(1) for a in (graph, x, y, u, part))
     piece = pack(
         me,
         node_feats[0],
@@ -528,22 +535,20 @@
         trip_count,
         graph_ids,
     )[None]
-    pair = join(piece, shift(piece, c=1))
-    gathered = join(pair, *[shift(pair, zl=k) for k in (1, 2, 3)])
+    own = join(piece, *[shift(piece, zl=k) for k in (1, 2, 3)])
+    other = shift(own, c=1)
     energy, pos_grad, node_grad, payload = batch(
-        me, gathered, w_src, w_dst, w_radial, w_trip, w_out, w_energy.reshape(1, D), energy_cot
+        me, part, u, own, other, w_src, w_dst, w_radial, w_trip, w_out, w_energy.reshape(1, D), energy_cot
     )
-    part = total([payload[0]] + [shift(payload[k], u=k) for k in ORDER]).astype(BF)
-    part = total([part[0]] + [shift(part[k], v=k) for k in ORDER]).astype(BF)
-    part = (part.astype(F32) + shift(part, zh=1).astype(F32)).astype(BF)[None]
-    part = join(part, *[shift(part, zl=k) for k in (1, 2, 3)])
-    back = [shift(part, v=k) for k in ORDER]
-    part = join(part, back[0], back[2], back[1])
-    back = [shift(part, u=k) for k in ORDER]
-    part = join(part, back[0], back[2], back[1])
-    other = shift(part, c=1)
-    where = jnp.stack([x, y, zl, core]).astype(jnp.int32)
-    gs, gd, gr, gt, go, ge = place(where, part, other)
+    one, three, two = [shift(payload[k], u=k) for k in ORDER]
+    held = total(payload[0], two, one, three)
+    one, three, two = [shift(held, v=k) for k in ORDER]
+    held = total(held, two, one, three)
+    held = (held.astype(F32) + shift(held, zh=1, zl=3).astype(F32)).astype(BF)
+    held = join(held, *[shift(held, zl=k) for k in (1, 2, 3)])
+    one, three, two = [shift(held, u=k) for k in ORDER]
+    held = join(held, one, two, three)
+    gs, gd, gr, gt, go, ge = place(x, y, part, held, shift(held, c=1))
     return (energy, jnp.swapaxes(pos_grad, 0, 1), node_grad[None], gs, gd, gr, gt, go, ge.reshape(D))
 
 

time: 127 us -> 101 us (0.80)
  Pallas kernels: 38.8 us -> 25 us
  starting transfers between devices: 40.9 us -> 32.5 us
  waiting for transfers between devices: 40.2 us -> 33.5 us
  local copies, waits for them, and re-layouts: 2.98 us -> 6.6 us
    pallas_call x1, Pallas kernels: 32.2 us -> 20.1 us  [batch(): pl.pallas_call(main_kernel, out_shape=(jax.ShapeDtypeStruct((1, 16), F32)...]
    ppermute x21 -> x18, starting transfers between devices: 40.9 us -> 32.5 us  [shift(): return lax.ppermute(value, AXES, moves(fn))]
    ppermute x21 -> x18, waiting for transfers between devices: 40.2 us -> 33.5 us  [shift(): return lax.ppermute(value, AXES, moves(fn))]
    unnamed x26 -> x17, local copies, waits for them, and re-layouts: 2.18 us -> 5.86 us
  transfers between devices with their start and end apart: 21 -> 18, of which waited for: 14 -> 12; matrix products, arithmetic and copies ran while one was open for 1% -> 1% of each run, Pallas kernels for 0% -> 0%
where the time goes in v3:
time: 101 us
  waiting for transfers between devices  33.5 us (33%)
  starting transfers between devices  32.5 us (32%)
  Pallas kernels  25 us (25%)
  local copies, waits for them, and re-layouts  6.6 us (7%)
  between operations  2.23 us (2%)
  other arithmetic  1.09 us (1%)
    ppermute x18, waiting for transfers between devices, shift(): return lax.ppermute(value, AXES, moves(fn))  33.5 us
    ppermute x18, starting transfers between devices, shift(): return lax.ppermute(value, AXES, moves(fn))  32.5 us
    pallas_call x1, Pallas kernels, batch(): pl.pallas_call(main_kernel, out_shape=(jax.ShapeDtypeStruct((1, 16), F32)...  20.1 us
    unnamed x17, local copies, waits for them, and re-layouts  5.86 us
    pallas_call x1, Pallas kernels, place(): pl.pallas_call(place_kernel, out_shape=(big, big, jax.ShapeDtypeStruct((K...  3.32 us
  transfers between devices with their start and end apart: 18, of which 12 were waited for; matrix products, arithmetic and copies ran while one was open for 1% of the time, Pallas kernels for 0%

profile of v3, /device:TPU:1, one launch (start us, length us, event | category | flops | bytes accessed | tf_op | source)
XLA Modules:
  0.0 101.0 jit_solution(6902671236855344823)
XLA Ops:
  1.9 1.6 %pack.1 = bf16[80,512]{1,0:T(8,128)(2,1)} custom-call(s32[1]{0:T(128)} %bitcast.me_ref, bf16[64,512]{1,0:T(8,128)(2,1)} %bitcast.24, f32[3,1,64]{2,1,0:T(1,128)} %bitcast.25, s32[1,256]{1,0:T(1,128)} %src_ref.1, s32[1,256]{1,0:T(1,128)} %dst_ref.1, s32[1,1]{1,0:T(1,128)S(6)} %copy.31.ec_ref, s32[1,1024]{1,0:T(1,128)} %tin_ref.1, s32[1,1024]{1,0:T(1,128)} %tout_ref.1, ...), custom_call_target="tpu_custom_call" | custom-call | tf_op jit(solution)/shard_map/pack/pallas_call | solution.py:74
  3.6 5.2 %collective-permute-start.2 = (bf16[1,80,512]{2,1,0:T(8,128)(2,1)}, bf16[1,80,512]{2,1,0:T(8,128)(2,1)S(1)}, u32[]{:S(2)}, u32[]{:S(2)}) collective-permute-start(bf16[1,80,512]{2,1,0:T(8,128)(2,1)} %bitcast.20), channel_id=1, source_target_pairs={{0,6},{1,7},{2,4},{3,5},{4,2},{5,3},{6,0},{7,1},{8,14},{9,15},{10,... | collective-permute-start | bytes 245768 | tf_op jit(solution)/shard_map/ppermute | solution.py:487
  8.7 0.0 collective-permute-start.1
  8.7 0.3 collective-permute-start
  9.0 1.9 %collective-permute-done.2 = bf16[1,80,512]{2,1,0:T(8,128)(2,1)S(1)} collective-permute-done((bf16[1,80,512]{2,1,0:T(8,128)(2,1)}, bf16[1,80,512]{2,1,0:T(8,128)(2,1)S(1)}, u32[]{:S(2)}, u32[]{:S(2)}) %collective-permute-start.2) | collective-permute-done | bytes 81952 | tf_op jit(solution)/shard_map/ppermute | solution.py:487
  10.9 4.9 %collective-permute-done.1 = bf16[1,80,512]{2,1,0:T(8,128)(2,1)S(1)} collective-permute-done((bf16[1,80,512]{2,1,0:T(8,128)(2,1)}, bf16[1,80,512]{2,1,0:T(8,128)(2,1)S(1)}, u32[]{:S(2)}, u32[]{:S(2)}) %collective-permute-start.1) | collective-permute-done | bytes 81952 | tf_op jit(solution)/shard_map/ppermute | solution.py:487
  15.7 0.0 collective-permute-done
  15.8 0.9 pad_maximum_fusion.own_ref
  16.7 0.8 collective-permute-start.3
  17.5 0.7 reshape.44.we_ref
  18.1 0.6 collective-permute-done.3.other_ref
  18.7 0.0 copy-start
  18.7 1.0 %copy-done = bf16[512,512]{1,0:T(8,128)(2,1)S(1)} copy-done((bf16[512,512]{1,0:T(8,128)(2,1)S(1)}, bf16[512,512]{1,0:T(8,128)(2,1)}, u32[]{:S(2)}) %copy-start) | copy-done | bytes 524312
  19.8 0.0 copy-start.1
  19.8 1.0 %copy-done.1 = bf16[512,512]{1,0:T(8,128)(2,1)S(1)} copy-done((bf16[512,512]{1,0:T(8,128)(2,1)S(1)}, bf16[512,512]{1,0:T(8,128)(2,1)}, u32[]{:S(2)}) %copy-start.1) | copy-done | bytes 524312
  20.8 0.0 copy-start.2
  20.8 1.0 %copy-done.2 = bf16[512,512]{1,0:T(8,128)(2,1)S(1)} copy-done((bf16[512,512]{1,0:T(8,128)(2,1)S(1)}, bf16[512,512]{1,0:T(8,128)(2,1)}, u32[]{:S(2)}) %copy-start.2) | copy-done | bytes 524312
  21.8 0.0 copy-start.3
  21.8 1.0 %copy-done.3 = bf16[512,512]{1,0:T(8,128)(2,1)S(1)} copy-done((bf16[512,512]{1,0:T(8,128)(2,1)S(1)}, bf16[512,512]{1,0:T(8,128)(2,1)}, u32[]{:S(2)}) %copy-start.3) | copy-done | bytes 524312
  22.9 0.0 copy-start.4
  22.9 0.9 copy-done.4
  23.8 0.0 copy-start.5
  23.8 0.7 copy-done.5
  24.4 20.1 %batch.1 = (f32[1,16]{1,0:T(1,128)}, f32[3,1,64]{2,1,0:T(1,128)}, f32[64,512]{1,0:T(8,128)}, bf16[4,4,80,128]{3,2,1,0:T(8,128)(2,1)S(1)}) custom-call(s32[1]{0:T(128)} %bitcast.me_ref, s32[1]{0:T(128)} %bitcast.1.slice_ref, s32[1]{0:T(128)} %bitcast.2.u_ref, bf16[4,80,512]{2,1,0:T(8,128)(2,1)S(1)} %pad_maximum_fusion.own_ref, ...), custom_call_target="tpu_custom_call" | custom-call | tf_op jit(solution)/shard_map/batch/pallas_call | solution.py:354
  44.6 2.9 %collective-permute-start.4 = (bf16[4,80,128]{2,1,0:T(8,128)(2,1)S(1)}, bf16[4,80,128]{2,1,0:T(8,128)(2,1)S(1)}, u32[]{:S(2)}, u32[]{:S(2)}) collective-permute-start(bf16[4,80,128]{2,1,0:T(8,128)(2,1)S(1)} %get-tuple-element.31), channel_id=1, source_target_pairs={{0,64},{1,17},{2,66},{3,19},{4,68},{5,21},{6,70},{7,23},{8,72},{9,... | collective-permute-start | bytes 245768 | tf_op jit(solution)/shard_map/ppermute | solution.py:487
  47.5 0.8 collective-permute-start.6
  48.2 0.7 collective-permute-start.5
  48.9 0.8 collective-permute-done.4
  49.7 1.0 collective-permute-done.6
  50.8 2.0 %collective-permute-done.5 = bf16[4,80,128]{2,1,0:T(8,128)(2,1)S(1)} collective-permute-done((bf16[4,80,128]{2,1,0:T(8,128)(2,1)S(1)}, bf16[4,80,128]{2,1,0:T(8,128)(2,1)S(1)}, u32[]{:S(2)}, u32[]{:S(2)}) %collective-permute-start.5) | collective-permute-done | bytes 81952 | tf_op jit(solution)/shard_map/ppermute | solution.py:487
  52.8 2.5 %collective-permute-start.9 = (bf16[4,80,128]{2,1,0:T(8,128)(2,1)S(1)}, bf16[4,80,128]{2,1,0:T(8,128)(2,1)S(1)}, u32[]{:S(2)}, u32[]{:S(2)}) collective-permute-start(bf16[4,80,128]{2,1,0:T(8,128)(2,1)S(1)} %fusion.1), channel_id=1, source_target_pairs={{0,24},{1,97},{2,26},{3,99},{4,28},{5,101},{6,30},{7,103},{8,0},{9... | collective-permute-start | bytes 245768 | tf_op jit(solution)/shard_map/ppermute | solution.py:487
  55.3 0.0 collective-permute-start.8
  55.3 1.7 %collective-permute-start.7 = (bf16[4,80,128]{2,1,0:T(8,128)(2,1)S(1)}, bf16[4,80,128]{2,1,0:T(8,128)(2,1)S(1)}, u32[]{:S(2)}, u32[]{:S(2)}) collective-permute-start(bf16[4,80,128]{2,1,0:T(8,128)(2,1)S(1)} %fusion.1), channel_id=1, source_target_pairs={{0,16},{1,65},{2,18},{3,67},{4,20},{5,69},{6,22},{7,71},{8,24},{9,... | collective-permute-start | bytes 245768 | tf_op jit(solution)/shard_map/ppermute | solution.py:487
  57.1 0.0 collective-permute-done.9
  57.1 3.6 %collective-permute-done.8 = bf16[4,80,128]{2,1,0:T(8,128)(2,1)S(1)} collective-permute-done((bf16[4,80,128]{2,1,0:T(8,128)(2,1)S(1)}, bf16[4,80,128]{2,1,0:T(8,128)(2,1)S(1)}, u32[]{:S(2)}, u32[]{:S(2)}) %collective-permute-start.8) | collective-permute-done | bytes 81952 | tf_op jit(solution)/shard_map/ppermute | solution.py:487
  60.7 0.0 collective-permute-done.7
  60.8 4.8 %collective-permute-start.10 = (bf16[4,80,128]{2,1,0:T(8,128)(2,1)S(1)}, bf16[4,80,128]{2,1,0:T(8,128)(2,1)S(1)}, u32[]{:S(2)}, u32[]{:S(2)}) collective-permute-start(bf16[4,80,128]{2,1,0:T(8,128)(2,1)S(1)} %add_convert_fusion.1), channel_id=1, source_target_pairs={{0,134},{1,135},{2,132},{3,133},{4,130},{5,131},{6,128},{7,129},{8... | collective-permute-start | bytes 245768 | tf_op jit(solution)/shard_map/ppermute | solution.py:487
  65.5 2.3 %collective-permute-done.10 = bf16[4,80,128]{2,1,0:T(8,128)(2,1)S(1)} collective-permute-done((bf16[4,80,128]{2,1,0:T(8,128)(2,1)S(1)}, bf16[4,80,128]{2,1,0:T(8,128)(2,1)S(1)}, u32[]{:S(2)}, u32[]{:S(2)}) %collective-permute-start.10) | collective-permute-done | bytes 81952 | tf_op jit(solution)/shard_map/ppermute | solution.py:487
  67.9 1.3 %collective-permute-start.13 = (bf16[4,80,128]{2,1,0:T(8,128)(2,1)S(1)}, bf16[4,80,128]{2,1,0:T(8,128)(2,1)S(1)}, u32[]{:S(2)}, u32[]{:S(2)}) collective-permute-start(bf16[4,80,128]{2,1,0:T(8,128)(2,1)S(1)} %get-tuple-element.30), channel_id=1, source_target_pairs={{0,6},{1,7},{2,4},{3,5},{4,2},{5,3},{6,0},{7,1},{8,14},{9,15},{10,... | collective-permute-start | bytes 245768 | tf_op jit(solution)/shard_map/ppermute | solution.py:487
  69.2 0.4 collective-permute-start.12
  69.5 2.0 %collective-permute-start.11 = (bf16[4,80,128]{2,1,0:T(8,128)(2,1)S(1)}, bf16[4,80,128]{2,1,0:T(8,128)(2,1)S(1)}, u32[]{:S(2)}, u32[]{:S(2)}) collective-permute-start(bf16[4,80,128]{2,1,0:T(8,128)(2,1)S(1)} %get-tuple-element.30), channel_id=1, source_target_pairs={{0,2},{1,3},{2,0},{3,1},{4,6},{5,7},{6,4},{7,5},{8,10},{9,11},{10,... | collective-permute-start | bytes 245768 | tf_op jit(solution)/shard_map/ppermute | solution.py:487
  71.6 1.7 %collective-permute-done.13 = bf16[4,80,128]{2,1,0:T(8,128)(2,1)S(1)} collective-permute-done((bf16[4,80,128]{2,1,0:T(8,128)(2,1)S(1)}, bf16[4,80,128]{2,1,0:T(8,128)(2,1)S(1)}, u32[]{:S(2)}, u32[]{:S(2)}) %collective-permute-start.13) | collective-permute-done | bytes 81952 | tf_op jit(solution)/shard_map/ppermute | solution.py:487
  73.2 1.6 %collective-permute-done.12 = bf16[4,80,128]{2,1,0:T(8,128)(2,1)S(1)} collective-permute-done((bf16[4,80,128]{2,1,0:T(8,128)(2,1)S(1)}, bf16[4,80,128]{2,1,0:T(8,128)(2,1)S(1)}, u32[]{:S(2)}, u32[]{:S(2)}) %collective-permute-start.12) | collective-permute-done | bytes 81952 | tf_op jit(solution)/shard_map/ppermute | solution.py:487
  74.8 0.0 collective-permute-done.11
  74.9 1.4 %collective-permute-start.16 = (bf16[16,80,128]{2,1,0:T(8,128)(2,1)S(1)}, bf16[16,80,128]{2,1,0:T(8,128)(2,1)S(1)}, u32[]{:S(2)}, u32[]{:S(2)}) collective-permute-start(bf16[16,80,128]{2,1,0:T(8,128)(2,1)S(1)} %pad_maximum_fusion.1), channel_id=1, source_target_pairs={{0,96},{1,25},{2,98},{3,27},{4,100},{5,29},{6,102},{7,31},{8,104},... | collective-permute-start | bytes 983048 | tf_op jit(solution)/shard_map/ppermute | solution.py:487
  76.3 0.2 collective-permute-start.15
  76.5 0.5 collective-permute-start.14
  77.1 10.4 %collective-permute-done.14 = bf16[16,80,128]{2,1,0:T(8,128)(2,1)S(1)} collective-permute-done((bf16[16,80,128]{2,1,0:T(8,128)(2,1)S(1)}, bf16[16,80,128]{2,1,0:T(8,128)(2,1)S(1)}, u32[]{:S(2)}, u32[]{:S(2)}) %collective-permute-start.14) | collective-permute-done | bytes 327712 | tf_op jit(solution)/shard_map/ppermute | solution.py:487
  87.5 0.0 collective-permute-done.15
  87.6 0.0 collective-permute-done.16
  87.7 7.2 %collective-permute-start.17 = (bf16[64,80,128]{2,1,0:T(8,128)(2,1)S(1)}, bf16[64,80,128]{2,1,0:T(8,128)(2,1)S(1)}, u32[]{:S(2)}, u32[]{:S(2)}) collective-permute-start(bf16[64,80,128]{2,1,0:T(8,128)(2,1)S(1)} %constant_dynamic-update-slice_fusion.own_ref), channel_id=1, source_target_pairs={{0,1},{1,0},{2,3},{3,2},{4,5},{5,4},{6,7},{7,6},{8,9},{9,8},{10,11... | collective-permute-start | bytes 3932168 | tf_op jit(solution)/shard_map/ppermute | solution.py:487
  94.8 2.7 %collective-permute-done.17.other_ref = bf16[64,80,128]{2,1,0:T(8,128)(2,1)S(1)} collective-permute-done((bf16[64,80,128]{2,1,0:T(8,128)(2,1)S(1)}, bf16[64,80,128]{2,1,0:T(8,128)(2,1)S(1)}, u32[]{:S(2)}, u32[]{:S(2)}) %collective-permute-start.17) | collective-permute-done | bytes 1310752 | tf_op jit(solution)/shard_map/ppermute | solution.py:487
  97.5 3.3 %place.1 = (f32[512,512]{1,0:T(8,128)}, f32[512,512]{1,0:T(8,128)}, f32[128,512]{1,0:T(8,128)}, f32[512,512]{1,0:T(8,128)}, f32[512,512]{1,0:T(8,128)}, /*index=5*/f32[1,512]{1,0:T(1,128)}) custom-call(s32[1]{0:T(128)} %bitcast.8.x_ref, s32[1]{0:T(128)} %bitcast.9.y_ref, s32[1]{0:T(128)} %bitcast.1.slice_ref, ...), custom_call_target="tpu_custom_call" | custom-call | tf_op jit(solution)/shard_map/place/pallas_call | solution.py:451
  (11 shorter events, 0.4 us)
Async XLA Ops:
  3.6 7.3 %collective-permute-start.2 = (bf16[1,80,512]{2,1,0:T(8,128)(2,1)}, bf16[1,80,512]{2,1,0:T(8,128)(2,1)S(1)}, u32[]{:S(2)}, u32[]{:S(2)}) collective-permute-start(bf16[1,80,512]{2,1,0:T(8,128)(2,1)} %bitcast.20), channel_id=1, source_target_pairs={{0,6},{1,7},{2,4},{3,5},{4,2},{5,3},{6,0},{7,1},{8,14},{9,15},{10,... | collective-permute-start | bytes 245768 | tf_op jit(solution)/shard_map/ppermute | solution.py:487
  8.7 7.0 %collective-permute-start.1 = (bf16[1,80,512]{2,1,0:T(8,128)(2,1)}, bf16[1,80,512]{2,1,0:T(8,128)(2,1)S(1)}, u32[]{:S(2)}, u32[]{:S(2)}) collective-permute-start(bf16[1,80,512]{2,1,0:T(8,128)(2,1)} %bitcast.21), channel_id=1, source_target_pairs={{0,4},{1,5},{2,6},{3,7},{4,0},{5,1},{6,2},{7,3},{8,12},{9,13},{10,... | collective-permute-start | bytes 245768 | tf_op jit(solution)/shard_map/ppermute | solution.py:487
  8.7 7.0 %collective-permute-start = (bf16[1,80,512]{2,1,0:T(8,128)(2,1)}, bf16[1,80,512]{2,1,0:T(8,128)(2,1)S(1)}, u32[]{:S(2)}, u32[]{:S(2)}) collective-permute-start(bf16[1,80,512]{2,1,0:T(8,128)(2,1)} %bitcast.22), channel_id=1, source_target_pairs={{0,2},{1,3},{2,0},{3,1},{4,6},{5,7},{6,4},{7,5},{8,10},{9,11},{10,... | collective-permute-start | bytes 245768 | tf_op jit(solution)/shard_map/ppermute | solution.py:487
  16.7 2.0 %collective-permute-start.3 = (bf16[4,80,512]{2,1,0:T(8,128)(2,1)S(1)}, bf16[4,80,512]{2,1,0:T(8,128)(2,1)S(1)}, u32[]{:S(2)}, u32[]{:S(2)}) collective-permute-start(bf16[4,80,512]{2,1,0:T(8,128)(2,1)S(1)} %pad_maximum_fusion.own_ref), channel_id=1, source_target_pairs={{0,1},{1,0},{2,3},{3,2},{4,5},{5,4},{6,7},{7,6},{8,9},{9,8},{10,11... | collective-permute-start | bytes 983048 | tf_op jit(solution)/shard_map/ppermute | solution.py:487
  18.7 1.0 %copy-start = (bf16[512,512]{1,0:T(8,128)(2,1)S(1)}, bf16[512,512]{1,0:T(8,128)(2,1)}, u32[]{:S(2)}) copy-start(bf16[512,512]{1,0:T(8,128)(2,1)} %ws_hbm.1) | copy-start | bytes 1572868
  19.8 1.0 %copy-start.1 = (bf16[512,512]{1,0:T(8,128)(2,1)S(1)}, bf16[512,512]{1,0:T(8,128)(2,1)}, u32[]{:S(2)}) copy-start(bf16[512,512]{1,0:T(8,128)(2,1)} %wd_hbm.1) | copy-start | bytes 1572868
  20.8 1.0 %copy-start.2 = (bf16[512,512]{1,0:T(8,128)(2,1)S(1)}, bf16[512,512]{1,0:T(8,128)(2,1)}, u32[]{:S(2)}) copy-start(bf16[512,512]{1,0:T(8,128)(2,1)} %wt_hbm.1) | copy-start | bytes 1572868
  21.8 1.0 %copy-start.3 = (bf16[512,512]{1,0:T(8,128)(2,1)S(1)}, bf16[512,512]{1,0:T(8,128)(2,1)}, u32[]{:S(2)}) copy-start(bf16[512,512]{1,0:T(8,128)(2,1)} %wo_hbm.1) | copy-start | bytes 1572868
  22.9 0.9 copy-start.4
  23.8 0.7 copy-start.5
  44.6 5.2 %collective-permute-start.4 = (bf16[4,80,128]{2,1,0:T(8,128)(2,1)S(1)}, bf16[4,80,128]{2,1,0:T(8,128)(2,1)S(1)}, u32[]{:S(2)}, u32[]{:S(2)}) collective-permute-start(bf16[4,80,128]{2,1,0:T(8,128)(2,1)S(1)} %get-tuple-element.31), channel_id=1, source_target_pairs={{0,64},{1,17},{2,66},{3,19},{4,68},{5,21},{6,70},{7,23},{8,72},{9,... | collective-permute-start | bytes 245768 | tf_op jit(solution)/shard_map/ppermute | solution.py:487
  47.5 3.3 %collective-permute-start.6 = (bf16[4,80,128]{2,1,0:T(8,128)(2,1)S(1)}, bf16[4,80,128]{2,1,0:T(8,128)(2,1)S(1)}, u32[]{:S(2)}, u32[]{:S(2)}) collective-permute-start(bf16[4,80,128]{2,1,0:T(8,128)(2,1)S(1)} %get-tuple-element.32), channel_id=1, source_target_pairs={{0,96},{1,25},{2,98},{3,27},{4,100},{5,29},{6,102},{7,31},{8,104},... | collective-permute-start | bytes 245768 | tf_op jit(solution)/shard_map/ppermute | solution.py:487
  48.2 4.5 %collective-permute-start.5 = (bf16[4,80,128]{2,1,0:T(8,128)(2,1)S(1)}, bf16[4,80,128]{2,1,0:T(8,128)(2,1)S(1)}, u32[]{:S(2)}, u32[]{:S(2)}) collective-permute-start(bf16[4,80,128]{2,1,0:T(8,128)(2,1)S(1)} %get-tuple-element.33), channel_id=1, source_target_pairs={{0,32},{1,9},{2,34},{3,11},{4,36},{5,13},{6,38},{7,15},{8,40},{9,1... | collective-permute-start | bytes 245768 | tf_op jit(solution)/shard_map/ppermute | solution.py:487
  52.8 4.3 %collective-permute-start.9 = (bf16[4,80,128]{2,1,0:T(8,128)(2,1)S(1)}, bf16[4,80,128]{2,1,0:T(8,128)(2,1)S(1)}, u32[]{:S(2)}, u32[]{:S(2)}) collective-permute-start(bf16[4,80,128]{2,1,0:T(8,128)(2,1)S(1)} %fusion.1), channel_id=1, source_target_pairs={{0,24},{1,97},{2,26},{3,99},{4,28},{5,101},{6,30},{7,103},{8,0},{9... | collective-permute-start | bytes 245768 | tf_op jit(solution)/shard_map/ppermute | solution.py:487
  55.3 5.4 %collective-permute-start.8 = (bf16[4,80,128]{2,1,0:T(8,128)(2,1)S(1)}, bf16[4,80,128]{2,1,0:T(8,128)(2,1)S(1)}, u32[]{:S(2)}, u32[]{:S(2)}) collective-permute-start(bf16[4,80,128]{2,1,0:T(8,128)(2,1)S(1)} %fusion.1), channel_id=1, source_target_pairs={{0,8},{1,33},{2,10},{3,35},{4,12},{5,37},{6,14},{7,39},{8,16},{9,4... | collective-permute-start | bytes 245768 | tf_op jit(solution)/shard_map/ppermute | solution.py:487
  55.3 5.4 %collective-permute-start.7 = (bf16[4,80,128]{2,1,0:T(8,128)(2,1)S(1)}, bf16[4,80,128]{2,1,0:T(8,128)(2,1)S(1)}, u32[]{:S(2)}, u32[]{:S(2)}) collective-permute-start(bf16[4,80,128]{2,1,0:T(8,128)(2,1)S(1)} %fusion.1), channel_id=1, source_target_pairs={{0,16},{1,65},{2,18},{3,67},{4,20},{5,69},{6,22},{7,71},{8,24},{9,... | collective-permute-start | bytes 245768 | tf_op jit(solution)/shard_map/ppermute | solution.py:487
  60.8 7.1 %collective-permute-start.10 = (bf16[4,80,128]{2,1,0:T(8,128)(2,1)S(1)}, bf16[4,80,128]{2,1,0:T(8,128)(2,1)S(1)}, u32[]{:S(2)}, u32[]{:S(2)}) collective-permute-start(bf16[4,80,128]{2,1,0:T(8,128)(2,1)S(1)} %add_convert_fusion.1), channel_id=1, source_target_pairs={{0,134},{1,135},{2,132},{3,133},{4,130},{5,131},{6,128},{7,129},{8... | collective-permute-start | bytes 245768 | tf_op jit(solution)/shard_map/ppermute | solution.py:487
  67.9 5.3 %collective-permute-start.13 = (bf16[4,80,128]{2,1,0:T(8,128)(2,1)S(1)}, bf16[4,80,128]{2,1,0:T(8,128)(2,1)S(1)}, u32[]{:S(2)}, u32[]{:S(2)}) collective-permute-start(bf16[4,80,128]{2,1,0:T(8,128)(2,1)S(1)} %get-tuple-element.30), channel_id=1, source_target_pairs={{0,6},{1,7},{2,4},{3,5},{4,2},{5,3},{6,0},{7,1},{8,14},{9,15},{10,... | collective-permute-start | bytes 245768 | tf_op jit(solution)/shard_map/ppermute | solution.py:487
  69.2 5.7 %collective-permute-start.12 = (bf16[4,80,128]{2,1,0:T(8,128)(2,1)S(1)}, bf16[4,80,128]{2,1,0:T(8,128)(2,1)S(1)}, u32[]{:S(2)}, u32[]{:S(2)}) collective-permute-start(bf16[4,80,128]{2,1,0:T(8,128)(2,1)S(1)} %get-tuple-element.30), channel_id=1, source_target_pairs={{0,4},{1,5},{2,6},{3,7},{4,0},{5,1},{6,2},{7,3},{8,12},{9,13},{10,... | collective-permute-start | bytes 245768 | tf_op jit(solution)/shard_map/ppermute | solution.py:487
  69.5 5.3 %collective-permute-start.11 = (bf16[4,80,128]{2,1,0:T(8,128)(2,1)S(1)}, bf16[4,80,128]{2,1,0:T(8,128)(2,1)S(1)}, u32[]{:S(2)}, u32[]{:S(2)}) collective-permute-start(bf16[4,80,128]{2,1,0:T(8,128)(2,1)S(1)} %get-tuple-element.30), channel_id=1, source_target_pairs={{0,2},{1,3},{2,0},{3,1},{4,6},{5,7},{6,4},{7,5},{8,10},{9,11},{10,... | collective-permute-start | bytes 245768 | tf_op jit(solution)/shard_map/ppermute | solution.py:487
  74.9 12.7 %collective-permute-start.16 = (bf16[16,80,128]{2,1,0:T(8,128)(2,1)S(1)}, bf16[16,80,128]{2,1,0:T(8,128)(2,1)S(1)}, u32[]{:S(2)}, u32[]{:S(2)}) collective-permute-start(bf16[16,80,128]{2,1,0:T(8,128)(2,1)S(1)} %pad_maximum_fusion.1), channel_id=1, source_target_pairs={{0,96},{1,25},{2,98},{3,27},{4,100},{5,29},{6,102},{7,31},{8,104},... | collective-permute-start | bytes 983048 | tf_op jit(solution)/shard_map/ppermute | solution.py:487
  76.3 11.2 %collective-permute-start.15 = (bf16[16,80,128]{2,1,0:T(8,128)(2,1)S(1)}, bf16[16,80,128]{2,1,0:T(8,128)(2,1)S(1)}, u32[]{:S(2)}, u32[]{:S(2)}) collective-permute-start(bf16[16,80,128]{2,1,0:T(8,128)(2,1)S(1)} %pad_maximum_fusion.1), channel_id=1, source_target_pairs={{0,64},{1,17},{2,66},{3,19},{4,68},{5,21},{6,70},{7,23},{8,72},{9,... | collective-permute-start | bytes 983048 | tf_op jit(solution)/shard_map/ppermute | solution.py:487
  76.5 10.9 %collective-permute-start.14 = (bf16[16,80,128]{2,1,0:T(8,128)(2,1)S(1)}, bf16[16,80,128]{2,1,0:T(8,128)(2,1)S(1)}, u32[]{:S(2)}, u32[]{:S(2)}) collective-permute-start(bf16[16,80,128]{2,1,0:T(8,128)(2,1)S(1)} %pad_maximum_fusion.1), channel_id=1, source_target_pairs={{0,32},{1,9},{2,34},{3,11},{4,36},{5,13},{6,38},{7,15},{8,40},{9,1... | collective-permute-start | bytes 983048 | tf_op jit(solution)/shard_map/ppermute | solution.py:487
  87.7 9.8 %collective-permute-start.17 = (bf16[64,80,128]{2,1,0:T(8,128)(2,1)S(1)}, bf16[64,80,128]{2,1,0:T(8,128)(2,1)S(1)}, u32[]{:S(2)}, u32[]{:S(2)}) collective-permute-start(bf16[64,80,128]{2,1,0:T(8,128)(2,1)S(1)} %constant_dynamic-update-slice_fusion.own_ref), channel_id=1, source_target_pairs={{0,1},{1,0},{2,3},{3,2},{4,5},{5,4},{6,7},{7,6},{8,9},{9,8},{10,11... | collective-permute-start | bytes 3932168 | tf_op jit(solution)/shard_map/ppermute | solution.py:487

commit v4 on v3

--- a/solution.py
+++ b/solution.py
@@ -1,3 +1,5 @@
+import functools
+
 import jax
 import jax.numpy as jnp
 from jax import lax
@@ -17,7 +19,7 @@
 BLK = 128
 TPB = 512
 PIECE = 80
-CH = 80
+CH = 72
 AXES = ("dp", "graph")
 HI = lax.Precision.HIGHEST
 
@@ -96,7 +98,8 @@
     ecot_ref,
     energy_ref,
     pos_out_ref,
-    node_ref,
+    own_s_ref,
+    cot_ref,
     pay_ref,
     h_s,
     meta_s,
@@ -131,6 +134,7 @@
     wt_ref,
     wo_ref,
     sems,
+    wtt_s,
 ):
     loads = [
         pltpu.make_async_copy(far, near, sems.at[i])
@@ -282,7 +286,7 @@
             )
         dm2 = jnp.concatenate(halves, axis=0)
         dm2_s[edges, :] = dm2
-        dmsg = ug + nt(dm2, wt_ref[...])
+        dmsg = ug + nn(dm2, wtt_s[...])
         dpre_s[edges, :] = (dmsg * f_s[s].astype(F32)).astype(BF)
         drad = (dmsg * sg_s[s].astype(F32)).astype(BF)
         drad_s[edges, :] = drad
@@ -297,28 +301,25 @@
         top = dv.astype(BF).astype(F32)
         dv_s[:, edges] = jnp.concatenate([top, dv - top, jnp.zeros((10, ES), F32)], axis=0).astype(BF)
 
+    wtt_s[...] = jnp.transpose(wt_ref[...])
     for s in range(NG):
         backward(s)
 
     own = pl.multiple_of(me * AT, AT)
     ohs_own = oht_s[pl.ds(own, AT), :]
     ohd_own = oht_s[pl.ds(ATOMS + own, AT), :]
-    dpre = dpre_s[...]
-    s_src = (0.5 * nn(ohs_own, dpre)).astype(BF)
-    s_dst = (0.5 * nn(ohd_own, dpre)).astype(BF)
-    node_ref[...] = (
-        cot_s[pl.ds(own, AT), 0:1] * we + nt(s_src, ws_ref[...]) + nt(s_dst, wd_ref[...])
-    )
-    pos = nt(dv_s[...], ohd_own) - nt(dv_s[...], ohs_own)
-    pos = pos[0:3] + pos[3:6]
-    for i in range(3):
-        pos_out_ref[i] = pos[i : i + 1]
-
     group = lax.div(my_slice, 4)
     block = pl.ds(pl.multiple_of(lax.rem(my_slice, 4) * 128, 128), 128)
     side = pl.ds(pl.multiple_of(group * ATOMS, ATOMS), ATOMS)
     rows_t = tn(h_s[:, block], oht_s[side, :]).astype(BF)
-    a_s[...] = 0.5 * nn(rows_t, dpre)
+    sums = nn(jnp.concatenate([rows_t, ohs_own, ohd_own], axis=0), dpre_s[...])
+    a_s[...] = 0.5 * sums[0:BLK]
+    own_s_ref[...] = (0.5 * sums[BLK : 2 * BLK]).astype(BF)
+    cot_ref[...] = cot_s[pl.ds(own, AT), :]
+    pos = nt(dv_s[...], ohd_own - ohs_own)
+    pos = pos[0:3] + pos[3:6]
+    for i in range(3):
+        pos_out_ref[i] = pos[i : i + 1]
 
     @pl.when(group == 0)
     def _():
@@ -356,11 +357,12 @@
         out_shape=(
             jax.ShapeDtypeStruct((1, 16), F32),
             jax.ShapeDtypeStruct((3, 1, AT), F32),
-            jax.ShapeDtypeStruct((AT, D), F32),
+            jax.ShapeDtypeStruct((2 * AT, D), BF),
+            jax.ShapeDtypeStruct((AT, 128), F32),
             jax.ShapeDtypeStruct((4, 4, CH, 128), BF),
         ),
-        in_specs=[sm] * 3 + [vm] * 2 + [pl.BlockSpec(memory_space=pl.ANY)] * 5 + [vm] * 2,
-        out_specs=(vm, vm, vm, vm),
+        in_specs=[sm] * 3 + [vm] * 2 + [pl.BlockSpec(memory_space=pltpu.HBM)] * 5 + [vm] * 2,
+        out_specs=(vm,) * 5,
         scratch_shapes=[
             V((ATOMS, D), BF),
             V((NG, 16, D), F32),
@@ -395,73 +397,107 @@
             V((D, D), BF),
             V((D, D), BF),
             pltpu.SemaphoreType.DMA((5,)),
+            V((D, D), BF),
         ],
-        compiler_params=pltpu.CompilerParams(vmem_limit_bytes=50 * 1024 * 1024),
+        compiler_params=pltpu.CompilerParams(vmem_limit_bytes=53760 * 1024),
         name="batch",
     )(me, part, u, own, other, ws, wd, wr, wt, wo, we, ecot)
 
 
-def place_kernel(x_ref, y_ref, slice_ref, own_ref, other_ref, gs_ref, gd_ref, gr_ref, gt_ref, go_ref, ge_ref, first, second, low, sems):
+def node_kernel(sums_ref, cot_ref, ws_ref, wd_ref, we_ref, out_ref):
+    out_ref[...] = (
+        cot_ref[:, 0:1] * we_ref[...].astype(F32)
+        + nt(sums_ref[0:AT, :], ws_ref[...])
+        + nt(sums_ref[AT : 2 * AT, :], wd_ref[...])
+    )
+
+
+def node(sums, cot, ws, wd, we):
+    vm = pl.BlockSpec(memory_space=pltpu.VMEM)
+    return pl.pallas_call(
+        node_kernel,
+        out_shape=jax.ShapeDtypeStruct((AT, D), F32),
+        in_specs=[vm] * 5,
+        out_specs=vm,
+        name="node",
+    )(sums, cot, ws, wd, we)
+
+
+def place_kernel(c, x_ref, y_ref, slice_ref, ref, *rest):
+    gs_ref, gd_ref, gr_ref, gt_ref, go_ref, ge_ref, first, second, low, radial, energy, sems = rest[-12:]
     x, y, mine = x_ref[0], y_ref[0], slice_ref[0]
-    core = mine & 1
-    for c, ref in ((0, own_ref), (1, other_ref)):
-        pc = core ^ c
-        my_u = jnp.where(pc == 0, x, y)
-
-        def body(i, carry, c=c, my_u=my_u, ref=ref):
-            u = lax.rem(my_u - lax.div(i, 4) + 4, 4)
-            kz = lax.rem(i, 4)
-            for k in range(4):
-                cols = slice(128 * k, 128 * (k + 1))
-                g = lax.bitwise_xor(mine, 2 * kz + c)
-                tile = ref[4 * i + k].astype(F32)
-                rows = pl.ds(pl.multiple_of(g * 128 + u * 32, 32), 32)
-                first[rows, cols] = tile[0:32]
-                second[rows, cols] = tile[32:64]
-                low[g * 4 + u, :, cols] = tile[64:72]
+    pc = (mine & 1) ^ c
+    my_u = jnp.where(pc == 0, x, y)
+
+    for kz in range(4):
+
+        def body(ku, carry, kz=kz):
+            u = lax.rem(my_u - ku + 4, 4)
+            rows = pl.ds(pl.multiple_of(u * 32, 32), 32)
+            for v in range(4):
+                cols = slice(128 * v, 128 * (v + 1))
+                tile = ref[16 * ku + 4 * kz + v].astype(F32)
+                first[kz, rows, cols] = tile[0:32]
+                second[kz, rows, cols] = tile[32:64]
+                low[4 * kz + u, :, cols] = tile[64:72]
             return carry
 
-        lax.fori_loop(0, 16, body, 0)
-    copies = [
-        pltpu.make_async_copy(near, far, sems.at[i])
-        for i, (near, far) in enumerate(
-            (
-                (first.at[0:D], gs_ref),
-                (first.at[D : 2 * D], gd_ref),
-                (second.at[0:D], gt_ref),
-                (second.at[D : 2 * D], go_ref),
-            )
-        )
-    ]
-    for copy in copies:
-        copy.start()
-    for i in range(K // 4):
-        gr_ref[4 * i : 4 * i + 4, :] = low[i, 0:4, :]
-    for g in range(4):
-        ge_ref[:, 128 * g : 128 * (g + 1)] = low[4 * g, 4:5, 0:128]
-    for copy in copies:
-        copy.wait()
-
-
-def place(x, y, part, own, other):
+        lax.fori_loop(0, 4, body, 0, unroll=True)
+        g = lax.bitwise_xor(mine, 2 * kz + c)
+        block = pl.ds(pl.multiple_of((g & 3) * 128, 128), 128)
+
+        def send(near, far, sem):
+            pltpu.make_async_copy(near, far, sem).start()
+
+        @pl.when(g < 4)
+        def _():
+            send(first.at[kz], gs_ref.at[block], sems.at[0, kz])
+            send(second.at[kz], gt_ref.at[block], sems.at[1, kz])
+
+        @pl.when(g >= 4)
+        def _():
+            send(first.at[kz], gd_ref.at[block], sems.at[0, kz])
+            send(second.at[kz], go_ref.at[block], sems.at[1, kz])
+
+        for u in range(4):
+            radial[kz, 4 * u : 4 * u + 4, :] = low[4 * kz + u, 0:4, :]
+        send(radial.at[kz], gr_ref.at[pl.ds(pl.multiple_of(g * 16, 16), 16)], sems.at[2, kz])
+
+        @pl.when(g < 4)
+        def _():
+            energy[kz] = low[4 * kz, 4:5, 0:128]
+            copy = pltpu.make_async_copy(energy.at[kz], ge_ref.at[:, block], sems.at[3, kz])
+            copy.start()
+            copy.wait()
+
+    for kz in range(4):
+        pltpu.make_async_copy(first.at[kz], gs_ref.at[0:128], sems.at[0, kz]).wait()
+        pltpu.make_async_copy(second.at[kz], gt_ref.at[0:128], sems.at[1, kz]).wait()
+        pltpu.make_async_copy(radial.at[kz], gr_ref.at[0:16], sems.at[2, kz]).wait()
+
+
+def place(c, x, y, part, pieces, *before):
     vm = pl.BlockSpec(memory_space=pltpu.VMEM)
     sm = pl.BlockSpec(memory_space=pltpu.SMEM)
     far = pl.BlockSpec(memory_space=pl.ANY)
     big = jax.ShapeDtypeStruct((D, D), F32)
     return pl.pallas_call(
-        place_kernel,
+        functools.partial(place_kernel, c),
         out_shape=(big, big, jax.ShapeDtypeStruct((K, D), F32), big, big, jax.ShapeDtypeStruct((1, D), F32)),
-        in_specs=[sm] * 3 + [vm] * 2,
-        out_specs=(far, far, vm, far, far, vm),
+        in_specs=[sm] * 3 + [vm] + [far] * len(before),
+        out_specs=(far,) * 6,
         scratch_shapes=[
-            pltpu.VMEM((2 * D, D), F32),
-            pltpu.VMEM((2 * D, D), F32),
-            pltpu.VMEM((K // 4, 8, D), F32),
-            pltpu.SemaphoreType.DMA((4,)),
+            pltpu.VMEM((4, 128, D), F32),
+            pltpu.VMEM((4, 128, D), F32),
+            pltpu.VMEM((16, 8, D), F32),
+            pltpu.VMEM((4, 16, D), F32),
+            pltpu.VMEM((4, 1, 128), F32),
+            pltpu.SemaphoreType.DMA((4, 4)),
         ],
-        compiler_params=pltpu.CompilerParams(vmem_limit_bytes=40 * 1024 * 1024),
+        input_output_aliases={4 + i: i for i in range(len(before))},
+        compiler_params=pltpu.CompilerParams(vmem_limit_bytes=30 * 1024 * 1024),
         name="place",
-    )(x, y, part, own, other)
+    )(x, y, part, pieces, *before)
 
 
 def moves(fn):
@@ -537,9 +573,11 @@
     )[None]
     own = join(piece, *[shift(piece, zl=k) for k in (1, 2, 3)])
     other = shift(own, c=1)
-    energy, pos_grad, node_grad, payload = batch(
-        me, part, u, own, other, w_src, w_dst, w_radial, w_trip, w_out, w_energy.reshape(1, D), energy_cot
+    we = w_energy.reshape(1, D)
+    energy, pos_grad, sums, cot, payload = batch(
+        me, part, u, own, other, w_src, w_dst, w_radial, w_trip, w_out, we, energy_cot
     )
+    node_grad = node(sums, cot, w_src, w_dst, we)
     one, three, two = [shift(payload[k], u=k) for k in ORDER]
     held = total(payload[0], two, one, three)
     one, three, two = [shift(held, v=k) for k in ORDER]
@@ -548,7 +586,8 @@
     held = join(held, *[shift(held, zl=k) for k in (1, 2, 3)])
     one, three, two = [shift(held, u=k) for k in ORDER]
     held = join(held, one, two, three)
-    gs, gd, gr, gt, go, ge = place(x, y, part, held, shift(held, c=1))
+    other = shift(held, c=1)
+    gs, gd, gr, gt, go, ge = place(1, x, y, part, other, *place(0, x, y, part, held))
     return (energy, jnp.swapaxes(pos_grad, 0, 1), node_grad[None], gs, gd, gr, gt, go, ge.reshape(D))
 
 

time: 101 us -> 96.3 us (0.953)
  waiting for transfers between devices: 33.5 us -> 29.2 us
  local copies, waits for them, and re-layouts: 6.6 us -> 2.45 us
  Pallas kernels: 25 us -> 28.3 us
    pallas_call x1 -> x3, Pallas kernels: 3.32 us -> 7.64 us  [the longest x2 5.28 us: place(): pl.pallas_call(functools.partial(place_kernel, c), out_shape=(big, big, j...]
    ppermute x18, waiting for transfers between devices: 33.5 us -> 29.2 us  [shift(): return lax.ppermute(value, AXES, moves(fn))]
    unnamed x17 -> x15, local copies, waits for them, and re-layouts: 5.86 us -> 1.7 us
    pallas_call x1, Pallas kernels: 20.1 us -> 19.1 us  [batch(): pl.pallas_call(main_kernel, out_shape=(jax.ShapeDtypeStruct((1, 16), F32)...]
  transfers between devices with their start and end apart: 18 -> 18, of which waited for: 12 -> 11; matrix products, arithmetic and copies ran while one was open for 1% -> 1% of each run, Pallas kernels for 0% -> 5%
where the time goes in v4:
time: 96.3 us; the launch traced here: 96 us
  starting transfers between devices  32.7 us (34%)
  waiting for transfers between devices  29.2 us (30%)
  Pallas kernels  28.3 us (29%)
  local copies, waits for them, and re-layouts  2.45 us (3%)
  between operations  2.28 us (2%)
  other arithmetic  1.08 us (1%)
    ppermute x18, starting transfers between devices, shift(): return lax.ppermute(value, AXES, moves(fn))  32.7 us
    ppermute x18, waiting for transfers between devices, shift(): return lax.ppermute(value, AXES, moves(fn))  29.2 us
    pallas_call x1, Pallas kernels, batch(): pl.pallas_call(main_kernel, out_shape=(jax.ShapeDtypeStruct((1, 16), F32)...  19.1 us
    pallas_call x2, Pallas kernels, place(): pl.pallas_call(functools.partial(place_kernel, c), out_shape=(big, big, j...  5.28 us
    pallas_call x1, Pallas kernels, node(): pl.pallas_call(node_kernel, out_shape=jax.ShapeDtypeStruct((AT, D), F32),...  2.36 us
  transfers between devices with their start and end apart: 18, of which 11 were waited for; matrix products, arithmetic and copies ran while one was open for 1% of the time, Pallas kernels for 5%

profile of v4, /device:TPU:1, one launch (start us, length us, event | category | flops | bytes accessed | tf_op | source)
XLA Modules:
  0.0 96.0 jit_solution(7438800981423559400)
XLA Ops:
  1.9 1.6 %pack.1 = bf16[80,512]{1,0:T(8,128)(2,1)} custom-call(s32[1]{0:T(128)} %bitcast.me_ref, bf16[64,512]{1,0:T(8,128)(2,1)} %bitcast.25, f32[3,1,64]{2,1,0:T(1,128)} %bitcast.27, s32[1,256]{1,0:T(1,128)} %src_ref.1, s32[1,256]{1,0:T(1,128)} %dst_ref.1, s32[1,1]{1,0:T(1,128)S(6)} %copy.43.ec_ref, s32[1,1024]{1,0:T(1,128)} %tin_ref.1, s32[1,1024]{1,0:T(1,128)} %tout_ref.1, ...), custom_call_target="tpu_custom_call" | custom-call | tf_op jit(solution)/shard_map/pack/pallas_call | solution.py:76
  3.6 5.2 %collective-permute-start.2 = (bf16[1,80,512]{2,1,0:T(8,128)(2,1)}, bf16[1,80,512]{2,1,0:T(8,128)(2,1)S(1)}, u32[]{:S(2)}, u32[]{:S(2)}) collective-permute-start(bf16[1,80,512]{2,1,0:T(8,128)(2,1)} %bitcast.20), channel_id=1, source_target_pairs={{0,6},{1,7},{2,4},{3,5},{4,2},{5,3},{6,0},{7,1},{8,14},{9,15},{10,... | collective-permute-start | bytes 245768 | tf_op jit(solution)/shard_map/ppermute | solution.py:523
  8.7 0.0 collective-permute-start.1
  8.7 0.3 collective-permute-start
  9.0 1.9 %collective-permute-done.2 = bf16[1,80,512]{2,1,0:T(8,128)(2,1)S(1)} collective-permute-done((bf16[1,80,512]{2,1,0:T(8,128)(2,1)}, bf16[1,80,512]{2,1,0:T(8,128)(2,1)S(1)}, u32[]{:S(2)}, u32[]{:S(2)}) %collective-permute-start.2) | collective-permute-done | bytes 81952 | tf_op jit(solution)/shard_map/ppermute | solution.py:523
  10.9 4.9 %collective-permute-done.1 = bf16[1,80,512]{2,1,0:T(8,128)(2,1)S(1)} collective-permute-done((bf16[1,80,512]{2,1,0:T(8,128)(2,1)}, bf16[1,80,512]{2,1,0:T(8,128)(2,1)S(1)}, u32[]{:S(2)}, u32[]{:S(2)}) %collective-permute-start.1) | collective-permute-done | bytes 81952 | tf_op jit(solution)/shard_map/ppermute | solution.py:523
  15.7 0.0 collective-permute-done
  15.8 0.9 pad_maximum_fusion.own_ref
  16.7 0.8 collective-permute-start.3
  17.5 0.7 reshape.44.we_ref
  18.1 0.0 copy-start.3
  18.1 0.6 collective-permute-done.3.other_ref
  18.7 0.0 copy-start
  18.7 0.9 copy-done
  19.6 0.0 copy-start.4
  19.6 0.7 copy-done.4
  20.3 19.1 %batch.1 = (f32[1,16]{1,0:T(1,128)}, f32[3,1,64]{2,1,0:T(1,128)}, bf16[128,512]{1,0:T(8,128)(2,1)S(1)}, f32[64,128]{1,0:T(8,128)S(1)}, bf16[4,4,72,128]{3,2,1,0:T(8,128)(2,1)S(1)}) custom-call(s32[1]{0:T(128)} %bitcast.me_ref, s32[1]{0:T(128)} %bitcast.1.slice_ref, s32[1]{0:T(128)} %bitcast.2.u_ref, bf16[4,80,512]{2,1,0:T(8,128)(2,1)S(1)} %pad_maximum_fusion.own_ref, ...), custom_call_target="tpu_custom_call" | custom-call | tf_op jit(solution)/shard_map/batch/pallas_call | solution.py:355
  39.4 0.0 copy-done.3
  39.4 0.0 copy-start.1
  39.4 0.0 copy-start.2
  39.4 2.9 %collective-permute-start.4 = (bf16[4,72,128]{2,1,0:T(8,128)(2,1)S(1)}, bf16[4,72,128]{2,1,0:T(8,128)(2,1)S(1)}, u32[]{:S(2)}, u32[]{:S(2)}) collective-permute-start(bf16[4,72,128]{2,1,0:T(8,128)(2,1)S(1)} %get-tuple-element.45), channel_id=1, source_target_pairs={{0,64},{1,17},{2,66},{3,19},{4,68},{5,21},{6,70},{7,23},{8,72},{9,... | collective-permute-start | bytes 221192 | tf_op jit(solution)/shard_map/ppermute | solution.py:523
  42.3 0.8 collective-permute-start.6
  43.1 0.7 collective-permute-start.5
  43.8 0.4 collective-permute-done.4
  44.2 1.3 %collective-permute-done.6 = bf16[4,72,128]{2,1,0:T(8,128)(2,1)S(1)} collective-permute-done((bf16[4,72,128]{2,1,0:T(8,128)(2,1)S(1)}, bf16[4,72,128]{2,1,0:T(8,128)(2,1)S(1)}, u32[]{:S(2)}, u32[]{:S(2)}) %collective-permute-start.6) | collective-permute-done | bytes 73760 | tf_op jit(solution)/shard_map/ppermute | solution.py:523
  45.5 2.0 %collective-permute-done.5 = bf16[4,72,128]{2,1,0:T(8,128)(2,1)S(1)} collective-permute-done((bf16[4,72,128]{2,1,0:T(8,128)(2,1)S(1)}, bf16[4,72,128]{2,1,0:T(8,128)(2,1)S(1)}, u32[]{:S(2)}, u32[]{:S(2)}) %collective-permute-start.5) | collective-permute-done | bytes 73760 | tf_op jit(solution)/shard_map/ppermute | solution.py:523
  47.5 2.6 %collective-permute-start.9 = (bf16[4,72,128]{2,1,0:T(8,128)(2,1)S(1)}, bf16[4,72,128]{2,1,0:T(8,128)(2,1)S(1)}, u32[]{:S(2)}, u32[]{:S(2)}) collective-permute-start(bf16[4,72,128]{2,1,0:T(8,128)(2,1)S(1)} %fusion.1), channel_id=1, source_target_pairs={{0,24},{1,97},{2,26},{3,99},{4,28},{5,101},{6,30},{7,103},{8,0},{9... | collective-permute-start | bytes 221192 | tf_op jit(solution)/shard_map/ppermute | solution.py:523
  50.1 0.0 collective-permute-start.8
  50.1 1.7 %collective-permute-start.7 = (bf16[4,72,128]{2,1,0:T(8,128)(2,1)S(1)}, bf16[4,72,128]{2,1,0:T(8,128)(2,1)S(1)}, u32[]{:S(2)}, u32[]{:S(2)}) collective-permute-start(bf16[4,72,128]{2,1,0:T(8,128)(2,1)S(1)} %fusion.1), channel_id=1, source_target_pairs={{0,16},{1,65},{2,18},{3,67},{4,20},{5,69},{6,22},{7,71},{8,24},{9,... | collective-permute-start | bytes 221192 | tf_op jit(solution)/shard_map/ppermute | solution.py:523
  51.8 0.0 collective-permute-done.9
  51.8 3.5 %collective-permute-done.8 = bf16[4,72,128]{2,1,0:T(8,128)(2,1)S(1)} collective-permute-done((bf16[4,72,128]{2,1,0:T(8,128)(2,1)S(1)}, bf16[4,72,128]{2,1,0:T(8,128)(2,1)S(1)}, u32[]{:S(2)}, u32[]{:S(2)}) %collective-permute-start.8) | collective-permute-done | bytes 73760 | tf_op jit(solution)/shard_map/ppermute | solution.py:523
  55.3 0.0 collective-permute-done.7
  55.4 4.8 %collective-permute-start.10 = (bf16[4,72,128]{2,1,0:T(8,128)(2,1)S(1)}, bf16[4,72,128]{2,1,0:T(8,128)(2,1)S(1)}, u32[]{:S(2)}, u32[]{:S(2)}) collective-permute-start(bf16[4,72,128]{2,1,0:T(8,128)(2,1)S(1)} %add_convert_fusion.1), channel_id=1, source_target_pairs={{0,134},{1,135},{2,132},{3,133},{4,130},{5,131},{6,128},{7,129},{8... | collective-permute-start | bytes 221192 | tf_op jit(solution)/shard_map/ppermute | solution.py:523
  60.1 2.2 %collective-permute-done.10 = bf16[4,72,128]{2,1,0:T(8,128)(2,1)S(1)} collective-permute-done((bf16[4,72,128]{2,1,0:T(8,128)(2,1)S(1)}, bf16[4,72,128]{2,1,0:T(8,128)(2,1)S(1)}, u32[]{:S(2)}, u32[]{:S(2)}) %collective-permute-start.10) | collective-permute-done | bytes 73760 | tf_op jit(solution)/shard_map/ppermute | solution.py:523
  62.3 1.3 %collective-permute-start.13 = (bf16[4,72,128]{2,1,0:T(8,128)(2,1)S(1)}, bf16[4,72,128]{2,1,0:T(8,128)(2,1)S(1)}, u32[]{:S(2)}, u32[]{:S(2)}) collective-permute-start(bf16[4,72,128]{2,1,0:T(8,128)(2,1)S(1)} %get-tuple-element.44), channel_id=1, source_target_pairs={{0,6},{1,7},{2,4},{3,5},{4,2},{5,3},{6,0},{7,1},{8,14},{9,15},{10,... | collective-permute-start | bytes 221192 | tf_op jit(solution)/shard_map/ppermute | solution.py:523
  63.6 0.4 collective-permute-start.12
  64.0 1.9 %collective-permute-start.11 = (bf16[4,72,128]{2,1,0:T(8,128)(2,1)S(1)}, bf16[4,72,128]{2,1,0:T(8,128)(2,1)S(1)}, u32[]{:S(2)}, u32[]{:S(2)}) collective-permute-start(bf16[4,72,128]{2,1,0:T(8,128)(2,1)S(1)} %get-tuple-element.44), channel_id=1, source_target_pairs={{0,2},{1,3},{2,0},{3,1},{4,6},{5,7},{6,4},{7,5},{8,10},{9,11},{10,... | collective-permute-start | bytes 221192 | tf_op jit(solution)/shard_map/ppermute | solution.py:523
  65.9 1.6 %collective-permute-done.13 = bf16[4,72,128]{2,1,0:T(8,128)(2,1)S(1)} collective-permute-done((bf16[4,72,128]{2,1,0:T(8,128)(2,1)S(1)}, bf16[4,72,128]{2,1,0:T(8,128)(2,1)S(1)}, u32[]{:S(2)}, u32[]{:S(2)}) %collective-permute-start.13) | collective-permute-done | bytes 73760 | tf_op jit(solution)/shard_map/ppermute | solution.py:523
  67.5 1.5 %collective-permute-done.12 = bf16[4,72,128]{2,1,0:T(8,128)(2,1)S(1)} collective-permute-done((bf16[4,72,128]{2,1,0:T(8,128)(2,1)S(1)}, bf16[4,72,128]{2,1,0:T(8,128)(2,1)S(1)}, u32[]{:S(2)}, u32[]{:S(2)}) %collective-permute-start.12) | collective-permute-done | bytes 73760 | tf_op jit(solution)/shard_map/ppermute | solution.py:523
  69.0 0.0 collective-permute-done.11
  69.0 1.3 %collective-permute-start.16 = (bf16[16,72,128]{2,1,0:T(8,128)(2,1)S(1)}, bf16[16,72,128]{2,1,0:T(8,128)(2,1)S(1)}, u32[]{:S(2)}, u32[]{:S(2)}) collective-permute-start(bf16[16,72,128]{2,1,0:T(8,128)(2,1)S(1)} %pad_maximum_fusion.1), channel_id=1, source_target_pairs={{0,96},{1,25},{2,98},{3,27},{4,100},{5,29},{6,102},{7,31},{8,104},... | collective-permute-start | bytes 884744 | tf_op jit(solution)/shard_map/ppermute | solution.py:523
  70.3 0.4 collective-permute-start.15
  70.7 0.3 collective-permute-start.14
  71.0 0.0 copy-done.1
  71.0 0.0 copy-done.2
  71.0 9.5 %collective-permute-done.14 = bf16[16,72,128]{2,1,0:T(8,128)(2,1)S(1)} collective-permute-done((bf16[16,72,128]{2,1,0:T(8,128)(2,1)S(1)}, bf16[16,72,128]{2,1,0:T(8,128)(2,1)S(1)}, u32[]{:S(2)}, u32[]{:S(2)}) %collective-permute-start.14) | collective-permute-done | bytes 294944 | tf_op jit(solution)/shard_map/ppermute | solution.py:523
  80.6 0.0 collective-permute-done.15
  80.6 0.0 collective-permute-done.16
  80.7 7.5 %collective-permute-start.17 = (bf16[64,72,128]{2,1,0:T(8,128)(2,1)S(1)}, bf16[64,72,128]{2,1,0:T(8,128)(2,1)S(1)}, u32[]{:S(2)}, u32[]{:S(2)}) collective-permute-start(bf16[64,72,128]{2,1,0:T(8,128)(2,1)S(1)} %constant_dynamic-update-slice_fusion.ref), channel_id=1, source_target_pairs={{0,1},{1,0},{2,3},{3,2},{4,5},{5,4},{6,7},{7,6},{8,9},{9,8},{10,11... | collective-permute-start | bytes 3538952 | tf_op jit(solution)/shard_map/ppermute | solution.py:523
  88.2 2.4 %node.1 = f32[64,512]{1,0:T(8,128)} custom-call(bf16[128,512]{1,0:T(8,128)(2,1)} %copy-done.1, f32[64,128]{1,0:T(8,128)} %copy-done.2, bf16[512,512]{1,0:T(8,128)(2,1)} %ws_ref.1, bf16[512,512]{1,0:T(8,128)(2,1)} %wd_ref.1, bf16[1,512]{1,0:T(2,128)(2,1)} %copy-done.3), custom_call_target="tpu_custom_call" | custom-call | tf_op jit(solution)/shard_map/node/pallas_call | solution.py:417
  90.5 2.6 %place.2 = (f32[512,512]{1,0:T(8,128)}, f32[512,512]{1,0:T(8,128)}, f32[128,512]{1,0:T(8,128)}, f32[512,512]{1,0:T(8,128)}, f32[512,512]{1,0:T(8,128)}, /*index=5*/f32[1,512]{1,0:T(1,128)}) custom-call(s32[1]{0:T(128)} %bitcast.8.x_ref, s32[1]{0:T(128)} %bitcast.9.y_ref, s32[1]{0:T(128)} %bitcast.1.slice_ref, ...), custom_call_target="tpu_custom_call" | custom-call | tf_op jit(solution)/shard_map/place/pallas_call | solution.py:484
  93.2 0.0 collective-permute-done.17.ref
  93.2 2.6 %place.3 = (f32[512,512]{1,0:T(8,128)}, f32[512,512]{1,0:T(8,128)}, f32[128,512]{1,0:T(8,128)}, f32[512,512]{1,0:T(8,128)}, f32[512,512]{1,0:T(8,128)}, /*index=5*/f32[1,512]{1,0:T(1,128)}) custom-call(s32[1]{0:T(128)} %bitcast.8.x_ref, s32[1]{0:T(128)} %bitcast.9.y_ref, ...), custom_call_target="tpu_custom_call", output_to_operand_aliasing={{0}: (4, {}), {1}: (5, {}), {2}: (6, {}), {3}: (7, {}), {4}... | custom-call | tf_op jit(solution)/shard_map/place/pallas_call | solution.py:484
  (11 shorter events, 0.3 us)
Async XLA Ops:
  3.6 7.3 %collective-permute-start.2 = (bf16[1,80,512]{2,1,0:T(8,128)(2,1)}, bf16[1,80,512]{2,1,0:T(8,128)(2,1)S(1)}, u32[]{:S(2)}, u32[]{:S(2)}) collective-permute-start(bf16[1,80,512]{2,1,0:T(8,128)(2,1)} %bitcast.20), channel_id=1, source_target_pairs={{0,6},{1,7},{2,4},{3,5},{4,2},{5,3},{6,0},{7,1},{8,14},{9,15},{10,... | collective-permute-start | bytes 245768 | tf_op jit(solution)/shard_map/ppermute | solution.py:523
  8.7 7.0 %collective-permute-start.1 = (bf16[1,80,512]{2,1,0:T(8,128)(2,1)}, bf16[1,80,512]{2,1,0:T(8,128)(2,1)S(1)}, u32[]{:S(2)}, u32[]{:S(2)}) collective-permute-start(bf16[1,80,512]{2,1,0:T(8,128)(2,1)} %bitcast.21), channel_id=1, source_target_pairs={{0,4},{1,5},{2,6},{3,7},{4,0},{5,1},{6,2},{7,3},{8,12},{9,13},{10,... | collective-permute-start | bytes 245768 | tf_op jit(solution)/shard_map/ppermute | solution.py:523
  8.7 7.0 %collective-permute-start = (bf16[1,80,512]{2,1,0:T(8,128)(2,1)}, bf16[1,80,512]{2,1,0:T(8,128)(2,1)S(1)}, u32[]{:S(2)}, u32[]{:S(2)}) collective-permute-start(bf16[1,80,512]{2,1,0:T(8,128)(2,1)} %bitcast.22), channel_id=1, source_target_pairs={{0,2},{1,3},{2,0},{3,1},{4,6},{5,7},{6,4},{7,5},{8,10},{9,11},{10,... | collective-permute-start | bytes 245768 | tf_op jit(solution)/shard_map/ppermute | solution.py:523
  16.7 2.0 %collective-permute-start.3 = (bf16[4,80,512]{2,1,0:T(8,128)(2,1)S(1)}, bf16[4,80,512]{2,1,0:T(8,128)(2,1)S(1)}, u32[]{:S(2)}, u32[]{:S(2)}) collective-permute-start(bf16[4,80,512]{2,1,0:T(8,128)(2,1)S(1)} %pad_maximum_fusion.own_ref), channel_id=1, source_target_pairs={{0,1},{1,0},{2,3},{3,2},{4,5},{5,4},{6,7},{7,6},{8,9},{9,8},{10,11... | collective-permute-start | bytes 983048 | tf_op jit(solution)/shard_map/ppermute | solution.py:523
  18.1 21.2 %copy-start.3 = (bf16[1,512]{1,0:T(2,128)(2,1)}, bf16[1,512]{1,0:T(2,128)(2,1)S(1)}, u32[]{:S(2)}) copy-start(bf16[1,512]{1,0:T(2,128)(2,1)S(1)} %reshape.44.we_ref) | copy-start | bytes 3076
  18.7 0.9 copy-start
  19.6 0.7 copy-start.4
  39.4 31.6 %copy-start.1 = (bf16[128,512]{1,0:T(8,128)(2,1)}, bf16[128,512]{1,0:T(8,128)(2,1)S(1)}, u32[]{:S(2)}) copy-start(bf16[128,512]{1,0:T(8,128)(2,1)S(1)} %get-tuple-element.28.sums_ref) | copy-start | bytes 393220
  39.4 31.6 %copy-start.2 = (f32[64,128]{1,0:T(8,128)}, f32[64,128]{1,0:T(8,128)S(1)}, u32[]{:S(2)}) copy-start(f32[64,128]{1,0:T(8,128)S(1)} %get-tuple-element.29.cot_ref) | copy-start | bytes 98308
  39.4 4.8 %collective-permute-start.4 = (bf16[4,72,128]{2,1,0:T(8,128)(2,1)S(1)}, bf16[4,72,128]{2,1,0:T(8,128)(2,1)S(1)}, u32[]{:S(2)}, u32[]{:S(2)}) collective-permute-start(bf16[4,72,128]{2,1,0:T(8,128)(2,1)S(1)} %get-tuple-element.45), channel_id=1, source_target_pairs={{0,64},{1,17},{2,66},{3,19},{4,68},{5,21},{6,70},{7,23},{8,72},{9,... | collective-permute-start | bytes 221192 | tf_op jit(solution)/shard_map/ppermute | solution.py:523
  42.3 3.2 %collective-permute-start.6 = (bf16[4,72,128]{2,1,0:T(8,128)(2,1)S(1)}, bf16[4,72,128]{2,1,0:T(8,128)(2,1)S(1)}, u32[]{:S(2)}, u32[]{:S(2)}) collective-permute-start(bf16[4,72,128]{2,1,0:T(8,128)(2,1)S(1)} %get-tuple-element.46), channel_id=1, source_target_pairs={{0,96},{1,25},{2,98},{3,27},{4,100},{5,29},{6,102},{7,31},{8,104},... | collective-permute-start | bytes 221192 | tf_op jit(solution)/shard_map/ppermute | solution.py:523
  43.1 4.4 %collective-permute-start.5 = (bf16[4,72,128]{2,1,0:T(8,128)(2,1)S(1)}, bf16[4,72,128]{2,1,0:T(8,128)(2,1)S(1)}, u32[]{:S(2)}, u32[]{:S(2)}) collective-permute-start(bf16[4,72,128]{2,1,0:T(8,128)(2,1)S(1)} %get-tuple-element.47), channel_id=1, source_target_pairs={{0,32},{1,9},{2,34},{3,11},{4,36},{5,13},{6,38},{7,15},{8,40},{9,1... | collective-permute-start | bytes 221192 | tf_op jit(solution)/shard_map/ppermute | solution.py:523
  47.5 4.3 %collective-permute-start.9 = (bf16[4,72,128]{2,1,0:T(8,128)(2,1)S(1)}, bf16[4,72,128]{2,1,0:T(8,128)(2,1)S(1)}, u32[]{:S(2)}, u32[]{:S(2)}) collective-permute-start(bf16[4,72,128]{2,1,0:T(8,128)(2,1)S(1)} %fusion.1), channel_id=1, source_target_pairs={{0,24},{1,97},{2,26},{3,99},{4,28},{5,101},{6,30},{7,103},{8,0},{9... | collective-permute-start | bytes 221192 | tf_op jit(solution)/shard_map/ppermute | solution.py:523
  50.1 5.2 %collective-permute-start.8 = (bf16[4,72,128]{2,1,0:T(8,128)(2,1)S(1)}, bf16[4,72,128]{2,1,0:T(8,128)(2,1)S(1)}, u32[]{:S(2)}, u32[]{:S(2)}) collective-permute-start(bf16[4,72,128]{2,1,0:T(8,128)(2,1)S(1)} %fusion.1), channel_id=1, source_target_pairs={{0,8},{1,33},{2,10},{3,35},{4,12},{5,37},{6,14},{7,39},{8,16},{9,4... | collective-permute-start | bytes 221192 | tf_op jit(solution)/shard_map/ppermute | solution.py:523
  50.1 5.2 %collective-permute-start.7 = (bf16[4,72,128]{2,1,0:T(8,128)(2,1)S(1)}, bf16[4,72,128]{2,1,0:T(8,128)(2,1)S(1)}, u32[]{:S(2)}, u32[]{:S(2)}) collective-permute-start(bf16[4,72,128]{2,1,0:T(8,128)(2,1)S(1)} %fusion.1), channel_id=1, source_target_pairs={{0,16},{1,65},{2,18},{3,67},{4,20},{5,69},{6,22},{7,71},{8,24},{9,... | collective-permute-start | bytes 221192 | tf_op jit(solution)/shard_map/ppermute | solution.py:523
  55.4 6.9 %collective-permute-start.10 = (bf16[4,72,128]{2,1,0:T(8,128)(2,1)S(1)}, bf16[4,72,128]{2,1,0:T(8,128)(2,1)S(1)}, u32[]{:S(2)}, u32[]{:S(2)}) collective-permute-start(bf16[4,72,128]{2,1,0:T(8,128)(2,1)S(1)} %add_convert_fusion.1), channel_id=1, source_target_pairs={{0,134},{1,135},{2,132},{3,133},{4,130},{5,131},{6,128},{7,129},{8... | collective-permute-start | bytes 221192 | tf_op jit(solution)/shard_map/ppermute | solution.py:523
  62.3 5.2 %collective-permute-start.13 = (bf16[4,72,128]{2,1,0:T(8,128)(2,1)S(1)}, bf16[4,72,128]{2,1,0:T(8,128)(2,1)S(1)}, u32[]{:S(2)}, u32[]{:S(2)}) collective-permute-start(bf16[4,72,128]{2,1,0:T(8,128)(2,1)S(1)} %get-tuple-element.44), channel_id=1, source_target_pairs={{0,6},{1,7},{2,4},{3,5},{4,2},{5,3},{6,0},{7,1},{8,14},{9,15},{10,... | collective-permute-start | bytes 221192 | tf_op jit(solution)/shard_map/ppermute | solution.py:523
  63.6 5.4 %collective-permute-start.12 = (bf16[4,72,128]{2,1,0:T(8,128)(2,1)S(1)}, bf16[4,72,128]{2,1,0:T(8,128)(2,1)S(1)}, u32[]{:S(2)}, u32[]{:S(2)}) collective-permute-start(bf16[4,72,128]{2,1,0:T(8,128)(2,1)S(1)} %get-tuple-element.44), channel_id=1, source_target_pairs={{0,4},{1,5},{2,6},{3,7},{4,0},{5,1},{6,2},{7,3},{8,12},{9,13},{10,... | collective-permute-start | bytes 221192 | tf_op jit(solution)/shard_map/ppermute | solution.py:523
  64.0 5.0 %collective-permute-start.11 = (bf16[4,72,128]{2,1,0:T(8,128)(2,1)S(1)}, bf16[4,72,128]{2,1,0:T(8,128)(2,1)S(1)}, u32[]{:S(2)}, u32[]{:S(2)}) collective-permute-start(bf16[4,72,128]{2,1,0:T(8,128)(2,1)S(1)} %get-tuple-element.44), channel_id=1, source_target_pairs={{0,2},{1,3},{2,0},{3,1},{4,6},{5,7},{6,4},{7,5},{8,10},{9,11},{10,... | collective-permute-start | bytes 221192 | tf_op jit(solution)/shard_map/ppermute | solution.py:523
  69.0 11.6 %collective-permute-start.16 = (bf16[16,72,128]{2,1,0:T(8,128)(2,1)S(1)}, bf16[16,72,128]{2,1,0:T(8,128)(2,1)S(1)}, u32[]{:S(2)}, u32[]{:S(2)}) collective-permute-start(bf16[16,72,128]{2,1,0:T(8,128)(2,1)S(1)} %pad_maximum_fusion.1), channel_id=1, source_target_pairs={{0,96},{1,25},{2,98},{3,27},{4,100},{5,29},{6,102},{7,31},{8,104},... | collective-permute-start | bytes 884744 | tf_op jit(solution)/shard_map/ppermute | solution.py:523
  70.3 10.3 %collective-permute-start.15 = (bf16[16,72,128]{2,1,0:T(8,128)(2,1)S(1)}, bf16[16,72,128]{2,1,0:T(8,128)(2,1)S(1)}, u32[]{:S(2)}, u32[]{:S(2)}) collective-permute-start(bf16[16,72,128]{2,1,0:T(8,128)(2,1)S(1)} %pad_maximum_fusion.1), channel_id=1, source_target_pairs={{0,64},{1,17},{2,66},{3,19},{4,68},{5,21},{6,70},{7,23},{8,72},{9,... | collective-permute-start | bytes 884744 | tf_op jit(solution)/shard_map/ppermute | solution.py:523
  70.7 9.8 %collective-permute-start.14 = (bf16[16,72,128]{2,1,0:T(8,128)(2,1)S(1)}, bf16[16,72,128]{2,1,0:T(8,128)(2,1)S(1)}, u32[]{:S(2)}, u32[]{:S(2)}) collective-permute-start(bf16[16,72,128]{2,1,0:T(8,128)(2,1)S(1)} %pad_maximum_fusion.1), channel_id=1, source_target_pairs={{0,32},{1,9},{2,34},{3,11},{4,36},{5,13},{6,38},{7,15},{8,40},{9,1... | collective-permute-start | bytes 884744 | tf_op jit(solution)/shard_map/ppermute | solution.py:523
  80.7 12.5 %collective-permute-start.17 = (bf16[64,72,128]{2,1,0:T(8,128)(2,1)S(1)}, bf16[64,72,128]{2,1,0:T(8,128)(2,1)S(1)}, u32[]{:S(2)}, u32[]{:S(2)}) collective-permute-start(bf16[64,72,128]{2,1,0:T(8,128)(2,1)S(1)} %constant_dynamic-update-slice_fusion.ref), channel_id=1, source_target_pairs={{0,1},{1,0},{2,3},{3,2},{4,5},{5,4},{6,7},{7,6},{8,9},{9,8},{10,11... | collective-permute-start | bytes 3538952 | tf_op jit(solution)/shard_map/ppermute | solution.py:523

commit v5 on v4

--- a/solution.py
+++ b/solution.py
@@ -36,7 +36,9 @@
     return lax.dot_general(a, b, (((0,), (0,)), ((), ())), preferred_element_type=F32)
 
 
-def pack_kernel(me_ref, h_ref, pos_ref, src_ref, dst_ref, ec_ref, tin_ref, tout_ref, tc_ref, gid_ref, out_ref, meta):
+def pack_kernel(me_ref, h_ref, pos_ref, src_ref, dst_ref, ec_ref, tin_ref, tout_ref, tc_ref, gid_ref, ecot_ref, wr_ref, out_ref, cot_ref, wr_out, meta):
+    cot_ref[...] = ecot_ref[...]
+    wr_out[...] = wr_ref[...]
     odd = lax.rem(me_ref[0], 2)
     out_ref[0:AT, :] = h_ref[...]
 
@@ -70,17 +72,17 @@
     out_ref[AT:PIECE, :] = meta[...].astype(BF)
 
 
-def pack(me, h, pos, src, dst, ec, tin, tout, tc, gid):
+def pack(me, h, pos, src, dst, ec, tin, tout, tc, gid, ecot, wr):
     vm = pl.BlockSpec(memory_space=pltpu.VMEM)
     sm = pl.BlockSpec(memory_space=pltpu.SMEM)
     return pl.pallas_call(
         pack_kernel,
-        out_shape=jax.ShapeDtypeStruct((PIECE, D), BF),
-        in_specs=[sm, vm, vm, vm, vm, sm, vm, vm, sm, vm],
-        out_specs=vm,
+        out_shape=(jax.ShapeDtypeStruct((PIECE, D), BF), jax.ShapeDtypeStruct((1, 16), F32), jax.ShapeDtypeStruct((K, D), BF)),
+        in_specs=[sm, vm, vm, vm, vm, sm, vm, vm, sm, vm, vm, vm],
+        out_specs=(vm,) * 3,
         scratch_shapes=[pltpu.VMEM((16, D), F32)],
         name="pack",
-    )(me, h, pos, src, dst, ec, tin, tout, tc, gid)
+    )(me, h, pos, src, dst, ec, tin, tout, tc, gid, ecot, wr)
 
 
 def main_kernel(
@@ -91,7 +93,7 @@
     other_ref,
     ws_hbm,
     wd_hbm,
-    wr_hbm,
+    wr_ref,
     wt_hbm,
     wo_hbm,
     we_ref,
@@ -130,7 +132,6 @@
     r_s,
     ws_ref,
     wd_ref,
-    wr_ref,
     wt_ref,
     wo_ref,
     sems,
@@ -139,7 +140,7 @@
     loads = [
         pltpu.make_async_copy(far, near, sems.at[i])
         for i, (far, near) in enumerate(
-            ((ws_hbm, ws_ref), (wd_hbm, wd_ref), (wr_hbm, wr_ref), (wt_hbm, wt_ref), (wo_hbm, wo_ref))
+            ((ws_hbm, ws_ref), (wd_hbm, wd_ref), (wt_hbm, wt_ref), (wo_hbm, wo_ref))
         )
     ]
     for load in loads:
@@ -196,12 +197,8 @@
         inv = 1.0 / dist
         geo_s[s] = jnp.concatenate([src, dst, live, dist, vec * inv, inv], axis=0)
 
-    def forward(s):
-        geo = geo_s[s]
-        meta = meta_s[s]
-        unit = geo[4:7]
-        tc = 8.0 * meta[15:16, 256:384] + meta[15:16, 384:512]
-        cols = jnp.transpose(geo)
+    def gather(s):
+        cols = jnp.transpose(geo_s[s])
         ohs = onehot(lane_a == cols[:, 0:1])
         ohd = onehot(lane_a == cols[:, 1:2])
         ohd_s[s] = ohd
@@ -209,7 +206,9 @@
         basis = jnp.exp(-(t * t)) * cols[:, 2:3]
         bt_s[:, s * ES : (s + 1) * ES] = jnp.transpose(basis).astype(BF)
         q = nn(ohs, ab_s[0:ATOMS, :]) + nn(ohd, ab_s[ATOMS : 2 * ATOMS, :])
-        radial = nn(basis.astype(BF), wr_ref[...])
+        return s, cols, q, nn(basis.astype(BF), wr_ref[...])
+
+    def message(s, cols, q, radial):
         a = 1.0 + jnp.tanh(q)
         sil = q * a
         msg = (sil * radial).astype(BF)
@@ -218,6 +217,10 @@
         sg_s[s] = sil.astype(BF)
         m2 = nn(msg, wt_ref[...]).astype(BF)
         m2_s[s] = m2
+        meta = meta_s[s]
+        unit = geo_s[s][4:7]
+        tc = 8.0 * meta[15:16, 256:384] + meta[15:16, 384:512]
+        mixes = []
         for i in range(2):
             rows = slice(BLK * i, BLK * (i + 1))
             limit = jnp.concatenate([tc] * 4, axis=1) - float(TPB * i)
@@ -232,8 +235,24 @@
             )
             mix = count * gram
             tt_s[2 * s + i] = jnp.transpose(mix).astype(BF)
-            upd = msg[rows].astype(F32) + nn(mix.astype(BF), m2[rows])
+            mixes.append(mix.astype(BF))
+        return s, msg, m2, mixes
+
+    def update(s, msg, m2, mixes):
+        for i in range(2):
+            rows = slice(BLK * i, BLK * (i + 1))
+            upd = msg[rows].astype(F32) + nn(mixes[i], m2[rows])
             upd_s[s * ES + BLK * i : s * ES + BLK * (i + 1), :] = upd.astype(BF)
+
+    def staged(*stages):
+        waiting = [None] * len(stages)
+        for turn in range(NG + len(stages) - 1):
+            for k in reversed(range(len(stages))):
+                if k == 0:
+                    given = (turn,) if turn < NG else None
+                else:
+                    given = waiting[k - 1]
+                waiting[k] = None if given is None else stages[k](*given)
 
     for s in range(NG):
         geometry(s)
@@ -244,8 +263,7 @@
     ab_s[ATOMS : 2 * ATOMS, :] = (0.5 * nn(h, wd_ref[...])).astype(BF)
     for load in loads[2:]:
         load.wait()
-    for s in range(NG):
-        forward(s)
+    staged(gather, message, update)
 
     agg = nn(oht_s[ATOMS : 2 * ATOMS, :], upd_s[...]).astype(BF)
     aggb_s[...] = agg
@@ -266,30 +284,42 @@
     dzb_s[...] = dz
     ac_s[...] = nt(dz, wo_ref[...]).astype(BF)
 
-    def backward(s):
-        edges = slice(s * ES, (s + 1) * ES)
+    def fetch(s):
+        return s, nn(ohd_s[s], ac_s[...])
+
+    def mixed(s, ug):
         geo = geo_s[s]
         cols = jnp.transpose(geo)
-        ug = nn(ohd_s[s], ac_s[...])
         ugb = ug.astype(BF)
         m2 = m2_s[s]
-        halves, turns = [], []
+        halves, grams = [], []
         for i in range(2):
             rows = slice(BLK * i, BLK * (i + 1))
             halves.append(nn(tt_s[2 * s + i], ugb[rows]).astype(BF))
-            dgram = n_s[2 * s + i] * nt(ugb[rows], m2[rows])
-            both = dgram + jnp.transpose(dgram)
+            grams.append(n_s[2 * s + i] * nt(ugb[rows], m2[rows]))
+        dm2 = jnp.concatenate(halves, axis=0)
+        dm2_s[s * ES : (s + 1) * ES, :] = dm2
+        return s, geo, cols, ug, dm2, grams
+
+    def spread(s, geo, cols, ug, dm2, grams):
+        edges = slice(s * ES, (s + 1) * ES)
+        dmsg = ug + nn(dm2, wtt_s[...])
+        dpre_s[edges, :] = (dmsg * f_s[s].astype(F32)).astype(BF)
+        drad = (dmsg * sg_s[s].astype(F32)).astype(BF)
+        drad_s[edges, :] = drad
+        return s, geo, cols, drad, grams
+
+    def turn_back(s, geo, cols, drad, grams):
+        edges = slice(s * ES, (s + 1) * ES)
+        turns = []
+        for i in range(2):
+            rows = slice(BLK * i, BLK * (i + 1))
+            both = grams[i] + jnp.transpose(grams[i])
             turns.append(
                 jnp.concatenate(
                     [jnp.sum(both * cols[rows, a : a + 1], axis=0, keepdims=True) for a in (4, 5, 6)], axis=0
                 )
             )
-        dm2 = jnp.concatenate(halves, axis=0)
-        dm2_s[edges, :] = dm2
-        dmsg = ug + nn(dm2, wtt_s[...])
-        dpre_s[edges, :] = (dmsg * f_s[s].astype(F32)).astype(BF)
-        drad = (dmsg * sg_s[s].astype(F32)).astype(BF)
-        drad_s[edges, :] = drad
         t = (cols[:, 3:4] - centers) * inv_width
         slope = nt(drad, wr_ref[...]) * (jnp.exp(-(t * t)) * (t * (-2.0 * inv_width)))
         ddist = jnp.sum(jnp.transpose(slope), axis=0, keepdims=True) * geo[2:3]
@@ -302,8 +332,7 @@
         dv_s[:, edges] = jnp.concatenate([top, dv - top, jnp.zeros((10, ES), F32)], axis=0).astype(BF)
 
     wtt_s[...] = jnp.transpose(wt_ref[...])
-    for s in range(NG):
-        backward(s)
+    staged(fetch, mixed, spread, turn_back)
 
     own = pl.multiple_of(me * AT, AT)
     ohs_own = oht_s[pl.ds(own, AT), :]
@@ -351,6 +380,7 @@
 def batch(me, part, u, own, other, ws, wd, wr, wt, wo, we, ecot):
     vm = pl.BlockSpec(memory_space=pltpu.VMEM)
     sm = pl.BlockSpec(memory_space=pltpu.SMEM)
+    far = pl.BlockSpec(memory_space=pltpu.HBM)
     V = pltpu.VMEM
     return pl.pallas_call(
         main_kernel,
@@ -361,7 +391,7 @@
             jax.ShapeDtypeStruct((AT, 128), F32),
             jax.ShapeDtypeStruct((4, 4, CH, 128), BF),
         ),
-        in_specs=[sm] * 3 + [vm] * 2 + [pl.BlockSpec(memory_space=pltpu.HBM)] * 5 + [vm] * 2,
+        in_specs=[sm] * 3 + [vm] * 2 + [far] * 2 + [vm] + [far] * 2 + [vm] * 2,
         out_specs=(vm,) * 5,
         scratch_shapes=[
             V((ATOMS, D), BF),
@@ -393,10 +423,9 @@
             V((16, D), F32),
             V((D, D), BF),
             V((D, D), BF),
-            V((K, D), BF),
             V((D, D), BF),
             V((D, D), BF),
-            pltpu.SemaphoreType.DMA((5,)),
+            pltpu.SemaphoreType.DMA((4,)),
             V((D, D), BF),
         ],
         compiler_params=pltpu.CompilerParams(vmem_limit_bytes=53760 * 1024),
@@ -559,7 +588,7 @@
     u = jnp.where(core == 0, x, y)
     part = graph ^ (6 * zh)
     me, x, y, u, part = (a.astype(jnp.int32).reshape(1) for a in (graph, x, y, u, part))
-    piece = pack(
+    piece, ecot, wr = pack(
         me,
         node_feats[0],
         jnp.swapaxes(positions, 0, 1),
@@ -570,12 +599,15 @@
         trip_out,
         trip_count,
         graph_ids,
-    )[None]
+        energy_cot,
+        w_radial,
+    )
+    piece = piece[None]
     own = join(piece, *[shift(piece, zl=k) for k in (1, 2, 3)])
     other = shift(own, c=1)
     we = w_energy.reshape(1, D)
     energy, pos_grad, sums, cot, payload = batch(
-        me, part, u, own, other, w_src, w_dst, w_radial, w_trip, w_out, we, energy_cot
+        me, part, u, own, other, w_src, w_dst, wr, w_trip, w_out, we, ecot
     )
     node_grad = node(sums, cot, w_src, w_dst, we)
     one, three, two = [shift(payload[k], u=k) for k in ORDER]
@@ -585,6 +617,7 @@
     held = (held.astype(F32) + shift(held, zh=1, zl=3).astype(F32)).astype(BF)
     held = join(held, *[shift(held, zl=k) for k in (1, 2, 3)])
     one, three, two = [shift(held, u=k) for k in ORDER]
+    one, three, two, node_grad = lax.optimization_barrier((one, three, two, node_grad))
     held = join(held, one, two, three)
     other = shift(held, c=1)
     gs, gd, gr, gt, go, ge = place(1, x, y, part, other, *place(0, x, y, part, held))

time: 96.3 us -> 91.2 us (0.947)
  waiting for transfers between devices: 29.2 us -> 25.1 us
  Pallas kernels: 28.3 us -> 26.8 us
    ppermute x18, waiting for transfers between devices: 29.2 us -> 25.1 us  [shift(): return lax.ppermute(value, AXES, moves(fn))]
    pallas_call x1, Pallas kernels: 19.1 us -> 17.4 us  [batch(): pl.pallas_call(main_kernel, out_shape=(jax.ShapeDtypeStruct((1, 16), F32)...]
  transfers between devices with their start and end apart: 18 -> 18, of which waited for: 11 -> 12; matrix products, arithmetic and copies ran while one was open for 1% -> 1% of each run, Pallas kernels for 5% -> 5%
where the time goes in v5:
time: 91.2 us; the launch traced here: 90.9 us
  starting transfers between devices  33.2 us (36%)
  Pallas kernels  26.8 us (29%)
  waiting for transfers between devices  25.1 us (28%)
  local copies, waits for them, and re-layouts  2.45 us (3%)
  between operations  2.25 us (2%)
  other arithmetic  1.09 us (1%)
    ppermute x18, starting transfers between devices, shift(): return lax.ppermute(value, AXES, moves(fn))  33.2 us
    ppermute x18, waiting for transfers between devices, shift(): return lax.ppermute(value, AXES, moves(fn))  25.1 us
    pallas_call x1, Pallas kernels, batch(): pl.pallas_call(main_kernel, out_shape=(jax.ShapeDtypeStruct((1, 16), F32)...  17.4 us
    pallas_call x2, Pallas kernels, place(): pl.pallas_call(functools.partial(place_kernel, c), out_shape=(big, big, j...  5.28 us
    pallas_call x1, Pallas kernels, node(): pl.pallas_call(node_kernel, out_shape=jax.ShapeDtypeStruct((AT, D), F32),...  2.36 us
  transfers between devices with their start and end apart: 18, of which 12 were waited for; matrix products, arithmetic and copies ran while one was open for 1% of the time, Pallas kernels for 5%

profile of v5, /device:TPU:1, one launch (start us, length us, event | category | flops | bytes accessed | tf_op | source)
XLA Modules:
  0.0 90.9 jit_solution(9478965574851625494)
XLA Ops:
  1.9 1.8 %pack.1 = (bf16[80,512]{1,0:T(8,128)(2,1)}, f32[1,16]{1,0:T(1,128)}, bf16[128,512]{1,0:T(8,128)(2,1)}) custom-call(s32[1]{0:T(128)} %bitcast.me_ref, bf16[64,512]{1,0:T(8,128)(2,1)} %bitcast.25, f32[3,1,64]{2,1,0:T(1,128)} %bitcast.27, s32[1,256]{1,0:T(1,128)} %src_ref.1, s32[1,256]{1,0:T(1,128)} %dst_ref.1, s32[1,1]{1,0:T(1,128)S(6)} %copy.43.ec_ref, ...), custom_call_target="tpu_custom_call" | custom-call | tf_op jit(solution)/shard_map/pack/pallas_call | solution.py:78
  3.7 5.2 %collective-permute-start.2 = (bf16[1,80,512]{2,1,0:T(8,128)(2,1)}, bf16[1,80,512]{2,1,0:T(8,128)(2,1)S(1)}, u32[]{:S(2)}, u32[]{:S(2)}) collective-permute-start(bf16[1,80,512]{2,1,0:T(8,128)(2,1)} %bitcast.21), channel_id=1, source_target_pairs={{0,6},{1,7},{2,4},{3,5},{4,2},{5,3},{6,0},{7,1},{8,14},{9,15},{10,... | collective-permute-start | bytes 245768 | tf_op jit(solution)/shard_map/ppermute | solution.py:552
  8.9 0.0 collective-permute-start.1
  8.9 0.3 collective-permute-start
  9.2 1.9 %collective-permute-done.2 = bf16[1,80,512]{2,1,0:T(8,128)(2,1)S(1)} collective-permute-done((bf16[1,80,512]{2,1,0:T(8,128)(2,1)}, bf16[1,80,512]{2,1,0:T(8,128)(2,1)S(1)}, u32[]{:S(2)}, u32[]{:S(2)}) %collective-permute-start.2) | collective-permute-done | bytes 81952 | tf_op jit(solution)/shard_map/ppermute | solution.py:552
  11.0 4.9 %collective-permute-done.1 = bf16[1,80,512]{2,1,0:T(8,128)(2,1)S(1)} collective-permute-done((bf16[1,80,512]{2,1,0:T(8,128)(2,1)}, bf16[1,80,512]{2,1,0:T(8,128)(2,1)S(1)}, u32[]{:S(2)}, u32[]{:S(2)}) %collective-permute-start.1) | collective-permute-done | bytes 81952 | tf_op jit(solution)/shard_map/ppermute | solution.py:552
  15.9 0.0 collective-permute-done
  15.9 0.9 %pad_maximum_fusion.own_ref = bf16[4,80,512]{2,1,0:T(8,128)(2,1)S(1)} fusion(bf16[1,80,512]{2,1,0:T(8,128)(2,1)S(1)} %collective-permute-done.2, bf16[1,80,512]{2,1,0:T(8,128)(2,1)S(1)} %collective-permute-done.1, bf16[1,80,512]{2,1,0:T(8,128)(2,1)S(1)} %collective-permute-done, bf16[1,80,512]{2,1,0:T(8,128)(2,1)} %bitcast.24), kind=kLoop, calls=%fused_computation | loop fusion | flops 491520 | bytes 655360 | tf_op jit(solution)/shard_map/concatenate | solution.py:556
  16.8 1.0 %collective-permute-start.3 = (bf16[4,80,512]{2,1,0:T(8,128)(2,1)S(1)}, bf16[4,80,512]{2,1,0:T(8,128)(2,1)S(1)}, u32[]{:S(2)}, u32[]{:S(2)}) collective-permute-start(bf16[4,80,512]{2,1,0:T(8,128)(2,1)S(1)} %pad_maximum_fusion.own_ref), channel_id=1, source_target_pairs={{0,1},{1,0},{2,3},{3,2},{4,5},{5,4},{6,7},{7,6},{8,9},{9,8},{10,11... | collective-permute-start | bytes 983048 | tf_op jit(solution)/shard_map/ppermute | solution.py:552
  17.8 0.7 reshape.44.we_ref
  18.5 0.0 copy-start.3
  18.5 0.6 collective-permute-done.3.other_ref
  19.1 0.0 copy-start
  19.1 0.9 copy-done
  20.0 0.0 copy-start.4
  20.0 0.7 copy-done.4
  20.6 17.4 %batch.1 = (f32[1,16]{1,0:T(1,128)}, f32[3,1,64]{2,1,0:T(1,128)}, bf16[128,512]{1,0:T(8,128)(2,1)S(1)}, f32[64,128]{1,0:T(8,128)S(1)}, bf16[4,4,72,128]{3,2,1,0:T(8,128)(2,1)S(1)}) custom-call(s32[1]{0:T(128)} %bitcast.me_ref, s32[1]{0:T(128)} %bitcast.1.slice_ref, s32[1]{0:T(128)} %bitcast.2.u_ref, bf16[4,80,512]{2,1,0:T(8,128)(2,1)S(1)} %pad_maximum_fusion.own_ref, ...), custom_call_target="tpu_custom_call" | custom-call | tf_op jit(solution)/shard_map/batch/pallas_call | solution.py:385
  38.0 0.0 copy-done.3
  38.0 0.0 copy-start.1
  38.1 0.0 copy-start.2
  38.1 2.9 %collective-permute-start.4 = (bf16[4,72,128]{2,1,0:T(8,128)(2,1)S(1)}, bf16[4,72,128]{2,1,0:T(8,128)(2,1)S(1)}, u32[]{:S(2)}, u32[]{:S(2)}) collective-permute-start(bf16[4,72,128]{2,1,0:T(8,128)(2,1)S(1)} %get-tuple-element.59), channel_id=1, source_target_pairs={{0,64},{1,17},{2,66},{3,19},{4,68},{5,21},{6,70},{7,23},{8,72},{9,... | collective-permute-start | bytes 221192 | tf_op jit(solution)/shard_map/ppermute | solution.py:552
  41.0 0.8 collective-permute-start.6
  41.8 0.7 collective-permute-start.5
  42.5 0.4 collective-permute-done.4
  42.9 1.3 %collective-permute-done.6 = bf16[4,72,128]{2,1,0:T(8,128)(2,1)S(1)} collective-permute-done((bf16[4,72,128]{2,1,0:T(8,128)(2,1)S(1)}, bf16[4,72,128]{2,1,0:T(8,128)(2,1)S(1)}, u32[]{:S(2)}, u32[]{:S(2)}) %collective-permute-start.6) | collective-permute-done | bytes 73760 | tf_op jit(solution)/shard_map/ppermute | solution.py:552
  44.2 2.0 %collective-permute-done.5 = bf16[4,72,128]{2,1,0:T(8,128)(2,1)S(1)} collective-permute-done((bf16[4,72,128]{2,1,0:T(8,128)(2,1)S(1)}, bf16[4,72,128]{2,1,0:T(8,128)(2,1)S(1)}, u32[]{:S(2)}, u32[]{:S(2)}) %collective-permute-start.5) | collective-permute-done | bytes 73760 | tf_op jit(solution)/shard_map/ppermute | solution.py:552
  46.2 2.5 %collective-permute-start.9 = (bf16[4,72,128]{2,1,0:T(8,128)(2,1)S(1)}, bf16[4,72,128]{2,1,0:T(8,128)(2,1)S(1)}, u32[]{:S(2)}, u32[]{:S(2)}) collective-permute-start(bf16[4,72,128]{2,1,0:T(8,128)(2,1)S(1)} %fusion.1), channel_id=1, source_target_pairs={{0,24},{1,97},{2,26},{3,99},{4,28},{5,101},{6,30},{7,103},{8,0},{9... | collective-permute-start | bytes 221192 | tf_op jit(solution)/shard_map/ppermute | solution.py:552
  48.8 0.0 collective-permute-start.8
  48.8 1.7 %collective-permute-start.7 = (bf16[4,72,128]{2,1,0:T(8,128)(2,1)S(1)}, bf16[4,72,128]{2,1,0:T(8,128)(2,1)S(1)}, u32[]{:S(2)}, u32[]{:S(2)}) collective-permute-start(bf16[4,72,128]{2,1,0:T(8,128)(2,1)S(1)} %fusion.1), channel_id=1, source_target_pairs={{0,16},{1,65},{2,18},{3,67},{4,20},{5,69},{6,22},{7,71},{8,24},{9,... | collective-permute-start | bytes 221192 | tf_op jit(solution)/shard_map/ppermute | solution.py:552
  50.5 0.0 collective-permute-done.9
  50.5 3.5 %collective-permute-done.8 = bf16[4,72,128]{2,1,0:T(8,128)(2,1)S(1)} collective-permute-done((bf16[4,72,128]{2,1,0:T(8,128)(2,1)S(1)}, bf16[4,72,128]{2,1,0:T(8,128)(2,1)S(1)}, u32[]{:S(2)}, u32[]{:S(2)}) %collective-permute-start.8) | collective-permute-done | bytes 73760 | tf_op jit(solution)/shard_map/ppermute | solution.py:552
  54.0 0.0 collective-permute-done.7
  54.0 4.8 %collective-permute-start.10 = (bf16[4,72,128]{2,1,0:T(8,128)(2,1)S(1)}, bf16[4,72,128]{2,1,0:T(8,128)(2,1)S(1)}, u32[]{:S(2)}, u32[]{:S(2)}) collective-permute-start(bf16[4,72,128]{2,1,0:T(8,128)(2,1)S(1)} %add_convert_fusion.1), channel_id=1, source_target_pairs={{0,134},{1,135},{2,132},{3,133},{4,130},{5,131},{6,128},{7,129},{8... | collective-permute-start | bytes 221192 | tf_op jit(solution)/shard_map/ppermute | solution.py:552
  58.8 0.0 copy-done.1
  58.8 2.2 %collective-permute-done.10 = bf16[4,72,128]{2,1,0:T(8,128)(2,1)S(1)} collective-permute-done((bf16[4,72,128]{2,1,0:T(8,128)(2,1)S(1)}, bf16[4,72,128]{2,1,0:T(8,128)(2,1)S(1)}, u32[]{:S(2)}, u32[]{:S(2)}) %collective-permute-start.10) | collective-permute-done | bytes 73760 | tf_op jit(solution)/shard_map/ppermute | solution.py:552
  61.0 0.0 copy-done.2
  61.0 1.3 %collective-permute-start.13 = (bf16[4,72,128]{2,1,0:T(8,128)(2,1)S(1)}, bf16[4,72,128]{2,1,0:T(8,128)(2,1)S(1)}, u32[]{:S(2)}, u32[]{:S(2)}) collective-permute-start(bf16[4,72,128]{2,1,0:T(8,128)(2,1)S(1)} %get-tuple-element.58), channel_id=1, source_target_pairs={{0,6},{1,7},{2,4},{3,5},{4,2},{5,3},{6,0},{7,1},{8,14},{9,15},{10,... | collective-permute-start | bytes 221192 | tf_op jit(solution)/shard_map/ppermute | solution.py:552
  62.3 0.4 collective-permute-start.12
  62.7 1.9 %collective-permute-start.11 = (bf16[4,72,128]{2,1,0:T(8,128)(2,1)S(1)}, bf16[4,72,128]{2,1,0:T(8,128)(2,1)S(1)}, u32[]{:S(2)}, u32[]{:S(2)}) collective-permute-start(bf16[4,72,128]{2,1,0:T(8,128)(2,1)S(1)} %get-tuple-element.58), channel_id=1, source_target_pairs={{0,2},{1,3},{2,0},{3,1},{4,6},{5,7},{6,4},{7,5},{8,10},{9,11},{10,... | collective-permute-start | bytes 221192 | tf_op jit(solution)/shard_map/ppermute | solution.py:552
  64.6 2.4 %node.1 = f32[64,512]{1,0:T(8,128)} custom-call(bf16[128,512]{1,0:T(8,128)(2,1)} %copy-done.1, f32[64,128]{1,0:T(8,128)} %copy-done.2, bf16[512,512]{1,0:T(8,128)(2,1)} %ws_ref.1, bf16[512,512]{1,0:T(8,128)(2,1)} %wd_ref.1, bf16[1,512]{1,0:T(2,128)(2,1)} %copy-done.3), custom_call_target="tpu_custom_call" | custom-call | tf_op jit(solution)/shard_map/node/pallas_call | solution.py:446
  67.0 0.0 collective-permute-done.13
  67.0 0.7 collective-permute-done.12
  67.7 0.0 collective-permute-done.11
  67.7 1.0 %collective-permute-start.16 = (bf16[16,72,128]{2,1,0:T(8,128)(2,1)S(1)}, bf16[16,72,128]{2,1,0:T(8,128)(2,1)S(1)}, u32[]{:S(2)}, u32[]{:S(2)}) collective-permute-start(bf16[16,72,128]{2,1,0:T(8,128)(2,1)S(1)} %pad_maximum_fusion.1), channel_id=1, source_target_pairs={{0,64},{1,17},{2,66},{3,19},{4,68},{5,21},{6,70},{7,23},{8,72},{9,... | collective-permute-start | bytes 884744 | tf_op jit(solution)/shard_map/ppermute | solution.py:552
  68.7 1.2 %collective-permute-start.15 = (bf16[16,72,128]{2,1,0:T(8,128)(2,1)S(1)}, bf16[16,72,128]{2,1,0:T(8,128)(2,1)S(1)}, u32[]{:S(2)}, u32[]{:S(2)}) collective-permute-start(bf16[16,72,128]{2,1,0:T(8,128)(2,1)S(1)} %pad_maximum_fusion.1), channel_id=1, source_target_pairs={{0,96},{1,25},{2,98},{3,27},{4,100},{5,29},{6,102},{7,31},{8,104},... | collective-permute-start | bytes 884744 | tf_op jit(solution)/shard_map/ppermute | solution.py:552
  70.0 0.2 collective-permute-start.14
  70.2 4.7 %collective-permute-done.16 = bf16[16,72,128]{2,1,0:T(8,128)(2,1)S(1)} collective-permute-done((bf16[16,72,128]{2,1,0:T(8,128)(2,1)S(1)}, bf16[16,72,128]{2,1,0:T(8,128)(2,1)S(1)}, u32[]{:S(2)}, u32[]{:S(2)}) %collective-permute-start.16) | collective-permute-done | bytes 294944 | tf_op jit(solution)/shard_map/ppermute | solution.py:552
  75.0 1.9 %collective-permute-done.15 = bf16[16,72,128]{2,1,0:T(8,128)(2,1)S(1)} collective-permute-done((bf16[16,72,128]{2,1,0:T(8,128)(2,1)S(1)}, bf16[16,72,128]{2,1,0:T(8,128)(2,1)S(1)}, u32[]{:S(2)}, u32[]{:S(2)}) %collective-permute-start.15) | collective-permute-done | bytes 294944 | tf_op jit(solution)/shard_map/ppermute | solution.py:552
  76.9 1.2 %collective-permute-done.14 = bf16[16,72,128]{2,1,0:T(8,128)(2,1)S(1)} collective-permute-done((bf16[16,72,128]{2,1,0:T(8,128)(2,1)S(1)}, bf16[16,72,128]{2,1,0:T(8,128)(2,1)S(1)}, u32[]{:S(2)}, u32[]{:S(2)}) %collective-permute-start.14) | collective-permute-done | bytes 294944 | tf_op jit(solution)/shard_map/ppermute | solution.py:552
  78.2 7.2 %collective-permute-start.17 = (bf16[64,72,128]{2,1,0:T(8,128)(2,1)S(1)}, bf16[64,72,128]{2,1,0:T(8,128)(2,1)S(1)}, u32[]{:S(2)}, u32[]{:S(2)}) collective-permute-start(bf16[64,72,128]{2,1,0:T(8,128)(2,1)S(1)} %constant_dynamic-update-slice_fusion.ref), channel_id=1, source_target_pairs={{0,1},{1,0},{2,3},{3,2},{4,5},{5,4},{6,7},{7,6},{8,9},{9,8},{10,11... | collective-permute-start | bytes 3538952 | tf_op jit(solution)/shard_map/ppermute | solution.py:552
  85.4 2.6 %place.2 = (f32[512,512]{1,0:T(8,128)}, f32[512,512]{1,0:T(8,128)}, f32[128,512]{1,0:T(8,128)}, f32[512,512]{1,0:T(8,128)}, f32[512,512]{1,0:T(8,128)}, /*index=5*/f32[1,512]{1,0:T(1,128)}) custom-call(s32[1]{0:T(128)} %bitcast.12.x_ref, s32[1]{0:T(128)} %bitcast.13.y_ref, s32[1]{0:T(128)} %bitcast.1.slice_ref, ...), custom_call_target="tpu_custom_call" | custom-call | tf_op jit(solution)/shard_map/place/pallas_call | solution.py:513
  88.1 0.0 collective-permute-done.17.ref
  88.1 2.6 %place.3 = (f32[512,512]{1,0:T(8,128)}, f32[512,512]{1,0:T(8,128)}, f32[128,512]{1,0:T(8,128)}, f32[512,512]{1,0:T(8,128)}, f32[512,512]{1,0:T(8,128)}, /*index=5*/f32[1,512]{1,0:T(1,128)}) custom-call(s32[1]{0:T(128)} %bitcast.12.x_ref, s32[1]{0:T(128)} %bitcast.13.y_ref, ...), custom_call_target="tpu_custom_call", output_to_operand_aliasing={{0}: (4, {}), {1}: (5, {}), {2}: (6, {}), {3}: (7, {}), {4}... | custom-call | tf_op jit(solution)/shard_map/place/pallas_call | solution.py:513
  (11 shorter events, 0.3 us)
Async XLA Ops:
  3.7 7.3 %collective-permute-start.2 = (bf16[1,80,512]{2,1,0:T(8,128)(2,1)}, bf16[1,80,512]{2,1,0:T(8,128)(2,1)S(1)}, u32[]{:S(2)}, u32[]{:S(2)}) collective-permute-start(bf16[1,80,512]{2,1,0:T(8,128)(2,1)} %bitcast.21), channel_id=1, source_target_pairs={{0,6},{1,7},{2,4},{3,5},{4,2},{5,3},{6,0},{7,1},{8,14},{9,15},{10,... | collective-permute-start | bytes 245768 | tf_op jit(solution)/shard_map/ppermute | solution.py:552
  8.9 7.0 %collective-permute-start.1 = (bf16[1,80,512]{2,1,0:T(8,128)(2,1)}, bf16[1,80,512]{2,1,0:T(8,128)(2,1)S(1)}, u32[]{:S(2)}, u32[]{:S(2)}) collective-permute-start(bf16[1,80,512]{2,1,0:T(8,128)(2,1)} %bitcast.22), channel_id=1, source_target_pairs={{0,4},{1,5},{2,6},{3,7},{4,0},{5,1},{6,2},{7,3},{8,12},{9,13},{10,... | collective-permute-start | bytes 245768 | tf_op jit(solution)/shard_map/ppermute | solution.py:552
  8.9 7.0 %collective-permute-start = (bf16[1,80,512]{2,1,0:T(8,128)(2,1)}, bf16[1,80,512]{2,1,0:T(8,128)(2,1)S(1)}, u32[]{:S(2)}, u32[]{:S(2)}) collective-permute-start(bf16[1,80,512]{2,1,0:T(8,128)(2,1)} %bitcast.23), channel_id=1, source_target_pairs={{0,2},{1,3},{2,0},{3,1},{4,6},{5,7},{6,4},{7,5},{8,10},{9,11},{10,... | collective-permute-start | bytes 245768 | tf_op jit(solution)/shard_map/ppermute | solution.py:552
  16.8 2.2 %collective-permute-start.3 = (bf16[4,80,512]{2,1,0:T(8,128)(2,1)S(1)}, bf16[4,80,512]{2,1,0:T(8,128)(2,1)S(1)}, u32[]{:S(2)}, u32[]{:S(2)}) collective-permute-start(bf16[4,80,512]{2,1,0:T(8,128)(2,1)S(1)} %pad_maximum_fusion.own_ref), channel_id=1, source_target_pairs={{0,1},{1,0},{2,3},{3,2},{4,5},{5,4},{6,7},{7,6},{8,9},{9,8},{10,11... | collective-permute-start | bytes 983048 | tf_op jit(solution)/shard_map/ppermute | solution.py:552
  18.5 19.6 %copy-start.3 = (bf16[1,512]{1,0:T(2,128)(2,1)}, bf16[1,512]{1,0:T(2,128)(2,1)S(1)}, u32[]{:S(2)}) copy-start(bf16[1,512]{1,0:T(2,128)(2,1)S(1)} %reshape.44.we_ref) | copy-start | bytes 3076
  19.1 0.9 copy-start
  20.0 0.7 copy-start.4
  38.0 20.8 %copy-start.1 = (bf16[128,512]{1,0:T(8,128)(2,1)}, bf16[128,512]{1,0:T(8,128)(2,1)S(1)}, u32[]{:S(2)}) copy-start(bf16[128,512]{1,0:T(8,128)(2,1)S(1)} %get-tuple-element.39.sums_ref) | copy-start | bytes 393220
  38.1 22.9 %copy-start.2 = (f32[64,128]{1,0:T(8,128)}, f32[64,128]{1,0:T(8,128)S(1)}, u32[]{:S(2)}) copy-start(f32[64,128]{1,0:T(8,128)S(1)} %get-tuple-element.40.cot_ref) | copy-start | bytes 98308
  38.1 4.8 %collective-permute-start.4 = (bf16[4,72,128]{2,1,0:T(8,128)(2,1)S(1)}, bf16[4,72,128]{2,1,0:T(8,128)(2,1)S(1)}, u32[]{:S(2)}, u32[]{:S(2)}) collective-permute-start(bf16[4,72,128]{2,1,0:T(8,128)(2,1)S(1)} %get-tuple-element.59), channel_id=1, source_target_pairs={{0,64},{1,17},{2,66},{3,19},{4,68},{5,21},{6,70},{7,23},{8,72},{9,... | collective-permute-start | bytes 221192 | tf_op jit(solution)/shard_map/ppermute | solution.py:552
  41.0 3.2 %collective-permute-start.6 = (bf16[4,72,128]{2,1,0:T(8,128)(2,1)S(1)}, bf16[4,72,128]{2,1,0:T(8,128)(2,1)S(1)}, u32[]{:S(2)}, u32[]{:S(2)}) collective-permute-start(bf16[4,72,128]{2,1,0:T(8,128)(2,1)S(1)} %get-tuple-element.60), channel_id=1, source_target_pairs={{0,96},{1,25},{2,98},{3,27},{4,100},{5,29},{6,102},{7,31},{8,104},... | collective-permute-start | bytes 221192 | tf_op jit(solution)/shard_map/ppermute | solution.py:552
  41.8 4.4 %collective-permute-start.5 = (bf16[4,72,128]{2,1,0:T(8,128)(2,1)S(1)}, bf16[4,72,128]{2,1,0:T(8,128)(2,1)S(1)}, u32[]{:S(2)}, u32[]{:S(2)}) collective-permute-start(bf16[4,72,128]{2,1,0:T(8,128)(2,1)S(1)} %get-tuple-element.61), channel_id=1, source_target_pairs={{0,32},{1,9},{2,34},{3,11},{4,36},{5,13},{6,38},{7,15},{8,40},{9,1... | collective-permute-start | bytes 221192 | tf_op jit(solution)/shard_map/ppermute | solution.py:552
  46.2 4.3 %collective-permute-start.9 = (bf16[4,72,128]{2,1,0:T(8,128)(2,1)S(1)}, bf16[4,72,128]{2,1,0:T(8,128)(2,1)S(1)}, u32[]{:S(2)}, u32[]{:S(2)}) collective-permute-start(bf16[4,72,128]{2,1,0:T(8,128)(2,1)S(1)} %fusion.1), channel_id=1, source_target_pairs={{0,24},{1,97},{2,26},{3,99},{4,28},{5,101},{6,30},{7,103},{8,0},{9... | collective-permute-start | bytes 221192 | tf_op jit(solution)/shard_map/ppermute | solution.py:552
  48.8 5.2 %collective-permute-start.8 = (bf16[4,72,128]{2,1,0:T(8,128)(2,1)S(1)}, bf16[4,72,128]{2,1,0:T(8,128)(2,1)S(1)}, u32[]{:S(2)}, u32[]{:S(2)}) collective-permute-start(bf16[4,72,128]{2,1,0:T(8,128)(2,1)S(1)} %fusion.1), channel_id=1, source_target_pairs={{0,8},{1,33},{2,10},{3,35},{4,12},{5,37},{6,14},{7,39},{8,16},{9,4... | collective-permute-start | bytes 221192 | tf_op jit(solution)/shard_map/ppermute | solution.py:552
  48.8 5.2 %collective-permute-start.7 = (bf16[4,72,128]{2,1,0:T(8,128)(2,1)S(1)}, bf16[4,72,128]{2,1,0:T(8,128)(2,1)S(1)}, u32[]{:S(2)}, u32[]{:S(2)}) collective-permute-start(bf16[4,72,128]{2,1,0:T(8,128)(2,1)S(1)} %fusion.1), channel_id=1, source_target_pairs={{0,16},{1,65},{2,18},{3,67},{4,20},{5,69},{6,22},{7,71},{8,24},{9,... | collective-permute-start | bytes 221192 | tf_op jit(solution)/shard_map/ppermute | solution.py:552
  54.0 6.9 %collective-permute-start.10 = (bf16[4,72,128]{2,1,0:T(8,128)(2,1)S(1)}, bf16[4,72,128]{2,1,0:T(8,128)(2,1)S(1)}, u32[]{:S(2)}, u32[]{:S(2)}) collective-permute-start(bf16[4,72,128]{2,1,0:T(8,128)(2,1)S(1)} %add_convert_fusion.1), channel_id=1, source_target_pairs={{0,134},{1,135},{2,132},{3,133},{4,130},{5,131},{6,128},{7,129},{8... | collective-permute-start | bytes 221192 | tf_op jit(solution)/shard_map/ppermute | solution.py:552
  61.0 6.0 %collective-permute-start.13 = (bf16[4,72,128]{2,1,0:T(8,128)(2,1)S(1)}, bf16[4,72,128]{2,1,0:T(8,128)(2,1)S(1)}, u32[]{:S(2)}, u32[]{:S(2)}) collective-permute-start(bf16[4,72,128]{2,1,0:T(8,128)(2,1)S(1)} %get-tuple-element.58), channel_id=1, source_target_pairs={{0,6},{1,7},{2,4},{3,5},{4,2},{5,3},{6,0},{7,1},{8,14},{9,15},{10,... | collective-permute-start | bytes 221192 | tf_op jit(solution)/shard_map/ppermute | solution.py:552
  62.3 5.4 %collective-permute-start.12 = (bf16[4,72,128]{2,1,0:T(8,128)(2,1)S(1)}, bf16[4,72,128]{2,1,0:T(8,128)(2,1)S(1)}, u32[]{:S(2)}, u32[]{:S(2)}) collective-permute-start(bf16[4,72,128]{2,1,0:T(8,128)(2,1)S(1)} %get-tuple-element.58), channel_id=1, source_target_pairs={{0,4},{1,5},{2,6},{3,7},{4,0},{5,1},{6,2},{7,3},{8,12},{9,13},{10,... | collective-permute-start | bytes 221192 | tf_op jit(solution)/shard_map/ppermute | solution.py:552
  62.7 5.0 %collective-permute-start.11 = (bf16[4,72,128]{2,1,0:T(8,128)(2,1)S(1)}, bf16[4,72,128]{2,1,0:T(8,128)(2,1)S(1)}, u32[]{:S(2)}, u32[]{:S(2)}) collective-permute-start(bf16[4,72,128]{2,1,0:T(8,128)(2,1)S(1)} %get-tuple-element.58), channel_id=1, source_target_pairs={{0,2},{1,3},{2,0},{3,1},{4,6},{5,7},{6,4},{7,5},{8,10},{9,11},{10,... | collective-permute-start | bytes 221192 | tf_op jit(solution)/shard_map/ppermute | solution.py:552
  67.7 7.3 %collective-permute-start.16 = (bf16[16,72,128]{2,1,0:T(8,128)(2,1)S(1)}, bf16[16,72,128]{2,1,0:T(8,128)(2,1)S(1)}, u32[]{:S(2)}, u32[]{:S(2)}) collective-permute-start(bf16[16,72,128]{2,1,0:T(8,128)(2,1)S(1)} %pad_maximum_fusion.1), channel_id=1, source_target_pairs={{0,64},{1,17},{2,66},{3,19},{4,68},{5,21},{6,70},{7,23},{8,72},{9,... | collective-permute-start | bytes 884744 | tf_op jit(solution)/shard_map/ppermute | solution.py:552
  68.7 8.1 %collective-permute-start.15 = (bf16[16,72,128]{2,1,0:T(8,128)(2,1)S(1)}, bf16[16,72,128]{2,1,0:T(8,128)(2,1)S(1)}, u32[]{:S(2)}, u32[]{:S(2)}) collective-permute-start(bf16[16,72,128]{2,1,0:T(8,128)(2,1)S(1)} %pad_maximum_fusion.1), channel_id=1, source_target_pairs={{0,96},{1,25},{2,98},{3,27},{4,100},{5,29},{6,102},{7,31},{8,104},... | collective-permute-start | bytes 884744 | tf_op jit(solution)/shard_map/ppermute | solution.py:552
  70.0 8.1 %collective-permute-start.14 = (bf16[16,72,128]{2,1,0:T(8,128)(2,1)S(1)}, bf16[16,72,128]{2,1,0:T(8,128)(2,1)S(1)}, u32[]{:S(2)}, u32[]{:S(2)}) collective-permute-start(bf16[16,72,128]{2,1,0:T(8,128)(2,1)S(1)} %pad_maximum_fusion.1), channel_id=1, source_target_pairs={{0,32},{1,9},{2,34},{3,11},{4,36},{5,13},{6,38},{7,15},{8,40},{9,1... | collective-permute-start | bytes 884744 | tf_op jit(solution)/shard_map/ppermute | solution.py:552
  78.2 9.9 %collective-permute-start.17 = (bf16[64,72,128]{2,1,0:T(8,128)(2,1)S(1)}, bf16[64,72,128]{2,1,0:T(8,128)(2,1)S(1)}, u32[]{:S(2)}, u32[]{:S(2)}) collective-permute-start(bf16[64,72,128]{2,1,0:T(8,128)(2,1)S(1)} %constant_dynamic-update-slice_fusion.ref), channel_id=1, source_target_pairs={{0,1},{1,0},{2,3},{3,2},{4,5},{5,4},{6,7},{7,6},{8,9},{9,8},{10,11... | collective-permute-start | bytes 3538952 | tf_op jit(solution)/shard_map/ppermute | solution.py:552

commit v6 on v5

--- a/solution.py
+++ b/solution.py
@@ -36,9 +36,7 @@
     return lax.dot_general(a, b, (((0,), (0,)), ((), ())), preferred_element_type=F32)
 
 
-def pack_kernel(me_ref, h_ref, pos_ref, src_ref, dst_ref, ec_ref, tin_ref, tout_ref, tc_ref, gid_ref, ecot_ref, wr_ref, out_ref, cot_ref, wr_out, meta):
-    cot_ref[...] = ecot_ref[...]
-    wr_out[...] = wr_ref[...]
+def pack_kernel(me_ref, h_ref, pos_ref, src_ref, dst_ref, ec_ref, tin_ref, tout_ref, tc_ref, gid_ref, ecot_ref, out_ref, meta):
     odd = lax.rem(me_ref[0], 2)
     out_ref[0:AT, :] = h_ref[...]
 
@@ -63,6 +61,12 @@
     meta[6:9, 0:128] = place(p1)
     meta[9:12, 0:128] = place(p2)
     meta[12:15, 0:128] = place(p3)
+    e = jnp.concatenate([ecot_ref[...], jnp.zeros((1, 112), F32)], axis=1)
+    e1 = e.astype(BF).astype(F32)
+    e2 = (e - e1).astype(BF).astype(F32)
+    meta[6:7, 128:256] = e1
+    meta[7:8, 128:256] = e2
+    meta[8:9, 128:256] = (e - e1) - e2
     meta[15:16, 0:128] = place(gid_ref[...].astype(F32))
     tc = tc_ref[0, 0]
     tc_half = lax.shift_right_logical(tc, 3)
@@ -72,17 +76,17 @@
     out_ref[AT:PIECE, :] = meta[...].astype(BF)
 
 
-def pack(me, h, pos, src, dst, ec, tin, tout, tc, gid, ecot, wr):
+def pack(me, h, pos, src, dst, ec, tin, tout, tc, gid, ecot):
     vm = pl.BlockSpec(memory_space=pltpu.VMEM)
     sm = pl.BlockSpec(memory_space=pltpu.SMEM)
     return pl.pallas_call(
         pack_kernel,
-        out_shape=(jax.ShapeDtypeStruct((PIECE, D), BF), jax.ShapeDtypeStruct((1, 16), F32), jax.ShapeDtypeStruct((K, D), BF)),
-        in_specs=[sm, vm, vm, vm, vm, sm, vm, vm, sm, vm, vm, vm],
-        out_specs=(vm,) * 3,
+        out_shape=jax.ShapeDtypeStruct((PIECE, D), BF),
+        in_specs=[sm, vm, vm, vm, vm, sm, vm, vm, sm, vm, vm],
+        out_specs=vm,
         scratch_shapes=[pltpu.VMEM((16, D), F32)],
         name="pack",
-    )(me, h, pos, src, dst, ec, tin, tout, tc, gid, ecot, wr)
+    )(me, h, pos, src, dst, ec, tin, tout, tc, gid, ecot)
 
 
 def main_kernel(
@@ -93,11 +97,9 @@
     other_ref,
     ws_hbm,
     wd_hbm,
-    wr_ref,
+    wide_ref,
     wt_hbm,
     wo_hbm,
-    we_ref,
-    ecot_ref,
     energy_ref,
     pos_out_ref,
     own_s_ref,
@@ -145,6 +147,7 @@
     ]
     for load in loads:
         load.start()
+    wr_ref, we_ref = wide_ref.at[0:K], wide_ref.at[K : K + 16]
     me, my_slice, my_u = me_ref[0], slice_ref[0], u_ref[0]
     for near, ref in ((0, own_ref), (1, other_ref)):
         for kz in range(4):
@@ -244,12 +247,12 @@
             upd = msg[rows].astype(F32) + nn(mixes[i], m2[rows])
             upd_s[s * ES + BLK * i : s * ES + BLK * (i + 1), :] = upd.astype(BF)
 
-    def staged(*stages):
+    def staged(count, *stages):
         waiting = [None] * len(stages)
-        for turn in range(NG + len(stages) - 1):
+        for turn in range(count + len(stages) - 1):
             for k in reversed(range(len(stages))):
                 if k == 0:
-                    given = (turn,) if turn < NG else None
+                    given = (turn,) if turn < count else None
                 else:
                     given = waiting[k - 1]
                 waiting[k] = None if given is None else stages[k](*given)
@@ -263,26 +266,37 @@
     ab_s[ATOMS : 2 * ATOMS, :] = (0.5 * nn(h, wd_ref[...])).astype(BF)
     for load in loads[2:]:
         load.wait()
-    staged(gather, message, update)
-
-    agg = nn(oht_s[ATOMS : 2 * ATOMS, :], upd_s[...]).astype(BF)
-    aggb_s[...] = agg
-    z = nn(agg, wo_ref[...])
-    sig = 0.5 + 0.5 * jnp.tanh(0.5 * z)
-    out = z * sig
-    we = we_ref[...].astype(F32)
-    x = h_s[...].astype(F32) + out
-    atom_energy = jnp.sum(x * we, axis=1, keepdims=True)
-    member = jnp.where(
-        lax.broadcasted_iota(jnp.int32, (ATOMS, 16), 1).astype(F32) == gid_col, 1.0, 0.0
-    )
-    energy_ref[...] = jnp.sum(member * atom_energy, axis=0, keepdims=True)
-    cot = jnp.sum(member * ecot_ref[...], axis=1, keepdims=True)
-    cot_s[...] = jnp.broadcast_to(cot, (ATOMS, 128))
-    ge_s[...] = jnp.sum(x * cot, axis=0, keepdims=True)
-    dz = (cot * we * (sig + out * (1.0 - sig))).astype(BF)
-    dzb_s[...] = dz
-    ac_s[...] = nt(dz, wo_ref[...]).astype(BF)
+    staged(NG, gather, message, update)
+
+    we = we_ref[...].astype(F32)[0:1]
+    ecot = (meta_s[0, 6:7, 128:144] + meta_s[0, 7:8, 128:144]) + meta_s[0, 8:9, 128:144]
+    energies, slopes = [], []
+
+    def collect(b):
+        agg = nn(oht_s[ATOMS + 512 * b : ATOMS + 512 * (b + 1), :], upd_s[...]).astype(BF)
+        aggb_s[512 * b : 512 * (b + 1), :] = agg
+        return b, nn(agg, wo_ref[...])
+
+    def settle(b, z):
+        rows = slice(512 * b, 512 * (b + 1))
+        sig = 0.5 + 0.5 * jnp.tanh(0.5 * z)
+        out = z * sig
+        x = h_s[rows, :].astype(F32) + out
+        atom_energy = jnp.sum(x * we, axis=1, keepdims=True)
+        places = lax.broadcasted_iota(jnp.int32, (512, 16), 1).astype(F32)
+        member = jnp.where(places == gid_col[rows], 1.0, 0.0)
+        energies.append(jnp.sum(member * atom_energy, axis=0, keepdims=True))
+        cot = jnp.sum(member * ecot, axis=1, keepdims=True)
+        cot_s[rows, :] = jnp.broadcast_to(cot, (512, 128))
+        slopes.append(jnp.sum(x * cot, axis=0, keepdims=True))
+        dz = (cot * we * (sig + out * (1.0 - sig))).astype(BF)
+        dzb_s[rows, :] = dz
+        ac_s[rows, :] = nt(dz, wo_ref[...]).astype(BF)
+        return (b,)
+
+    staged(1, collect, settle)
+    energy_ref[...] = sum(energies[1:], energies[0])
+    ge_s[...] = sum(slopes[1:], slopes[0])
 
     def fetch(s):
         return s, nn(ohd_s[s], ac_s[...])
@@ -332,7 +346,7 @@
         dv_s[:, edges] = jnp.concatenate([top, dv - top, jnp.zeros((10, ES), F32)], axis=0).astype(BF)
 
     wtt_s[...] = jnp.transpose(wt_ref[...])
-    staged(fetch, mixed, spread, turn_back)
+    staged(NG, fetch, mixed, spread, turn_back)
 
     own = pl.multiple_of(me * AT, AT)
     ohs_own = oht_s[pl.ds(own, AT), :]
@@ -377,7 +391,7 @@
             pay_ref[lax.rem(u - my_u + 4, 4), v] = chunk.astype(BF)
 
 
-def batch(me, part, u, own, other, ws, wd, wr, wt, wo, we, ecot):
+def batch(me, part, u, own, other, ws, wd, wide, wt, wo):
     vm = pl.BlockSpec(memory_space=pltpu.VMEM)
     sm = pl.BlockSpec(memory_space=pltpu.SMEM)
     far = pl.BlockSpec(memory_space=pltpu.HBM)
@@ -391,7 +405,7 @@
             jax.ShapeDtypeStruct((AT, 128), F32),
             jax.ShapeDtypeStruct((4, 4, CH, 128), BF),
         ),
-        in_specs=[sm] * 3 + [vm] * 2 + [far] * 2 + [vm] + [far] * 2 + [vm] * 2,
+        in_specs=[sm] * 3 + [vm] * 2 + [far] * 2 + [vm] + [far] * 2,
         out_specs=(vm,) * 5,
         scratch_shapes=[
             V((ATOMS, D), BF),
@@ -430,12 +444,12 @@
         ],
         compiler_params=pltpu.CompilerParams(vmem_limit_bytes=53760 * 1024),
         name="batch",
-    )(me, part, u, own, other, ws, wd, wr, wt, wo, we, ecot)
-
-
-def node_kernel(sums_ref, cot_ref, ws_ref, wd_ref, we_ref, out_ref):
+    )(me, part, u, own, other, ws, wd, wide, wt, wo)
+
+
+def node_kernel(sums_ref, cot_ref, ws_ref, wd_ref, wide_ref, out_ref):
     out_ref[...] = (
-        cot_ref[:, 0:1] * we_ref[...].astype(F32)
+        cot_ref[:, 0:1] * wide_ref[K : K + 16, :].astype(F32)[0:1]
         + nt(sums_ref[0:AT, :], ws_ref[...])
         + nt(sums_ref[AT : 2 * AT, :], wd_ref[...])
     )
@@ -448,6 +462,7 @@
         out_shape=jax.ShapeDtypeStruct((AT, D), F32),
         in_specs=[vm] * 5,
         out_specs=vm,
+        compiler_params=pltpu.CompilerParams(vmem_limit_bytes=24 * 1024 * 1024),
         name="node",
     )(sums, cot, ws, wd, we)
 
@@ -588,7 +603,7 @@
     u = jnp.where(core == 0, x, y)
     part = graph ^ (6 * zh)
     me, x, y, u, part = (a.astype(jnp.int32).reshape(1) for a in (graph, x, y, u, part))
-    piece, ecot, wr = pack(
+    piece = pack(
         me,
         node_feats[0],
         jnp.swapaxes(positions, 0, 1),
@@ -600,16 +615,14 @@
         trip_count,
         graph_ids,
         energy_cot,
-        w_radial,
-    )
-    piece = piece[None]
+    )[None]
     own = join(piece, *[shift(piece, zl=k) for k in (1, 2, 3)])
     other = shift(own, c=1)
-    we = w_energy.reshape(1, D)
+    wide = jnp.concatenate([w_radial, w_energy.reshape(1, D), jnp.zeros((15, D), BF)], axis=0)
     energy, pos_grad, sums, cot, payload = batch(
-        me, part, u, own, other, w_src, w_dst, wr, w_trip, w_out, we, ecot
+        me, part, u, own, other, w_src, w_dst, wide, w_trip, w_out
     )
-    node_grad = node(sums, cot, w_src, w_dst, we)
+    node_grad = node(sums, cot, w_src, w_dst, wide)
     one, three, two = [shift(payload[k], u=k) for k in ORDER]
     held = total(payload[0], two, one, three)
     one, three, two = [shift(held, v=k) for k in ORDER]

time: 91.2 us -> 89.7 us (0.984)
  local copies, waits for them, and re-layouts: 2.45 us -> 0.97 us
  Pallas kernels: 26.8 us -> 25.5 us
  waiting for transfers between devices: 25.1 us -> 26.3 us
  other arithmetic: 1.09 us -> 2.07 us
    unnamed x15 -> x9, local copies, waits for them, and re-layouts: 1.7 us -> 0.14 us
    pallas_call x1, Pallas kernels: 2.36 us -> 1.09 us  [node(): pl.pallas_call(node_kernel, out_shape=jax.ShapeDtypeStruct((AT, D), F32),...]
    ppermute x18, waiting for transfers between devices: 25.1 us -> 26.3 us  [shift(): return lax.ppermute(value, AXES, moves(fn))]
    concatenate x0 -> x1, other arithmetic: none -> 0.99 us  [per_device(): jnp.concatenate([w_radial, w_energy.reshape(1, D), jnp.zeros((15, D), BF)...]
  transfers between devices with their start and end apart: 18 -> 18, of which waited for: 12 -> 12; matrix products, arithmetic and copies ran while one was open for 1% -> 2% of each run, Pallas kernels for 5% -> 4%
where the time goes in v6:
time: 89.7 us; the launch traced here: 89.4 us
  starting transfers between devices  32.3 us (36%)
  waiting for transfers between devices  26.3 us (29%)
  Pallas kernels  25.5 us (28%)
  between operations  2.26 us (3%)
  other arithmetic  2.07 us (2%)
  local copies, waits for them, and re-layouts  0.97 us (1%)
    ppermute x18, starting transfers between devices, shift(): return lax.ppermute(value, AXES, moves(fn))  32.3 us
    ppermute x18, waiting for transfers between devices, shift(): return lax.ppermute(value, AXES, moves(fn))  26.3 us
    pallas_call x1, Pallas kernels, batch(): pl.pallas_call(main_kernel, out_shape=(jax.ShapeDtypeStruct((1, 16), F32)...  17.5 us
    pallas_call x2, Pallas kernels, place(): pl.pallas_call(functools.partial(place_kernel, c), out_shape=(big, big, j...  5.28 us
  transfers between devices with their start and end apart: 18, of which 12 were waited for; matrix products, arithmetic and copies ran while one was open for 2% of the time, Pallas kernels for 4%

profile of v6, /device:TPU:1, one launch (start us, length us, event | category | flops | bytes accessed | tf_op | source)
XLA Modules:
  0.0 89.4 jit_solution(13641115762897347036)
XLA Ops:
  1.9 1.6 %pack.1 = bf16[80,512]{1,0:T(8,128)(2,1)} custom-call(s32[1]{0:T(128)} %bitcast.me_ref, bf16[64,512]{1,0:T(8,128)(2,1)} %bitcast.25, f32[3,1,64]{2,1,0:T(1,128)} %bitcast.27, s32[1,256]{1,0:T(1,128)} %src_ref.1, s32[1,256]{1,0:T(1,128)} %dst_ref.1, s32[1,1]{1,0:T(1,128)S(6)} %copy.43.ec_ref, s32[1,1024]{1,0:T(1,128)} %tin_ref.1, s32[1,1024]{1,0:T(1,128)} %tout_ref.1, ...), custom_call_target="tpu_custom_call" | custom-call | tf_op jit(solution)/shard_map/pack/pallas_call | solution.py:82
  3.6 5.2 %collective-permute-start.2 = (bf16[1,80,512]{2,1,0:T(8,128)(2,1)}, bf16[1,80,512]{2,1,0:T(8,128)(2,1)S(1)}, u32[]{:S(2)}, u32[]{:S(2)}) collective-permute-start(bf16[1,80,512]{2,1,0:T(8,128)(2,1)} %bitcast.20), channel_id=1, source_target_pairs={{0,6},{1,7},{2,4},{3,5},{4,2},{5,3},{6,0},{7,1},{8,14},{9,15},{10,... | collective-permute-start | bytes 245768 | tf_op jit(solution)/shard_map/ppermute | solution.py:567
  8.7 0.0 collective-permute-start.1
  8.7 0.3 collective-permute-start
  9.0 1.9 %collective-permute-done.2 = bf16[1,80,512]{2,1,0:T(8,128)(2,1)S(1)} collective-permute-done((bf16[1,80,512]{2,1,0:T(8,128)(2,1)}, bf16[1,80,512]{2,1,0:T(8,128)(2,1)S(1)}, u32[]{:S(2)}, u32[]{:S(2)}) %collective-permute-start.2) | collective-permute-done | bytes 81952 | tf_op jit(solution)/shard_map/ppermute | solution.py:567
  10.9 4.9 %collective-permute-done.1 = bf16[1,80,512]{2,1,0:T(8,128)(2,1)S(1)} collective-permute-done((bf16[1,80,512]{2,1,0:T(8,128)(2,1)}, bf16[1,80,512]{2,1,0:T(8,128)(2,1)S(1)}, u32[]{:S(2)}, u32[]{:S(2)}) %collective-permute-start.1) | collective-permute-done | bytes 81952 | tf_op jit(solution)/shard_map/ppermute | solution.py:567
  15.8 0.0 collective-permute-done
  15.8 0.9 %pad_maximum_fusion.own_ref = bf16[4,80,512]{2,1,0:T(8,128)(2,1)S(1)} fusion(bf16[1,80,512]{2,1,0:T(8,128)(2,1)S(1)} %collective-permute-done.2, bf16[1,80,512]{2,1,0:T(8,128)(2,1)S(1)} %collective-permute-done.1, bf16[1,80,512]{2,1,0:T(8,128)(2,1)S(1)} %collective-permute-done, bf16[1,80,512]{2,1,0:T(8,128)(2,1)} %bitcast.23), kind=kLoop, calls=%fused_computation | loop fusion | flops 491520 | bytes 655360 | tf_op jit(solution)/shard_map/concatenate | solution.py:571
  16.7 1.0 %collective-permute-start.3 = (bf16[4,80,512]{2,1,0:T(8,128)(2,1)S(1)}, bf16[4,80,512]{2,1,0:T(8,128)(2,1)S(1)}, u32[]{:S(2)}, u32[]{:S(2)}) collective-permute-start(bf16[4,80,512]{2,1,0:T(8,128)(2,1)S(1)} %pad_maximum_fusion.own_ref), channel_id=1, source_target_pairs={{0,1},{1,0},{2,3},{3,2},{4,5},{5,4},{6,7},{7,6},{8,9},{9,8},{10,11... | collective-permute-start | bytes 983048 | tf_op jit(solution)/shard_map/ppermute | solution.py:567
  17.6 0.7 reshape.44
  18.3 0.1 pad.6.clone
  18.4 1.0 %maximum_maximum_fusion.wide_ref = bf16[144,512]{1,0:T(8,128)(2,1)S(1)} fusion(bf16[1,512]{1,0:T(2,128)(2,1)S(1)} %reshape.44, bf16[128,512]{1,0:T(8,128)(2,1)} %param.27, bf16[144]{0:T(256)(128)(2,1)S(1)} %pad.6.clone), kind=kLoop, calls=%fused_computation.2 | loop fusion | flops 442368 | bytes 279840 | tf_op jit(solution)/shard_map/concatenate | solution.py:621
  19.4 0.0 collective-permute-done.3.other_ref
  19.4 17.5 %batch.1 = (f32[1,16]{1,0:T(1,128)}, f32[3,1,64]{2,1,0:T(1,128)}, bf16[128,512]{1,0:T(8,128)(2,1)S(1)}, f32[64,128]{1,0:T(8,128)S(1)}, bf16[4,4,72,128]{3,2,1,0:T(8,128)(2,1)S(1)}) custom-call(s32[1]{0:T(128)} %bitcast.me_ref, s32[1]{0:T(128)} %bitcast.1.slice_ref, s32[1]{0:T(128)} %bitcast.2.u_ref, bf16[4,80,512]{2,1,0:T(8,128)(2,1)S(1)} %pad_maximum_fusion.own_ref, ...), custom_call_target="tpu_custom_call" | custom-call | tf_op jit(solution)/shard_map/batch/pallas_call | solution.py:399
  36.9 0.0 copy-start
  36.9 0.0 copy-start.1
  37.0 2.9 %collective-permute-start.4 = (bf16[4,72,128]{2,1,0:T(8,128)(2,1)S(1)}, bf16[4,72,128]{2,1,0:T(8,128)(2,1)S(1)}, u32[]{:S(2)}, u32[]{:S(2)}) collective-permute-start(bf16[4,72,128]{2,1,0:T(8,128)(2,1)S(1)} %get-tuple-element.53), channel_id=1, source_target_pairs={{0,64},{1,17},{2,66},{3,19},{4,68},{5,21},{6,70},{7,23},{8,72},{9,... | collective-permute-start | bytes 221192 | tf_op jit(solution)/shard_map/ppermute | solution.py:567
  39.8 0.8 collective-permute-start.6
  40.6 0.7 collective-permute-start.5
  41.3 0.7 collective-permute-done.4
  42.0 1.3 %collective-permute-done.6 = bf16[4,72,128]{2,1,0:T(8,128)(2,1)S(1)} collective-permute-done((bf16[4,72,128]{2,1,0:T(8,128)(2,1)S(1)}, bf16[4,72,128]{2,1,0:T(8,128)(2,1)S(1)}, u32[]{:S(2)}, u32[]{:S(2)}) %collective-permute-start.6) | collective-permute-done | bytes 73760 | tf_op jit(solution)/shard_map/ppermute | solution.py:567
  43.3 1.7 %collective-permute-done.5 = bf16[4,72,128]{2,1,0:T(8,128)(2,1)S(1)} collective-permute-done((bf16[4,72,128]{2,1,0:T(8,128)(2,1)S(1)}, bf16[4,72,128]{2,1,0:T(8,128)(2,1)S(1)}, u32[]{:S(2)}, u32[]{:S(2)}) %collective-permute-start.5) | collective-permute-done | bytes 73760 | tf_op jit(solution)/shard_map/ppermute | solution.py:567
  45.1 2.6 %collective-permute-start.9 = (bf16[4,72,128]{2,1,0:T(8,128)(2,1)S(1)}, bf16[4,72,128]{2,1,0:T(8,128)(2,1)S(1)}, u32[]{:S(2)}, u32[]{:S(2)}) collective-permute-start(bf16[4,72,128]{2,1,0:T(8,128)(2,1)S(1)} %fusion.1), channel_id=1, source_target_pairs={{0,24},{1,97},{2,26},{3,99},{4,28},{5,101},{6,30},{7,103},{8,0},{9... | collective-permute-start | bytes 221192 | tf_op jit(solution)/shard_map/ppermute | solution.py:567
  47.6 0.0 collective-permute-start.8
  47.6 1.7 %collective-permute-start.7 = (bf16[4,72,128]{2,1,0:T(8,128)(2,1)S(1)}, bf16[4,72,128]{2,1,0:T(8,128)(2,1)S(1)}, u32[]{:S(2)}, u32[]{:S(2)}) collective-permute-start(bf16[4,72,128]{2,1,0:T(8,128)(2,1)S(1)} %fusion.1), channel_id=1, source_target_pairs={{0,16},{1,65},{2,18},{3,67},{4,20},{5,69},{6,22},{7,71},{8,24},{9,... | collective-permute-start | bytes 221192 | tf_op jit(solution)/shard_map/ppermute | solution.py:567
  49.4 0.0 collective-permute-done.9
  49.4 3.5 %collective-permute-done.8 = bf16[4,72,128]{2,1,0:T(8,128)(2,1)S(1)} collective-permute-done((bf16[4,72,128]{2,1,0:T(8,128)(2,1)S(1)}, bf16[4,72,128]{2,1,0:T(8,128)(2,1)S(1)}, u32[]{:S(2)}, u32[]{:S(2)}) %collective-permute-start.8) | collective-permute-done | bytes 73760 | tf_op jit(solution)/shard_map/ppermute | solution.py:567
  52.8 0.0 collective-permute-done.7
  52.9 4.8 %collective-permute-start.10 = (bf16[4,72,128]{2,1,0:T(8,128)(2,1)S(1)}, bf16[4,72,128]{2,1,0:T(8,128)(2,1)S(1)}, u32[]{:S(2)}, u32[]{:S(2)}) collective-permute-start(bf16[4,72,128]{2,1,0:T(8,128)(2,1)S(1)} %add_convert_fusion.1), channel_id=1, source_target_pairs={{0,134},{1,135},{2,132},{3,133},{4,130},{5,131},{6,128},{7,129},{8... | collective-permute-start | bytes 221192 | tf_op jit(solution)/shard_map/ppermute | solution.py:567
  57.7 2.2 %collective-permute-done.10 = bf16[4,72,128]{2,1,0:T(8,128)(2,1)S(1)} collective-permute-done((bf16[4,72,128]{2,1,0:T(8,128)(2,1)S(1)}, bf16[4,72,128]{2,1,0:T(8,128)(2,1)S(1)}, u32[]{:S(2)}, u32[]{:S(2)}) %collective-permute-start.10) | collective-permute-done | bytes 73760 | tf_op jit(solution)/shard_map/ppermute | solution.py:567
  59.9 1.3 %collective-permute-start.13 = (bf16[4,72,128]{2,1,0:T(8,128)(2,1)S(1)}, bf16[4,72,128]{2,1,0:T(8,128)(2,1)S(1)}, u32[]{:S(2)}, u32[]{:S(2)}) collective-permute-start(bf16[4,72,128]{2,1,0:T(8,128)(2,1)S(1)} %get-tuple-element.52), channel_id=1, source_target_pairs={{0,6},{1,7},{2,4},{3,5},{4,2},{5,3},{6,0},{7,1},{8,14},{9,15},{10,... | collective-permute-start | bytes 221192 | tf_op jit(solution)/shard_map/ppermute | solution.py:567
  61.1 0.4 collective-permute-start.12
  61.6 1.9 %collective-permute-start.11 = (bf16[4,72,128]{2,1,0:T(8,128)(2,1)S(1)}, bf16[4,72,128]{2,1,0:T(8,128)(2,1)S(1)}, u32[]{:S(2)}, u32[]{:S(2)}) collective-permute-start(bf16[4,72,128]{2,1,0:T(8,128)(2,1)S(1)} %get-tuple-element.52), channel_id=1, source_target_pairs={{0,2},{1,3},{2,0},{3,1},{4,6},{5,7},{6,4},{7,5},{8,10},{9,11},{10,... | collective-permute-start | bytes 221192 | tf_op jit(solution)/shard_map/ppermute | solution.py:567
  63.5 0.0 copy-done
  63.5 0.0 copy-done.1
  63.5 1.1 %node.1 = f32[64,512]{1,0:T(8,128)} custom-call(bf16[128,512]{1,0:T(8,128)(2,1)S(1)} %get-tuple-element.33.sums_ref, f32[64,128]{1,0:T(8,128)S(1)} %get-tuple-element.34.cot_ref, bf16[512,512]{1,0:T(8,128)(2,1)S(1)} %copy-done, bf16[512,512]{1,0:T(8,128)(2,1)S(1)} %copy-done.1, bf16[144,512]{1,0:T(8,128)(2,1)S(1)} %maximum_maximum_fusion.wide_ref), custom_call_target="tpu_custom_call" | custom-call | tf_op jit(solution)/shard_map/node/pallas_call | solution.py:460
  64.6 0.5 collective-permute-done.13
  65.1 1.5 %collective-permute-done.12 = bf16[4,72,128]{2,1,0:T(8,128)(2,1)S(1)} collective-permute-done((bf16[4,72,128]{2,1,0:T(8,128)(2,1)S(1)}, bf16[4,72,128]{2,1,0:T(8,128)(2,1)S(1)}, u32[]{:S(2)}, u32[]{:S(2)}) %collective-permute-start.12) | collective-permute-done | bytes 73760 | tf_op jit(solution)/shard_map/ppermute | solution.py:567
  66.5 0.0 collective-permute-done.11
  66.6 0.7 collective-permute-start.16
  67.2 1.6 %collective-permute-start.15 = (bf16[16,72,128]{2,1,0:T(8,128)(2,1)S(1)}, bf16[16,72,128]{2,1,0:T(8,128)(2,1)S(1)}, u32[]{:S(2)}, u32[]{:S(2)}) collective-permute-start(bf16[16,72,128]{2,1,0:T(8,128)(2,1)S(1)} %pad_maximum_fusion.1), channel_id=1, source_target_pairs={{0,96},{1,25},{2,98},{3,27},{4,100},{5,29},{6,102},{7,31},{8,104},... | collective-permute-start | bytes 884744 | tf_op jit(solution)/shard_map/ppermute | solution.py:567
  68.8 0.0 collective-permute-start.14
  68.9 5.0 %collective-permute-done.16 = bf16[16,72,128]{2,1,0:T(8,128)(2,1)S(1)} collective-permute-done((bf16[16,72,128]{2,1,0:T(8,128)(2,1)S(1)}, bf16[16,72,128]{2,1,0:T(8,128)(2,1)S(1)}, u32[]{:S(2)}, u32[]{:S(2)}) %collective-permute-start.16) | collective-permute-done | bytes 294944 | tf_op jit(solution)/shard_map/ppermute | solution.py:567
  73.8 1.6 %collective-permute-done.15 = bf16[16,72,128]{2,1,0:T(8,128)(2,1)S(1)} collective-permute-done((bf16[16,72,128]{2,1,0:T(8,128)(2,1)S(1)}, bf16[16,72,128]{2,1,0:T(8,128)(2,1)S(1)}, u32[]{:S(2)}, u32[]{:S(2)}) %collective-permute-start.15) | collective-permute-done | bytes 294944 | tf_op jit(solution)/shard_map/ppermute | solution.py:567
  75.4 1.8 %collective-permute-done.14 = bf16[16,72,128]{2,1,0:T(8,128)(2,1)S(1)} collective-permute-done((bf16[16,72,128]{2,1,0:T(8,128)(2,1)S(1)}, bf16[16,72,128]{2,1,0:T(8,128)(2,1)S(1)}, u32[]{:S(2)}, u32[]{:S(2)}) %collective-permute-start.14) | collective-permute-done | bytes 294944 | tf_op jit(solution)/shard_map/ppermute | solution.py:567
  77.3 6.6 %collective-permute-start.17 = (bf16[64,72,128]{2,1,0:T(8,128)(2,1)S(1)}, bf16[64,72,128]{2,1,0:T(8,128)(2,1)S(1)}, u32[]{:S(2)}, u32[]{:S(2)}) collective-permute-start(bf16[64,72,128]{2,1,0:T(8,128)(2,1)S(1)} %constant_dynamic-update-slice_fusion.ref), channel_id=1, source_target_pairs={{0,1},{1,0},{2,3},{3,2},{4,5},{5,4},{6,7},{7,6},{8,9},{9,8},{10,11... | collective-permute-start | bytes 3538952 | tf_op jit(solution)/shard_map/ppermute | solution.py:567
  83.9 2.6 %place.2 = (f32[512,512]{1,0:T(8,128)}, f32[512,512]{1,0:T(8,128)}, f32[128,512]{1,0:T(8,128)}, f32[512,512]{1,0:T(8,128)}, f32[512,512]{1,0:T(8,128)}, /*index=5*/f32[1,512]{1,0:T(1,128)}) custom-call(s32[1]{0:T(128)} %bitcast.12.x_ref, s32[1]{0:T(128)} %bitcast.13.y_ref, s32[1]{0:T(128)} %bitcast.1.slice_ref, ...), custom_call_target="tpu_custom_call" | custom-call | tf_op jit(solution)/shard_map/place/pallas_call | solution.py:528
  86.6 0.0 collective-permute-done.17.ref
  86.6 2.6 %place.3 = (f32[512,512]{1,0:T(8,128)}, f32[512,512]{1,0:T(8,128)}, f32[128,512]{1,0:T(8,128)}, f32[512,512]{1,0:T(8,128)}, f32[512,512]{1,0:T(8,128)}, /*index=5*/f32[1,512]{1,0:T(1,128)}) custom-call(s32[1]{0:T(128)} %bitcast.12.x_ref, s32[1]{0:T(128)} %bitcast.13.y_ref, ...), custom_call_target="tpu_custom_call", output_to_operand_aliasing={{0}: (4, {}), {1}: (5, {}), {2}: (6, {}), {3}: (7, {}), {4}... | custom-call | tf_op jit(solution)/shard_map/place/pallas_call | solution.py:528
  (12 shorter events, 0.3 us)
Async XLA Ops:
  3.6 7.3 %collective-permute-start.2 = (bf16[1,80,512]{2,1,0:T(8,128)(2,1)}, bf16[1,80,512]{2,1,0:T(8,128)(2,1)S(1)}, u32[]{:S(2)}, u32[]{:S(2)}) collective-permute-start(bf16[1,80,512]{2,1,0:T(8,128)(2,1)} %bitcast.20), channel_id=1, source_target_pairs={{0,6},{1,7},{2,4},{3,5},{4,2},{5,3},{6,0},{7,1},{8,14},{9,15},{10,... | collective-permute-start | bytes 245768 | tf_op jit(solution)/shard_map/ppermute | solution.py:567
  8.7 7.0 %collective-permute-start.1 = (bf16[1,80,512]{2,1,0:T(8,128)(2,1)}, bf16[1,80,512]{2,1,0:T(8,128)(2,1)S(1)}, u32[]{:S(2)}, u32[]{:S(2)}) collective-permute-start(bf16[1,80,512]{2,1,0:T(8,128)(2,1)} %bitcast.21), channel_id=1, source_target_pairs={{0,4},{1,5},{2,6},{3,7},{4,0},{5,1},{6,2},{7,3},{8,12},{9,13},{10,... | collective-permute-start | bytes 245768 | tf_op jit(solution)/shard_map/ppermute | solution.py:567
  8.7 7.0 %collective-permute-start = (bf16[1,80,512]{2,1,0:T(8,128)(2,1)}, bf16[1,80,512]{2,1,0:T(8,128)(2,1)S(1)}, u32[]{:S(2)}, u32[]{:S(2)}) collective-permute-start(bf16[1,80,512]{2,1,0:T(8,128)(2,1)} %bitcast.22), channel_id=1, source_target_pairs={{0,2},{1,3},{2,0},{3,1},{4,6},{5,7},{6,4},{7,5},{8,10},{9,11},{10,... | collective-permute-start | bytes 245768 | tf_op jit(solution)/shard_map/ppermute | solution.py:567
  16.7 2.7 %collective-permute-start.3 = (bf16[4,80,512]{2,1,0:T(8,128)(2,1)S(1)}, bf16[4,80,512]{2,1,0:T(8,128)(2,1)S(1)}, u32[]{:S(2)}, u32[]{:S(2)}) collective-permute-start(bf16[4,80,512]{2,1,0:T(8,128)(2,1)S(1)} %pad_maximum_fusion.own_ref), channel_id=1, source_target_pairs={{0,1},{1,0},{2,3},{3,2},{4,5},{5,4},{6,7},{7,6},{8,9},{9,8},{10,11... | collective-permute-start | bytes 983048 | tf_op jit(solution)/shard_map/ppermute | solution.py:567
  36.9 26.6 %copy-start = (bf16[512,512]{1,0:T(8,128)(2,1)S(1)}, bf16[512,512]{1,0:T(8,128)(2,1)}, u32[]{:S(2)}) copy-start(bf16[512,512]{1,0:T(8,128)(2,1)} %ws_ref.1) | copy-start | bytes 1572868
  36.9 26.6 %copy-start.1 = (bf16[512,512]{1,0:T(8,128)(2,1)S(1)}, bf16[512,512]{1,0:T(8,128)(2,1)}, u32[]{:S(2)}) copy-start(bf16[512,512]{1,0:T(8,128)(2,1)} %wd_ref.1) | copy-start | bytes 1572868
  37.0 5.1 %collective-permute-start.4 = (bf16[4,72,128]{2,1,0:T(8,128)(2,1)S(1)}, bf16[4,72,128]{2,1,0:T(8,128)(2,1)S(1)}, u32[]{:S(2)}, u32[]{:S(2)}) collective-permute-start(bf16[4,72,128]{2,1,0:T(8,128)(2,1)S(1)} %get-tuple-element.53), channel_id=1, source_target_pairs={{0,64},{1,17},{2,66},{3,19},{4,68},{5,21},{6,70},{7,23},{8,72},{9,... | collective-permute-start | bytes 221192 | tf_op jit(solution)/shard_map/ppermute | solution.py:567
  39.8 3.5 %collective-permute-start.6 = (bf16[4,72,128]{2,1,0:T(8,128)(2,1)S(1)}, bf16[4,72,128]{2,1,0:T(8,128)(2,1)S(1)}, u32[]{:S(2)}, u32[]{:S(2)}) collective-permute-start(bf16[4,72,128]{2,1,0:T(8,128)(2,1)S(1)} %get-tuple-element.54), channel_id=1, source_target_pairs={{0,96},{1,25},{2,98},{3,27},{4,100},{5,29},{6,102},{7,31},{8,104},... | collective-permute-start | bytes 221192 | tf_op jit(solution)/shard_map/ppermute | solution.py:567
  40.6 4.4 %collective-permute-start.5 = (bf16[4,72,128]{2,1,0:T(8,128)(2,1)S(1)}, bf16[4,72,128]{2,1,0:T(8,128)(2,1)S(1)}, u32[]{:S(2)}, u32[]{:S(2)}) collective-permute-start(bf16[4,72,128]{2,1,0:T(8,128)(2,1)S(1)} %get-tuple-element.55), channel_id=1, source_target_pairs={{0,32},{1,9},{2,34},{3,11},{4,36},{5,13},{6,38},{7,15},{8,40},{9,1... | collective-permute-start | bytes 221192 | tf_op jit(solution)/shard_map/ppermute | solution.py:567
  45.1 4.3 %collective-permute-start.9 = (bf16[4,72,128]{2,1,0:T(8,128)(2,1)S(1)}, bf16[4,72,128]{2,1,0:T(8,128)(2,1)S(1)}, u32[]{:S(2)}, u32[]{:S(2)}) collective-permute-start(bf16[4,72,128]{2,1,0:T(8,128)(2,1)S(1)} %fusion.1), channel_id=1, source_target_pairs={{0,24},{1,97},{2,26},{3,99},{4,28},{5,101},{6,30},{7,103},{8,0},{9... | collective-permute-start | bytes 221192 | tf_op jit(solution)/shard_map/ppermute | solution.py:567
  47.6 5.2 %collective-permute-start.8 = (bf16[4,72,128]{2,1,0:T(8,128)(2,1)S(1)}, bf16[4,72,128]{2,1,0:T(8,128)(2,1)S(1)}, u32[]{:S(2)}, u32[]{:S(2)}) collective-permute-start(bf16[4,72,128]{2,1,0:T(8,128)(2,1)S(1)} %fusion.1), channel_id=1, source_target_pairs={{0,8},{1,33},{2,10},{3,35},{4,12},{5,37},{6,14},{7,39},{8,16},{9,4... | collective-permute-start | bytes 221192 | tf_op jit(solution)/shard_map/ppermute | solution.py:567
  47.6 5.2 %collective-permute-start.7 = (bf16[4,72,128]{2,1,0:T(8,128)(2,1)S(1)}, bf16[4,72,128]{2,1,0:T(8,128)(2,1)S(1)}, u32[]{:S(2)}, u32[]{:S(2)}) collective-permute-start(bf16[4,72,128]{2,1,0:T(8,128)(2,1)S(1)} %fusion.1), channel_id=1, source_target_pairs={{0,16},{1,65},{2,18},{3,67},{4,20},{5,69},{6,22},{7,71},{8,24},{9,... | collective-permute-start | bytes 221192 | tf_op jit(solution)/shard_map/ppermute | solution.py:567
  52.9 6.9 %collective-permute-start.10 = (bf16[4,72,128]{2,1,0:T(8,128)(2,1)S(1)}, bf16[4,72,128]{2,1,0:T(8,128)(2,1)S(1)}, u32[]{:S(2)}, u32[]{:S(2)}) collective-permute-start(bf16[4,72,128]{2,1,0:T(8,128)(2,1)S(1)} %add_convert_fusion.1), channel_id=1, source_target_pairs={{0,134},{1,135},{2,132},{3,133},{4,130},{5,131},{6,128},{7,129},{8... | collective-permute-start | bytes 221192 | tf_op jit(solution)/shard_map/ppermute | solution.py:567
  59.9 5.2 %collective-permute-start.13 = (bf16[4,72,128]{2,1,0:T(8,128)(2,1)S(1)}, bf16[4,72,128]{2,1,0:T(8,128)(2,1)S(1)}, u32[]{:S(2)}, u32[]{:S(2)}) collective-permute-start(bf16[4,72,128]{2,1,0:T(8,128)(2,1)S(1)} %get-tuple-element.52), channel_id=1, source_target_pairs={{0,6},{1,7},{2,4},{3,5},{4,2},{5,3},{6,0},{7,1},{8,14},{9,15},{10,... | collective-permute-start | bytes 221192 | tf_op jit(solution)/shard_map/ppermute | solution.py:567
  61.1 5.4 %collective-permute-start.12 = (bf16[4,72,128]{2,1,0:T(8,128)(2,1)S(1)}, bf16[4,72,128]{2,1,0:T(8,128)(2,1)S(1)}, u32[]{:S(2)}, u32[]{:S(2)}) collective-permute-start(bf16[4,72,128]{2,1,0:T(8,128)(2,1)S(1)} %get-tuple-element.52), channel_id=1, source_target_pairs={{0,4},{1,5},{2,6},{3,7},{4,0},{5,1},{6,2},{7,3},{8,12},{9,13},{10,... | collective-permute-start | bytes 221192 | tf_op jit(solution)/shard_map/ppermute | solution.py:567
  61.6 5.0 %collective-permute-start.11 = (bf16[4,72,128]{2,1,0:T(8,128)(2,1)S(1)}, bf16[4,72,128]{2,1,0:T(8,128)(2,1)S(1)}, u32[]{:S(2)}, u32[]{:S(2)}) collective-permute-start(bf16[4,72,128]{2,1,0:T(8,128)(2,1)S(1)} %get-tuple-element.52), channel_id=1, source_target_pairs={{0,2},{1,3},{2,0},{3,1},{4,6},{5,7},{6,4},{7,5},{8,10},{9,11},{10,... | collective-permute-start | bytes 221192 | tf_op jit(solution)/shard_map/ppermute | solution.py:567
  66.6 7.3 %collective-permute-start.16 = (bf16[16,72,128]{2,1,0:T(8,128)(2,1)S(1)}, bf16[16,72,128]{2,1,0:T(8,128)(2,1)S(1)}, u32[]{:S(2)}, u32[]{:S(2)}) collective-permute-start(bf16[16,72,128]{2,1,0:T(8,128)(2,1)S(1)} %pad_maximum_fusion.1), channel_id=1, source_target_pairs={{0,64},{1,17},{2,66},{3,19},{4,68},{5,21},{6,70},{7,23},{8,72},{9,... | collective-permute-start | bytes 884744 | tf_op jit(solution)/shard_map/ppermute | solution.py:567
  67.2 8.2 %collective-permute-start.15 = (bf16[16,72,128]{2,1,0:T(8,128)(2,1)S(1)}, bf16[16,72,128]{2,1,0:T(8,128)(2,1)S(1)}, u32[]{:S(2)}, u32[]{:S(2)}) collective-permute-start(bf16[16,72,128]{2,1,0:T(8,128)(2,1)S(1)} %pad_maximum_fusion.1), channel_id=1, source_target_pairs={{0,96},{1,25},{2,98},{3,27},{4,100},{5,29},{6,102},{7,31},{8,104},... | collective-permute-start | bytes 884744 | tf_op jit(solution)/shard_map/ppermute | solution.py:567
  68.8 8.4 %collective-permute-start.14 = (bf16[16,72,128]{2,1,0:T(8,128)(2,1)S(1)}, bf16[16,72,128]{2,1,0:T(8,128)(2,1)S(1)}, u32[]{:S(2)}, u32[]{:S(2)}) collective-permute-start(bf16[16,72,128]{2,1,0:T(8,128)(2,1)S(1)} %pad_maximum_fusion.1), channel_id=1, source_target_pairs={{0,32},{1,9},{2,34},{3,11},{4,36},{5,13},{6,38},{7,15},{8,40},{9,1... | collective-permute-start | bytes 884744 | tf_op jit(solution)/shard_map/ppermute | solution.py:567
  77.3 9.2 %collective-permute-start.17 = (bf16[64,72,128]{2,1,0:T(8,128)(2,1)S(1)}, bf16[64,72,128]{2,1,0:T(8,128)(2,1)S(1)}, u32[]{:S(2)}, u32[]{:S(2)}) collective-permute-start(bf16[64,72,128]{2,1,0:T(8,128)(2,1)S(1)} %constant_dynamic-update-slice_fusion.ref), channel_id=1, source_target_pairs={{0,1},{1,0},{2,3},{3,2},{4,5},{5,4},{6,7},{7,6},{8,9},{9,8},{10,11... | collective-permute-start | bytes 3538952 | tf_op jit(solution)/shard_map/ppermute | solution.py:567

commit v7 on v6

--- a/solution.py
+++ b/solution.py
@@ -616,9 +616,11 @@
         graph_ids,
         energy_cot,
     )[None]
-    own = join(piece, *[shift(piece, zl=k) for k in (1, 2, 3)])
+    wide = jnp.concatenate([w_radial, w_energy.reshape(1, D), jnp.zeros((15, D), BF)], axis=0)
+    near = [shift(piece, zl=k) for k in (1, 2, 3)]
+    *near, wide = lax.optimization_barrier((*near, wide))
+    own = join(piece, *near)
     other = shift(own, c=1)
-    wide = jnp.concatenate([w_radial, w_energy.reshape(1, D), jnp.zeros((15, D), BF)], axis=0)
     energy, pos_grad, sums, cot, payload = batch(
         me, part, u, own, other, w_src, w_dst, wide, w_trip, w_out
     )

time: 89.7 us -> 89.4 us (level)
  waiting for transfers between devices: 26.3 us -> 25.3 us
    ppermute x18, waiting for transfers between devices: 26.3 us -> 25.3 us  [shift(): return lax.ppermute(value, AXES, moves(fn))]
  transfers between devices with their start and end apart: 18 -> 18, of which waited for: 12 -> 13; matrix products, arithmetic and copies ran while one was open for 2% -> 2% of each run, Pallas kernels for 4% -> 4%
where the time goes in v7:
time: 89.4 us; the launch traced here: 89.2 us
  starting transfers between devices  33.1 us (37%)
  Pallas kernels  25.4 us (28%)
  waiting for transfers between devices  25.3 us (28%)
  between operations  2.25 us (3%)
  other arithmetic  2.07 us (2%)
  local copies, waits for them, and re-layouts  0.97 us (1%)
    ppermute x18, starting transfers between devices, shift(): return lax.ppermute(value, AXES, moves(fn))  33.1 us
    ppermute x18, waiting for transfers between devices, shift(): return lax.ppermute(value, AXES, moves(fn))  25.3 us
    pallas_call x1, Pallas kernels, batch(): pl.pallas_call(main_kernel, out_shape=(jax.ShapeDtypeStruct((1, 16), F32)...  17.4 us
    pallas_call x2, Pallas kernels, place(): pl.pallas_call(functools.partial(place_kernel, c), out_shape=(big, big, j...  5.28 us
  transfers between devices with their start and end apart: 18, of which 13 were waited for; matrix products, arithmetic and copies ran while one was open for 2% of the time, Pallas kernels for 4%

profile of v7, /device:TPU:1, one launch (start us, length us, event | category | flops | bytes accessed | tf_op | source)
XLA Modules:
  0.0 89.2 jit_solution(2016780978926014353)
XLA Ops:
  1.9 1.6 %pack.1 = bf16[80,512]{1,0:T(8,128)(2,1)} custom-call(s32[1]{0:T(128)} %bitcast.me_ref, bf16[64,512]{1,0:T(8,128)(2,1)} %bitcast.25, f32[3,1,64]{2,1,0:T(1,128)} %bitcast.27, s32[1,256]{1,0:T(1,128)} %src_ref.1, s32[1,256]{1,0:T(1,128)} %dst_ref.1, s32[1,1]{1,0:T(1,128)S(6)} %copy.43.ec_ref, s32[1,1024]{1,0:T(1,128)} %tin_ref.1, s32[1,1024]{1,0:T(1,128)} %tout_ref.1, ...), custom_call_target="tpu_custom_call" | custom-call | tf_op jit(solution)/shard_map/pack/pallas_call | solution.py:82
  3.6 5.2 %collective-permute-start.2 = (bf16[1,80,512]{2,1,0:T(8,128)(2,1)}, bf16[1,80,512]{2,1,0:T(8,128)(2,1)S(1)}, u32[]{:S(2)}, u32[]{:S(2)}) collective-permute-start(bf16[1,80,512]{2,1,0:T(8,128)(2,1)} %bitcast.20), channel_id=1, source_target_pairs={{0,6},{1,7},{2,4},{3,5},{4,2},{5,3},{6,0},{7,1},{8,14},{9,15},{10,... | collective-permute-start | bytes 245768 | tf_op jit(solution)/shard_map/ppermute | solution.py:567
  8.7 0.0 collective-permute-start.1
  8.7 0.3 collective-permute-start
  9.0 0.7 reshape.44
  9.7 0.1 pad.10.clone
  9.8 1.0 %maximum_maximum_fusion.wide_ref = bf16[144,512]{1,0:T(8,128)(2,1)S(1)} fusion(bf16[1,512]{1,0:T(2,128)(2,1)S(1)} %reshape.44, bf16[128,512]{1,0:T(8,128)(2,1)} %param.27, bf16[144]{0:T(256)(128)(2,1)S(1)} %pad.10.clone), kind=kLoop, calls=%fused_computation.2 | loop fusion | flops 442368 | bytes 279840 | tf_op jit(solution)/shard_map/concatenate | solution.py:619
  10.8 0.1 collective-permute-done.2
  10.9 4.9 %collective-permute-done.1 = bf16[1,80,512]{2,1,0:T(8,128)(2,1)S(1)} collective-permute-done((bf16[1,80,512]{2,1,0:T(8,128)(2,1)}, bf16[1,80,512]{2,1,0:T(8,128)(2,1)S(1)}, u32[]{:S(2)}, u32[]{:S(2)}) %collective-permute-start.1) | collective-permute-done | bytes 81952 | tf_op jit(solution)/shard_map/ppermute | solution.py:567
  15.8 0.0 collective-permute-done
  15.8 0.9 %pad_maximum_fusion.own_ref = bf16[4,80,512]{2,1,0:T(8,128)(2,1)S(1)} fusion(bf16[1,80,512]{2,1,0:T(8,128)(2,1)S(1)} %collective-permute-done.2, bf16[1,80,512]{2,1,0:T(8,128)(2,1)S(1)} %collective-permute-done.1, bf16[1,80,512]{2,1,0:T(8,128)(2,1)S(1)} %collective-permute-done, bf16[1,80,512]{2,1,0:T(8,128)(2,1)} %bitcast.23), kind=kLoop, calls=%fused_computation | loop fusion | flops 491520 | bytes 655360 | tf_op jit(solution)/shard_map/concatenate | solution.py:571
  16.7 1.0 %collective-permute-start.3 = (bf16[4,80,512]{2,1,0:T(8,128)(2,1)S(1)}, bf16[4,80,512]{2,1,0:T(8,128)(2,1)S(1)}, u32[]{:S(2)}, u32[]{:S(2)}) collective-permute-start(bf16[4,80,512]{2,1,0:T(8,128)(2,1)S(1)} %pad_maximum_fusion.own_ref), channel_id=1, source_target_pairs={{0,1},{1,0},{2,3},{3,2},{4,5},{5,4},{6,7},{7,6},{8,9},{9,8},{10,11... | collective-permute-start | bytes 983048 | tf_op jit(solution)/shard_map/ppermute | solution.py:567
  17.6 1.3 %collective-permute-done.3.other_ref = bf16[4,80,512]{2,1,0:T(8,128)(2,1)S(1)} collective-permute-done((bf16[4,80,512]{2,1,0:T(8,128)(2,1)S(1)}, bf16[4,80,512]{2,1,0:T(8,128)(2,1)S(1)}, u32[]{:S(2)}, u32[]{:S(2)}) %collective-permute-start.3) | collective-permute-done | bytes 327712 | tf_op jit(solution)/shard_map/ppermute | solution.py:567
  18.9 17.4 %batch.1 = (f32[1,16]{1,0:T(1,128)}, f32[3,1,64]{2,1,0:T(1,128)}, bf16[128,512]{1,0:T(8,128)(2,1)S(1)}, f32[64,128]{1,0:T(8,128)S(1)}, bf16[4,4,72,128]{3,2,1,0:T(8,128)(2,1)S(1)}) custom-call(s32[1]{0:T(128)} %bitcast.me_ref, s32[1]{0:T(128)} %bitcast.1.slice_ref, s32[1]{0:T(128)} %bitcast.2.u_ref, bf16[4,80,512]{2,1,0:T(8,128)(2,1)S(1)} %pad_maximum_fusion.own_ref, ...), custom_call_target="tpu_custom_call" | custom-call | tf_op jit(solution)/shard_map/batch/pallas_call | solution.py:399
  36.3 0.0 copy-start
  36.3 0.0 copy-start.1
  36.4 2.9 %collective-permute-start.4 = (bf16[4,72,128]{2,1,0:T(8,128)(2,1)S(1)}, bf16[4,72,128]{2,1,0:T(8,128)(2,1)S(1)}, u32[]{:S(2)}, u32[]{:S(2)}) collective-permute-start(bf16[4,72,128]{2,1,0:T(8,128)(2,1)S(1)} %get-tuple-element.61), channel_id=1, source_target_pairs={{0,64},{1,17},{2,66},{3,19},{4,68},{5,21},{6,70},{7,23},{8,72},{9,... | collective-permute-start | bytes 221192 | tf_op jit(solution)/shard_map/ppermute | solution.py:567
  39.3 0.8 collective-permute-start.6
  40.0 0.7 collective-permute-start.5
  40.7 0.4 collective-permute-done.4
  41.2 1.3 %collective-permute-done.6 = bf16[4,72,128]{2,1,0:T(8,128)(2,1)S(1)} collective-permute-done((bf16[4,72,128]{2,1,0:T(8,128)(2,1)S(1)}, bf16[4,72,128]{2,1,0:T(8,128)(2,1)S(1)}, u32[]{:S(2)}, u32[]{:S(2)}) %collective-permute-start.6) | collective-permute-done | bytes 73760 | tf_op jit(solution)/shard_map/ppermute | solution.py:567
  42.5 2.0 %collective-permute-done.5 = bf16[4,72,128]{2,1,0:T(8,128)(2,1)S(1)} collective-permute-done((bf16[4,72,128]{2,1,0:T(8,128)(2,1)S(1)}, bf16[4,72,128]{2,1,0:T(8,128)(2,1)S(1)}, u32[]{:S(2)}, u32[]{:S(2)}) %collective-permute-start.5) | collective-permute-done | bytes 73760 | tf_op jit(solution)/shard_map/ppermute | solution.py:567
  44.5 2.6 %collective-permute-start.9 = (bf16[4,72,128]{2,1,0:T(8,128)(2,1)S(1)}, bf16[4,72,128]{2,1,0:T(8,128)(2,1)S(1)}, u32[]{:S(2)}, u32[]{:S(2)}) collective-permute-start(bf16[4,72,128]{2,1,0:T(8,128)(2,1)S(1)} %fusion.1), channel_id=1, source_target_pairs={{0,24},{1,97},{2,26},{3,99},{4,28},{5,101},{6,30},{7,103},{8,0},{9... | collective-permute-start | bytes 221192 | tf_op jit(solution)/shard_map/ppermute | solution.py:567
  47.1 0.0 collective-permute-start.8
  47.1 1.7 %collective-permute-start.7 = (bf16[4,72,128]{2,1,0:T(8,128)(2,1)S(1)}, bf16[4,72,128]{2,1,0:T(8,128)(2,1)S(1)}, u32[]{:S(2)}, u32[]{:S(2)}) collective-permute-start(bf16[4,72,128]{2,1,0:T(8,128)(2,1)S(1)} %fusion.1), channel_id=1, source_target_pairs={{0,16},{1,65},{2,18},{3,67},{4,20},{5,69},{6,22},{7,71},{8,24},{9,... | collective-permute-start | bytes 221192 | tf_op jit(solution)/shard_map/ppermute | solution.py:567
  48.8 0.0 collective-permute-done.9
  48.8 3.5 %collective-permute-done.8 = bf16[4,72,128]{2,1,0:T(8,128)(2,1)S(1)} collective-permute-done((bf16[4,72,128]{2,1,0:T(8,128)(2,1)S(1)}, bf16[4,72,128]{2,1,0:T(8,128)(2,1)S(1)}, u32[]{:S(2)}, u32[]{:S(2)}) %collective-permute-start.8) | collective-permute-done | bytes 73760 | tf_op jit(solution)/shard_map/ppermute | solution.py:567
  52.3 0.0 collective-permute-done.7
  52.3 4.8 %collective-permute-start.10 = (bf16[4,72,128]{2,1,0:T(8,128)(2,1)S(1)}, bf16[4,72,128]{2,1,0:T(8,128)(2,1)S(1)}, u32[]{:S(2)}, u32[]{:S(2)}) collective-permute-start(bf16[4,72,128]{2,1,0:T(8,128)(2,1)S(1)} %add_convert_fusion.1), channel_id=1, source_target_pairs={{0,134},{1,135},{2,132},{3,133},{4,130},{5,131},{6,128},{7,129},{8... | collective-permute-start | bytes 221192 | tf_op jit(solution)/shard_map/ppermute | solution.py:567
  57.1 2.2 %collective-permute-done.10 = bf16[4,72,128]{2,1,0:T(8,128)(2,1)S(1)} collective-permute-done((bf16[4,72,128]{2,1,0:T(8,128)(2,1)S(1)}, bf16[4,72,128]{2,1,0:T(8,128)(2,1)S(1)}, u32[]{:S(2)}, u32[]{:S(2)}) %collective-permute-start.10) | collective-permute-done | bytes 73760 | tf_op jit(solution)/shard_map/ppermute | solution.py:567
  59.3 1.3 %collective-permute-start.13 = (bf16[4,72,128]{2,1,0:T(8,128)(2,1)S(1)}, bf16[4,72,128]{2,1,0:T(8,128)(2,1)S(1)}, u32[]{:S(2)}, u32[]{:S(2)}) collective-permute-start(bf16[4,72,128]{2,1,0:T(8,128)(2,1)S(1)} %get-tuple-element.60), channel_id=1, source_target_pairs={{0,6},{1,7},{2,4},{3,5},{4,2},{5,3},{6,0},{7,1},{8,14},{9,15},{10,... | collective-permute-start | bytes 221192 | tf_op jit(solution)/shard_map/ppermute | solution.py:567
  60.6 0.4 collective-permute-start.12
  61.0 1.9 %collective-permute-start.11 = (bf16[4,72,128]{2,1,0:T(8,128)(2,1)S(1)}, bf16[4,72,128]{2,1,0:T(8,128)(2,1)S(1)}, u32[]{:S(2)}, u32[]{:S(2)}) collective-permute-start(bf16[4,72,128]{2,1,0:T(8,128)(2,1)S(1)} %get-tuple-element.60), channel_id=1, source_target_pairs={{0,2},{1,3},{2,0},{3,1},{4,6},{5,7},{6,4},{7,5},{8,10},{9,11},{10,... | collective-permute-start | bytes 221192 | tf_op jit(solution)/shard_map/ppermute | solution.py:567
  62.9 0.0 copy-done
  62.9 0.0 copy-done.1
  62.9 1.1 %node.1 = f32[64,512]{1,0:T(8,128)} custom-call(bf16[128,512]{1,0:T(8,128)(2,1)S(1)} %get-tuple-element.41.sums_ref, f32[64,128]{1,0:T(8,128)S(1)} %get-tuple-element.42.cot_ref, bf16[512,512]{1,0:T(8,128)(2,1)S(1)} %copy-done, bf16[512,512]{1,0:T(8,128)(2,1)S(1)} %copy-done.1, bf16[144,512]{1,0:T(8,128)(2,1)S(1)} %maximum_maximum_fusion.wide_ref), custom_call_target="tpu_custom_call" | custom-call | tf_op jit(solution)/shard_map/node/pallas_call | solution.py:460
  64.0 0.5 collective-permute-done.13
  64.5 1.5 %collective-permute-done.12 = bf16[4,72,128]{2,1,0:T(8,128)(2,1)S(1)} collective-permute-done((bf16[4,72,128]{2,1,0:T(8,128)(2,1)S(1)}, bf16[4,72,128]{2,1,0:T(8,128)(2,1)S(1)}, u32[]{:S(2)}, u32[]{:S(2)}) %collective-permute-start.12) | collective-permute-done | bytes 73760 | tf_op jit(solution)/shard_map/ppermute | solution.py:567
  66.0 0.0 collective-permute-done.11
  66.0 1.0 %collective-permute-start.16 = (bf16[16,72,128]{2,1,0:T(8,128)(2,1)S(1)}, bf16[16,72,128]{2,1,0:T(8,128)(2,1)S(1)}, u32[]{:S(2)}, u32[]{:S(2)}) collective-permute-start(bf16[16,72,128]{2,1,0:T(8,128)(2,1)S(1)} %pad_maximum_fusion.1), channel_id=1, source_target_pairs={{0,64},{1,17},{2,66},{3,19},{4,68},{5,21},{6,70},{7,23},{8,72},{9,... | collective-permute-start | bytes 884744 | tf_op jit(solution)/shard_map/ppermute | solution.py:567
  67.0 1.3 %collective-permute-start.15 = (bf16[16,72,128]{2,1,0:T(8,128)(2,1)S(1)}, bf16[16,72,128]{2,1,0:T(8,128)(2,1)S(1)}, u32[]{:S(2)}, u32[]{:S(2)}) collective-permute-start(bf16[16,72,128]{2,1,0:T(8,128)(2,1)S(1)} %pad_maximum_fusion.1), channel_id=1, source_target_pairs={{0,96},{1,25},{2,98},{3,27},{4,100},{5,29},{6,102},{7,31},{8,104},... | collective-permute-start | bytes 884744 | tf_op jit(solution)/shard_map/ppermute | solution.py:567
  68.3 0.2 collective-permute-start.14
  68.5 4.8 %collective-permute-done.16 = bf16[16,72,128]{2,1,0:T(8,128)(2,1)S(1)} collective-permute-done((bf16[16,72,128]{2,1,0:T(8,128)(2,1)S(1)}, bf16[16,72,128]{2,1,0:T(8,128)(2,1)S(1)}, u32[]{:S(2)}, u32[]{:S(2)}) %collective-permute-start.16) | collective-permute-done | bytes 294944 | tf_op jit(solution)/shard_map/ppermute | solution.py:567
  73.3 1.9 %collective-permute-done.15 = bf16[16,72,128]{2,1,0:T(8,128)(2,1)S(1)} collective-permute-done((bf16[16,72,128]{2,1,0:T(8,128)(2,1)S(1)}, bf16[16,72,128]{2,1,0:T(8,128)(2,1)S(1)}, u32[]{:S(2)}, u32[]{:S(2)}) %collective-permute-start.15) | collective-permute-done | bytes 294944 | tf_op jit(solution)/shard_map/ppermute | solution.py:567
  75.2 1.2 %collective-permute-done.14 = bf16[16,72,128]{2,1,0:T(8,128)(2,1)S(1)} collective-permute-done((bf16[16,72,128]{2,1,0:T(8,128)(2,1)S(1)}, bf16[16,72,128]{2,1,0:T(8,128)(2,1)S(1)}, u32[]{:S(2)}, u32[]{:S(2)}) %collective-permute-start.14) | collective-permute-done | bytes 294944 | tf_op jit(solution)/shard_map/ppermute | solution.py:567
  76.5 7.2 %collective-permute-start.17 = (bf16[64,72,128]{2,1,0:T(8,128)(2,1)S(1)}, bf16[64,72,128]{2,1,0:T(8,128)(2,1)S(1)}, u32[]{:S(2)}, u32[]{:S(2)}) collective-permute-start(bf16[64,72,128]{2,1,0:T(8,128)(2,1)S(1)} %constant_dynamic-update-slice_fusion.ref), channel_id=1, source_target_pairs={{0,1},{1,0},{2,3},{3,2},{4,5},{5,4},{6,7},{7,6},{8,9},{9,8},{10,11... | collective-permute-start | bytes 3538952 | tf_op jit(solution)/shard_map/ppermute | solution.py:567
  83.7 2.6 %place.2 = (f32[512,512]{1,0:T(8,128)}, f32[512,512]{1,0:T(8,128)}, f32[128,512]{1,0:T(8,128)}, f32[512,512]{1,0:T(8,128)}, f32[512,512]{1,0:T(8,128)}, /*index=5*/f32[1,512]{1,0:T(1,128)}) custom-call(s32[1]{0:T(128)} %bitcast.12.x_ref, s32[1]{0:T(128)} %bitcast.13.y_ref, s32[1]{0:T(128)} %bitcast.1.slice_ref, ...), custom_call_target="tpu_custom_call" | custom-call | tf_op jit(solution)/shard_map/place/pallas_call | solution.py:528
  86.3 0.0 collective-permute-done.17.ref
  86.4 2.6 %place.3 = (f32[512,512]{1,0:T(8,128)}, f32[512,512]{1,0:T(8,128)}, f32[128,512]{1,0:T(8,128)}, f32[512,512]{1,0:T(8,128)}, f32[512,512]{1,0:T(8,128)}, /*index=5*/f32[1,512]{1,0:T(1,128)}) custom-call(s32[1]{0:T(128)} %bitcast.12.x_ref, s32[1]{0:T(128)} %bitcast.13.y_ref, ...), custom_call_target="tpu_custom_call", output_to_operand_aliasing={{0}: (4, {}), {1}: (5, {}), {2}: (6, {}), {3}: (7, {}), {4}... | custom-call | tf_op jit(solution)/shard_map/place/pallas_call | solution.py:528
  (12 shorter events, 0.3 us)
Async XLA Ops:
  3.6 7.3 %collective-permute-start.2 = (bf16[1,80,512]{2,1,0:T(8,128)(2,1)}, bf16[1,80,512]{2,1,0:T(8,128)(2,1)S(1)}, u32[]{:S(2)}, u32[]{:S(2)}) collective-permute-start(bf16[1,80,512]{2,1,0:T(8,128)(2,1)} %bitcast.20), channel_id=1, source_target_pairs={{0,6},{1,7},{2,4},{3,5},{4,2},{5,3},{6,0},{7,1},{8,14},{9,15},{10,... | collective-permute-start | bytes 245768 | tf_op jit(solution)/shard_map/ppermute | solution.py:567
  8.7 7.0 %collective-permute-start.1 = (bf16[1,80,512]{2,1,0:T(8,128)(2,1)}, bf16[1,80,512]{2,1,0:T(8,128)(2,1)S(1)}, u32[]{:S(2)}, u32[]{:S(2)}) collective-permute-start(bf16[1,80,512]{2,1,0:T(8,128)(2,1)} %bitcast.21), channel_id=1, source_target_pairs={{0,4},{1,5},{2,6},{3,7},{4,0},{5,1},{6,2},{7,3},{8,12},{9,13},{10,... | collective-permute-start | bytes 245768 | tf_op jit(solution)/shard_map/ppermute | solution.py:567
  8.7 7.0 %collective-permute-start = (bf16[1,80,512]{2,1,0:T(8,128)(2,1)}, bf16[1,80,512]{2,1,0:T(8,128)(2,1)S(1)}, u32[]{:S(2)}, u32[]{:S(2)}) collective-permute-start(bf16[1,80,512]{2,1,0:T(8,128)(2,1)} %bitcast.22), channel_id=1, source_target_pairs={{0,2},{1,3},{2,0},{3,1},{4,6},{5,7},{6,4},{7,5},{8,10},{9,11},{10,... | collective-permute-start | bytes 245768 | tf_op jit(solution)/shard_map/ppermute | solution.py:567
  16.7 2.2 %collective-permute-start.3 = (bf16[4,80,512]{2,1,0:T(8,128)(2,1)S(1)}, bf16[4,80,512]{2,1,0:T(8,128)(2,1)S(1)}, u32[]{:S(2)}, u32[]{:S(2)}) collective-permute-start(bf16[4,80,512]{2,1,0:T(8,128)(2,1)S(1)} %pad_maximum_fusion.own_ref), channel_id=1, source_target_pairs={{0,1},{1,0},{2,3},{3,2},{4,5},{5,4},{6,7},{7,6},{8,9},{9,8},{10,11... | collective-permute-start | bytes 983048 | tf_op jit(solution)/shard_map/ppermute | solution.py:567
  36.3 26.6 %copy-start = (bf16[512,512]{1,0:T(8,128)(2,1)S(1)}, bf16[512,512]{1,0:T(8,128)(2,1)}, u32[]{:S(2)}) copy-start(bf16[512,512]{1,0:T(8,128)(2,1)} %ws_ref.1) | copy-start | bytes 1572868
  36.3 26.6 %copy-start.1 = (bf16[512,512]{1,0:T(8,128)(2,1)S(1)}, bf16[512,512]{1,0:T(8,128)(2,1)}, u32[]{:S(2)}) copy-start(bf16[512,512]{1,0:T(8,128)(2,1)} %wd_ref.1) | copy-start | bytes 1572868
  36.4 4.8 %collective-permute-start.4 = (bf16[4,72,128]{2,1,0:T(8,128)(2,1)S(1)}, bf16[4,72,128]{2,1,0:T(8,128)(2,1)S(1)}, u32[]{:S(2)}, u32[]{:S(2)}) collective-permute-start(bf16[4,72,128]{2,1,0:T(8,128)(2,1)S(1)} %get-tuple-element.61), channel_id=1, source_target_pairs={{0,64},{1,17},{2,66},{3,19},{4,68},{5,21},{6,70},{7,23},{8,72},{9,... | collective-permute-start | bytes 221192 | tf_op jit(solution)/shard_map/ppermute | solution.py:567
  39.3 3.2 %collective-permute-start.6 = (bf16[4,72,128]{2,1,0:T(8,128)(2,1)S(1)}, bf16[4,72,128]{2,1,0:T(8,128)(2,1)S(1)}, u32[]{:S(2)}, u32[]{:S(2)}) collective-permute-start(bf16[4,72,128]{2,1,0:T(8,128)(2,1)S(1)} %get-tuple-element.62), channel_id=1, source_target_pairs={{0,96},{1,25},{2,98},{3,27},{4,100},{5,29},{6,102},{7,31},{8,104},... | collective-permute-start | bytes 221192 | tf_op jit(solution)/shard_map/ppermute | solution.py:567
  40.0 4.4 %collective-permute-start.5 = (bf16[4,72,128]{2,1,0:T(8,128)(2,1)S(1)}, bf16[4,72,128]{2,1,0:T(8,128)(2,1)S(1)}, u32[]{:S(2)}, u32[]{:S(2)}) collective-permute-start(bf16[4,72,128]{2,1,0:T(8,128)(2,1)S(1)} %get-tuple-element.63), channel_id=1, source_target_pairs={{0,32},{1,9},{2,34},{3,11},{4,36},{5,13},{6,38},{7,15},{8,40},{9,1... | collective-permute-start | bytes 221192 | tf_op jit(solution)/shard_map/ppermute | solution.py:567
  44.5 4.3 %collective-permute-start.9 = (bf16[4,72,128]{2,1,0:T(8,128)(2,1)S(1)}, bf16[4,72,128]{2,1,0:T(8,128)(2,1)S(1)}, u32[]{:S(2)}, u32[]{:S(2)}) collective-permute-start(bf16[4,72,128]{2,1,0:T(8,128)(2,1)S(1)} %fusion.1), channel_id=1, source_target_pairs={{0,24},{1,97},{2,26},{3,99},{4,28},{5,101},{6,30},{7,103},{8,0},{9... | collective-permute-start | bytes 221192 | tf_op jit(solution)/shard_map/ppermute | solution.py:567
  47.1 5.2 %collective-permute-start.8 = (bf16[4,72,128]{2,1,0:T(8,128)(2,1)S(1)}, bf16[4,72,128]{2,1,0:T(8,128)(2,1)S(1)}, u32[]{:S(2)}, u32[]{:S(2)}) collective-permute-start(bf16[4,72,128]{2,1,0:T(8,128)(2,1)S(1)} %fusion.1), channel_id=1, source_target_pairs={{0,8},{1,33},{2,10},{3,35},{4,12},{5,37},{6,14},{7,39},{8,16},{9,4... | collective-permute-start | bytes 221192 | tf_op jit(solution)/shard_map/ppermute | solution.py:567
  47.1 5.2 %collective-permute-start.7 = (bf16[4,72,128]{2,1,0:T(8,128)(2,1)S(1)}, bf16[4,72,128]{2,1,0:T(8,128)(2,1)S(1)}, u32[]{:S(2)}, u32[]{:S(2)}) collective-permute-start(bf16[4,72,128]{2,1,0:T(8,128)(2,1)S(1)} %fusion.1), channel_id=1, source_target_pairs={{0,16},{1,65},{2,18},{3,67},{4,20},{5,69},{6,22},{7,71},{8,24},{9,... | collective-permute-start | bytes 221192 | tf_op jit(solution)/shard_map/ppermute | solution.py:567
  52.3 6.9 %collective-permute-start.10 = (bf16[4,72,128]{2,1,0:T(8,128)(2,1)S(1)}, bf16[4,72,128]{2,1,0:T(8,128)(2,1)S(1)}, u32[]{:S(2)}, u32[]{:S(2)}) collective-permute-start(bf16[4,72,128]{2,1,0:T(8,128)(2,1)S(1)} %add_convert_fusion.1), channel_id=1, source_target_pairs={{0,134},{1,135},{2,132},{3,133},{4,130},{5,131},{6,128},{7,129},{8... | collective-permute-start | bytes 221192 | tf_op jit(solution)/shard_map/ppermute | solution.py:567
  59.3 5.2 %collective-permute-start.13 = (bf16[4,72,128]{2,1,0:T(8,128)(2,1)S(1)}, bf16[4,72,128]{2,1,0:T(8,128)(2,1)S(1)}, u32[]{:S(2)}, u32[]{:S(2)}) collective-permute-start(bf16[4,72,128]{2,1,0:T(8,128)(2,1)S(1)} %get-tuple-element.60), channel_id=1, source_target_pairs={{0,6},{1,7},{2,4},{3,5},{4,2},{5,3},{6,0},{7,1},{8,14},{9,15},{10,... | collective-permute-start | bytes 221192 | tf_op jit(solution)/shard_map/ppermute | solution.py:567
  60.6 5.4 %collective-permute-start.12 = (bf16[4,72,128]{2,1,0:T(8,128)(2,1)S(1)}, bf16[4,72,128]{2,1,0:T(8,128)(2,1)S(1)}, u32[]{:S(2)}, u32[]{:S(2)}) collective-permute-start(bf16[4,72,128]{2,1,0:T(8,128)(2,1)S(1)} %get-tuple-element.60), channel_id=1, source_target_pairs={{0,4},{1,5},{2,6},{3,7},{4,0},{5,1},{6,2},{7,3},{8,12},{9,13},{10,... | collective-permute-start | bytes 221192 | tf_op jit(solution)/shard_map/ppermute | solution.py:567
  61.0 5.0 %collective-permute-start.11 = (bf16[4,72,128]{2,1,0:T(8,128)(2,1)S(1)}, bf16[4,72,128]{2,1,0:T(8,128)(2,1)S(1)}, u32[]{:S(2)}, u32[]{:S(2)}) collective-permute-start(bf16[4,72,128]{2,1,0:T(8,128)(2,1)S(1)} %get-tuple-element.60), channel_id=1, source_target_pairs={{0,2},{1,3},{2,0},{3,1},{4,6},{5,7},{6,4},{7,5},{8,10},{9,11},{10,... | collective-permute-start | bytes 221192 | tf_op jit(solution)/shard_map/ppermute | solution.py:567
  66.0 7.3 %collective-permute-start.16 = (bf16[16,72,128]{2,1,0:T(8,128)(2,1)S(1)}, bf16[16,72,128]{2,1,0:T(8,128)(2,1)S(1)}, u32[]{:S(2)}, u32[]{:S(2)}) collective-permute-start(bf16[16,72,128]{2,1,0:T(8,128)(2,1)S(1)} %pad_maximum_fusion.1), channel_id=1, source_target_pairs={{0,64},{1,17},{2,66},{3,19},{4,68},{5,21},{6,70},{7,23},{8,72},{9,... | collective-permute-start | bytes 884744 | tf_op jit(solution)/shard_map/ppermute | solution.py:567
  67.0 8.2 %collective-permute-start.15 = (bf16[16,72,128]{2,1,0:T(8,128)(2,1)S(1)}, bf16[16,72,128]{2,1,0:T(8,128)(2,1)S(1)}, u32[]{:S(2)}, u32[]{:S(2)}) collective-permute-start(bf16[16,72,128]{2,1,0:T(8,128)(2,1)S(1)} %pad_maximum_fusion.1), channel_id=1, source_target_pairs={{0,96},{1,25},{2,98},{3,27},{4,100},{5,29},{6,102},{7,31},{8,104},... | collective-permute-start | bytes 884744 | tf_op jit(solution)/shard_map/ppermute | solution.py:567
  68.3 8.1 %collective-permute-start.14 = (bf16[16,72,128]{2,1,0:T(8,128)(2,1)S(1)}, bf16[16,72,128]{2,1,0:T(8,128)(2,1)S(1)}, u32[]{:S(2)}, u32[]{:S(2)}) collective-permute-start(bf16[16,72,128]{2,1,0:T(8,128)(2,1)S(1)} %pad_maximum_fusion.1), channel_id=1, source_target_pairs={{0,32},{1,9},{2,34},{3,11},{4,36},{5,13},{6,38},{7,15},{8,40},{9,1... | collective-permute-start | bytes 884744 | tf_op jit(solution)/shard_map/ppermute | solution.py:567
  76.5 9.9 %collective-permute-start.17 = (bf16[64,72,128]{2,1,0:T(8,128)(2,1)S(1)}, bf16[64,72,128]{2,1,0:T(8,128)(2,1)S(1)}, u32[]{:S(2)}, u32[]{:S(2)}) collective-permute-start(bf16[64,72,128]{2,1,0:T(8,128)(2,1)S(1)} %constant_dynamic-update-slice_fusion.ref), channel_id=1, source_target_pairs={{0,1},{1,0},{2,3},{3,2},{4,5},{5,4},{6,7},{7,6},{8,9},{9,8},{10,11... | collective-permute-start | bytes 3538952 | tf_op jit(solution)/shard_map/ppermute | solution.py:567

commit v8 on v6

--- a/solution.py
+++ b/solution.py
@@ -93,8 +93,14 @@
     me_ref,
     slice_ref,
     u_ref,
-    own_ref,
-    other_ref,
+    own_0,
+    own_1,
+    own_2,
+    own_3,
+    other_0,
+    other_1,
+    other_2,
+    other_3,
     ws_hbm,
     wd_hbm,
     wide_ref,
@@ -149,11 +155,11 @@
         load.start()
     wr_ref, we_ref = wide_ref.at[0:K], wide_ref.at[K : K + 16]
     me, my_slice, my_u = me_ref[0], slice_ref[0], u_ref[0]
-    for near, ref in ((0, own_ref), (1, other_ref)):
-        for kz in range(4):
+    for near, refs in ((0, (own_0, own_1, own_2, own_3)), (1, (other_0, other_1, other_2, other_3))):
+        for kz, ref in enumerate(refs):
             shard = me ^ (2 * kz + near)
-            h_s[pl.ds(pl.multiple_of(shard * AT, AT), AT), :] = ref[kz, 0:AT, :]
-            meta_s[shard] = ref[kz, AT:PIECE, :].astype(F32)
+            h_s[pl.ds(pl.multiple_of(shard * AT, AT), AT), :] = ref[0:AT, :]
+            meta_s[shard] = ref[AT:PIECE, :].astype(F32)
     gid_rows = []
     for j in range(4):
         both = meta_s[2 * j, :, 0:128] + meta_s[2 * j + 1, :, 0:128]
@@ -405,7 +411,7 @@
             jax.ShapeDtypeStruct((AT, 128), F32),
             jax.ShapeDtypeStruct((4, 4, CH, 128), BF),
         ),
-        in_specs=[sm] * 3 + [vm] * 2 + [far] * 2 + [vm] + [far] * 2,
+        in_specs=[sm] * 3 + [vm] * 8 + [far] * 2 + [vm] + [far] * 2,
         out_specs=(vm,) * 5,
         scratch_shapes=[
             V((ATOMS, D), BF),
@@ -444,7 +450,7 @@
         ],
         compiler_params=pltpu.CompilerParams(vmem_limit_bytes=53760 * 1024),
         name="batch",
-    )(me, part, u, own, other, ws, wd, wide, wt, wo)
+    )(me, part, u, *own, *other, ws, wd, wide, wt, wo)
 
 
 def node_kernel(sums_ref, cot_ref, ws_ref, wd_ref, wide_ref, out_ref):
@@ -615,10 +621,10 @@
         trip_count,
         graph_ids,
         energy_cot,
-    )[None]
-    own = join(piece, *[shift(piece, zl=k) for k in (1, 2, 3)])
-    other = shift(own, c=1)
+    )
     wide = jnp.concatenate([w_radial, w_energy.reshape(1, D), jnp.zeros((15, D), BF)], axis=0)
+    own = [piece] + [shift(piece, zl=k) for k in (1, 2, 3)]
+    other = [shift(p, c=1) for p in own]
     energy, pos_grad, sums, cot, payload = batch(
         me, part, u, own, other, w_src, w_dst, wide, w_trip, w_out
     )

time: 89.7 us -> 88.8 us (0.990)
  waiting for transfers between devices: 26.3 us -> 21.7 us
  starting transfers between devices: 32.3 us -> 36.1 us
  other arithmetic: 2.07 us -> 1.14 us
    ppermute x18 -> x21, waiting for transfers between devices: 26.3 us -> 21.7 us  [shift(): return lax.ppermute(value, AXES, moves(fn))]
    ppermute x18 -> x21, starting transfers between devices: 32.3 us -> 36.1 us  [shift(): return lax.ppermute(value, AXES, moves(fn))]
    concatenate x2 -> x1, other arithmetic: 0.97 us -> 0.04 us  [join(): return jnp.concatenate(parts, axis=0)]
  transfers between devices with their start and end apart: 18 -> 21, of which waited for: 12 -> 12; matrix products, arithmetic and copies ran while one was open for 2% -> 2% of each run, Pallas kernels for 4% -> 4%
where the time goes in v8:
time: 88.8 us; the launch traced here: 88.5 us
  starting transfers between devices  36.1 us (41%)
  Pallas kernels  25.4 us (29%)
  waiting for transfers between devices  21.7 us (24%)
  between operations  2.29 us (3%)
  local copies, waits for them, and re-layouts  1.85 us (2%)
  other arithmetic  1.14 us (1%)
    ppermute x21, starting transfers between devices, shift(): return lax.ppermute(value, AXES, moves(fn))  36.1 us
    ppermute x21, waiting for transfers between devices, shift(): return lax.ppermute(value, AXES, moves(fn))  21.7 us
    pallas_call x1, Pallas kernels, batch(): pl.pallas_call(main_kernel, out_shape=(jax.ShapeDtypeStruct((1, 16), F32)...  17.4 us
    pallas_call x2, Pallas kernels, place(): pl.pallas_call(functools.partial(place_kernel, c), out_shape=(big, big, j...  5.28 us
  transfers between devices with their start and end apart: 21, of which 12 were waited for; matrix products, arithmetic and copies ran while one was open for 2% of the time, Pallas kernels for 4%

profile of v8, /device:TPU:1, one launch (start us, length us, event | category | flops | bytes accessed | tf_op | source)
XLA Modules:
  0.0 88.5 jit_solution(14124899113857324239)
XLA Ops:
  1.9 1.6 %pack.1.own_0 = bf16[80,512]{1,0:T(8,128)(2,1)} custom-call(s32[1]{0:T(128)} %bitcast.me_ref, bf16[64,512]{1,0:T(8,128)(2,1)} %bitcast.20, f32[3,1,64]{2,1,0:T(1,128)} %bitcast.22, s32[1,256]{1,0:T(1,128)} %src_ref.1, s32[1,256]{1,0:T(1,128)} %dst_ref.1, s32[1,1]{1,0:T(1,128)S(6)} %copy.43.ec_ref, s32[1,1024]{1,0:T(1,128)} %tin_ref.1, s32[1,1024]{1,0:T(1,128)} %tout_ref.1, ...), custom_call_target="tpu_custom_call" | custom-call | tf_op jit(solution)/shard_map/pack/pallas_call | solution.py:82
  3.6 5.2 %collective-permute-start.2 = (bf16[80,512]{1,0:T(8,128)(2,1)}, bf16[80,512]{1,0:T(8,128)(2,1)S(1)}, u32[]{:S(2)}, u32[]{:S(2)}) collective-permute-start(bf16[80,512]{1,0:T(8,128)(2,1)} %pack.1.own_0), channel_id=1, source_target_pairs={{0,6},{1,7},{2,4},{3,5},{4,2},{5,3},{6,0},{7,1},{8,14},{9,15},{10,... | collective-permute-start | bytes 245768 | tf_op jit(solution)/shard_map/ppermute | solution.py:573
  8.7 0.0 collective-permute-start.1
  8.7 0.3 collective-permute-start
  9.0 2.2 %collective-permute-start.3 = (bf16[80,512]{1,0:T(8,128)(2,1)}, bf16[80,512]{1,0:T(8,128)(2,1)S(1)}, u32[]{:S(2)}, u32[]{:S(2)}) collective-permute-start(bf16[80,512]{1,0:T(8,128)(2,1)} %pack.1.own_0), channel_id=1, source_target_pairs={{0,1},{1,0},{2,3},{3,2},{4,5},{5,4},{6,7},{7,6},{8,9},{9,8},{10,11... | collective-permute-start | bytes 245768 | tf_op jit(solution)/shard_map/ppermute | solution.py:573
  11.2 0.7 reshape.44
  11.9 0.1 pad.6.clone
  12.0 0.0 collective-permute-done.2.own_3
  12.0 1.5 %collective-permute-start.6 = (bf16[80,512]{1,0:T(8,128)(2,1)S(1)}, bf16[80,512]{1,0:T(8,128)(2,1)S(1)}, u32[]{:S(2)}, u32[]{:S(2)}) collective-permute-start(bf16[80,512]{1,0:T(8,128)(2,1)S(1)} %collective-permute-done.2.own_3), channel_id=1, source_target_pairs={{0,1},{1,0},{2,3},{3,2},{4,5},{5,4},{6,7},{7,6},{8,9},{9,8},{10,11... | collective-permute-start | bytes 245768 | tf_op jit(solution)/shard_map/ppermute | solution.py:573
  13.5 2.3 %collective-permute-done.1.own_2 = bf16[80,512]{1,0:T(8,128)(2,1)S(1)} collective-permute-done((bf16[80,512]{1,0:T(8,128)(2,1)}, bf16[80,512]{1,0:T(8,128)(2,1)S(1)}, u32[]{:S(2)}, u32[]{:S(2)}) %collective-permute-start.1) | collective-permute-done | bytes 81952 | tf_op jit(solution)/shard_map/ppermute | solution.py:573
  15.8 0.7 collective-permute-start.5
  16.4 0.0 collective-permute-done.own_1
  16.4 0.0 collective-permute-start.4
  16.5 1.0 %maximum_maximum_fusion.wide_ref = bf16[144,512]{1,0:T(8,128)(2,1)S(1)} fusion(bf16[1,512]{1,0:T(2,128)(2,1)S(1)} %reshape.44, bf16[128,512]{1,0:T(8,128)(2,1)} %param.27, bf16[144]{0:T(256)(128)(2,1)S(1)} %pad.6.clone), kind=kLoop, calls=%fused_computation.1 | loop fusion | flops 442368 | bytes 279840 | tf_op jit(solution)/shard_map/concatenate | solution.py:625
  17.5 0.0 collective-permute-done.3.other_0
  17.5 0.0 collective-permute-done.6.other_3
  17.5 0.0 collective-permute-done.5.other_2
  17.5 0.2 collective-permute-done.4.other_1
  17.7 0.0 copy-start.2
  17.7 0.9 copy-done.2
  18.6 17.4 %batch.1 = (f32[1,16]{1,0:T(1,128)}, f32[3,1,64]{2,1,0:T(1,128)}, bf16[128,512]{1,0:T(8,128)(2,1)S(1)}, f32[64,128]{1,0:T(8,128)S(1)}, bf16[4,4,72,128]{3,2,1,0:T(8,128)(2,1)S(1)}) custom-call(s32[1]{0:T(128)} %bitcast.me_ref, s32[1]{0:T(128)} %bitcast.1.slice_ref, s32[1]{0:T(128)} %bitcast.2.u_ref, bf16[80,512]{1,0:T(8,128)(2,1)S(1)} %copy-done.2, ...), custom_call_target="tpu_custom_call" | custom-call | tf_op jit(solution)/shard_map/batch/pallas_call | solution.py:405
  36.1 0.0 copy-start
  36.1 0.0 copy-start.1
  36.1 2.9 %collective-permute-start.7 = (bf16[4,72,128]{2,1,0:T(8,128)(2,1)S(1)}, bf16[4,72,128]{2,1,0:T(8,128)(2,1)S(1)}, u32[]{:S(2)}, u32[]{:S(2)}) collective-permute-start(bf16[4,72,128]{2,1,0:T(8,128)(2,1)S(1)} %get-tuple-element.53), channel_id=1, source_target_pairs={{0,64},{1,17},{2,66},{3,19},{4,68},{5,21},{6,70},{7,23},{8,72},{9,... | collective-permute-start | bytes 221192 | tf_op jit(solution)/shard_map/ppermute | solution.py:573
  39.0 0.8 collective-permute-start.9
  39.8 0.7 collective-permute-start.8
  40.5 0.7 collective-permute-done.7
  41.2 1.0 %collective-permute-done.9 = bf16[4,72,128]{2,1,0:T(8,128)(2,1)S(1)} collective-permute-done((bf16[4,72,128]{2,1,0:T(8,128)(2,1)S(1)}, bf16[4,72,128]{2,1,0:T(8,128)(2,1)S(1)}, u32[]{:S(2)}, u32[]{:S(2)}) %collective-permute-start.9) | collective-permute-done | bytes 73760 | tf_op jit(solution)/shard_map/ppermute | solution.py:573
  42.2 2.0 %collective-permute-done.8 = bf16[4,72,128]{2,1,0:T(8,128)(2,1)S(1)} collective-permute-done((bf16[4,72,128]{2,1,0:T(8,128)(2,1)S(1)}, bf16[4,72,128]{2,1,0:T(8,128)(2,1)S(1)}, u32[]{:S(2)}, u32[]{:S(2)}) %collective-permute-start.8) | collective-permute-done | bytes 73760 | tf_op jit(solution)/shard_map/ppermute | solution.py:573
  44.2 2.6 %collective-permute-start.12 = (bf16[4,72,128]{2,1,0:T(8,128)(2,1)S(1)}, bf16[4,72,128]{2,1,0:T(8,128)(2,1)S(1)}, u32[]{:S(2)}, u32[]{:S(2)}) collective-permute-start(bf16[4,72,128]{2,1,0:T(8,128)(2,1)S(1)} %fusion.1), channel_id=1, source_target_pairs={{0,24},{1,97},{2,26},{3,99},{4,28},{5,101},{6,30},{7,103},{8,0},{9... | collective-permute-start | bytes 221192 | tf_op jit(solution)/shard_map/ppermute | solution.py:573
  46.8 0.0 collective-permute-start.11
  46.8 1.7 %collective-permute-start.10 = (bf16[4,72,128]{2,1,0:T(8,128)(2,1)S(1)}, bf16[4,72,128]{2,1,0:T(8,128)(2,1)S(1)}, u32[]{:S(2)}, u32[]{:S(2)}) collective-permute-start(bf16[4,72,128]{2,1,0:T(8,128)(2,1)S(1)} %fusion.1), channel_id=1, source_target_pairs={{0,16},{1,65},{2,18},{3,67},{4,20},{5,69},{6,22},{7,71},{8,24},{9,... | collective-permute-start | bytes 221192 | tf_op jit(solution)/shard_map/ppermute | solution.py:573
  48.5 0.0 collective-permute-done.12
  48.5 3.5 %collective-permute-done.11 = bf16[4,72,128]{2,1,0:T(8,128)(2,1)S(1)} collective-permute-done((bf16[4,72,128]{2,1,0:T(8,128)(2,1)S(1)}, bf16[4,72,128]{2,1,0:T(8,128)(2,1)S(1)}, u32[]{:S(2)}, u32[]{:S(2)}) %collective-permute-start.11) | collective-permute-done | bytes 73760 | tf_op jit(solution)/shard_map/ppermute | solution.py:573
  52.0 0.0 collective-permute-done.10
  52.0 4.8 %collective-permute-start.13 = (bf16[4,72,128]{2,1,0:T(8,128)(2,1)S(1)}, bf16[4,72,128]{2,1,0:T(8,128)(2,1)S(1)}, u32[]{:S(2)}, u32[]{:S(2)}) collective-permute-start(bf16[4,72,128]{2,1,0:T(8,128)(2,1)S(1)} %add_convert_fusion.1), channel_id=1, source_target_pairs={{0,134},{1,135},{2,132},{3,133},{4,130},{5,131},{6,128},{7,129},{8... | collective-permute-start | bytes 221192 | tf_op jit(solution)/shard_map/ppermute | solution.py:573
  56.8 2.1 %collective-permute-done.13 = bf16[4,72,128]{2,1,0:T(8,128)(2,1)S(1)} collective-permute-done((bf16[4,72,128]{2,1,0:T(8,128)(2,1)S(1)}, bf16[4,72,128]{2,1,0:T(8,128)(2,1)S(1)}, u32[]{:S(2)}, u32[]{:S(2)}) %collective-permute-start.13) | collective-permute-done | bytes 73760 | tf_op jit(solution)/shard_map/ppermute | solution.py:573
  58.9 1.5 %collective-permute-start.16 = (bf16[4,72,128]{2,1,0:T(8,128)(2,1)S(1)}, bf16[4,72,128]{2,1,0:T(8,128)(2,1)S(1)}, u32[]{:S(2)}, u32[]{:S(2)}) collective-permute-start(bf16[4,72,128]{2,1,0:T(8,128)(2,1)S(1)} %get-tuple-element.52), channel_id=1, source_target_pairs={{0,6},{1,7},{2,4},{3,5},{4,2},{5,3},{6,0},{7,1},{8,14},{9,15},{10,... | collective-permute-start | bytes 221192 | tf_op jit(solution)/shard_map/ppermute | solution.py:573
  60.4 0.0 collective-permute-start.15
  60.5 2.1 %collective-permute-start.14 = (bf16[4,72,128]{2,1,0:T(8,128)(2,1)S(1)}, bf16[4,72,128]{2,1,0:T(8,128)(2,1)S(1)}, u32[]{:S(2)}, u32[]{:S(2)}) collective-permute-start(bf16[4,72,128]{2,1,0:T(8,128)(2,1)S(1)} %get-tuple-element.52), channel_id=1, source_target_pairs={{0,2},{1,3},{2,0},{3,1},{4,6},{5,7},{6,4},{7,5},{8,10},{9,11},{10,... | collective-permute-start | bytes 221192 | tf_op jit(solution)/shard_map/ppermute | solution.py:573
  62.6 0.0 copy-done
  62.6 0.0 copy-done.1
  62.6 1.1 %node.1 = f32[64,512]{1,0:T(8,128)} custom-call(bf16[128,512]{1,0:T(8,128)(2,1)S(1)} %get-tuple-element.33.sums_ref, f32[64,128]{1,0:T(8,128)S(1)} %get-tuple-element.34.cot_ref, bf16[512,512]{1,0:T(8,128)(2,1)S(1)} %copy-done, bf16[512,512]{1,0:T(8,128)(2,1)S(1)} %copy-done.1, bf16[144,512]{1,0:T(8,128)(2,1)S(1)} %maximum_maximum_fusion.wide_ref), custom_call_target="tpu_custom_call" | custom-call | tf_op jit(solution)/shard_map/node/pallas_call | solution.py:466
  63.6 0.4 collective-permute-done.16
  64.1 1.5 %collective-permute-done.15 = bf16[4,72,128]{2,1,0:T(8,128)(2,1)S(1)} collective-permute-done((bf16[4,72,128]{2,1,0:T(8,128)(2,1)S(1)}, bf16[4,72,128]{2,1,0:T(8,128)(2,1)S(1)}, u32[]{:S(2)}, u32[]{:S(2)}) %collective-permute-start.15) | collective-permute-done | bytes 73760 | tf_op jit(solution)/shard_map/ppermute | solution.py:573
  65.6 0.0 collective-permute-done.14
  65.6 1.2 %collective-permute-start.19 = (bf16[16,72,128]{2,1,0:T(8,128)(2,1)S(1)}, bf16[16,72,128]{2,1,0:T(8,128)(2,1)S(1)}, u32[]{:S(2)}, u32[]{:S(2)}) collective-permute-start(bf16[16,72,128]{2,1,0:T(8,128)(2,1)S(1)} %pad_maximum_fusion), channel_id=1, source_target_pairs={{0,64},{1,17},{2,66},{3,19},{4,68},{5,21},{6,70},{7,23},{8,72},{9,... | collective-permute-start | bytes 884744 | tf_op jit(solution)/shard_map/ppermute | solution.py:573
  66.8 1.1 %collective-permute-start.18 = (bf16[16,72,128]{2,1,0:T(8,128)(2,1)S(1)}, bf16[16,72,128]{2,1,0:T(8,128)(2,1)S(1)}, u32[]{:S(2)}, u32[]{:S(2)}) collective-permute-start(bf16[16,72,128]{2,1,0:T(8,128)(2,1)S(1)} %pad_maximum_fusion), channel_id=1, source_target_pairs={{0,96},{1,25},{2,98},{3,27},{4,100},{5,29},{6,102},{7,31},{8,104},... | collective-permute-start | bytes 884744 | tf_op jit(solution)/shard_map/ppermute | solution.py:573
  67.9 0.4 collective-permute-start.17
  68.3 4.6 %collective-permute-done.19 = bf16[16,72,128]{2,1,0:T(8,128)(2,1)S(1)} collective-permute-done((bf16[16,72,128]{2,1,0:T(8,128)(2,1)S(1)}, bf16[16,72,128]{2,1,0:T(8,128)(2,1)S(1)}, u32[]{:S(2)}, u32[]{:S(2)}) %collective-permute-start.19) | collective-permute-done | bytes 294944 | tf_op jit(solution)/shard_map/ppermute | solution.py:573
  72.9 1.8 %collective-permute-done.18 = bf16[16,72,128]{2,1,0:T(8,128)(2,1)S(1)} collective-permute-done((bf16[16,72,128]{2,1,0:T(8,128)(2,1)S(1)}, bf16[16,72,128]{2,1,0:T(8,128)(2,1)S(1)}, u32[]{:S(2)}, u32[]{:S(2)}) %collective-permute-start.18) | collective-permute-done | bytes 294944 | tf_op jit(solution)/shard_map/ppermute | solution.py:573
  74.7 1.6 %collective-permute-done.17 = bf16[16,72,128]{2,1,0:T(8,128)(2,1)S(1)} collective-permute-done((bf16[16,72,128]{2,1,0:T(8,128)(2,1)S(1)}, bf16[16,72,128]{2,1,0:T(8,128)(2,1)S(1)}, u32[]{:S(2)}, u32[]{:S(2)}) %collective-permute-start.17) | collective-permute-done | bytes 294944 | tf_op jit(solution)/shard_map/ppermute | solution.py:573
  76.4 6.6 %collective-permute-start.20 = (bf16[64,72,128]{2,1,0:T(8,128)(2,1)S(1)}, bf16[64,72,128]{2,1,0:T(8,128)(2,1)S(1)}, u32[]{:S(2)}, u32[]{:S(2)}) collective-permute-start(bf16[64,72,128]{2,1,0:T(8,128)(2,1)S(1)} %constant_dynamic-update-slice_fusion.ref), channel_id=1, source_target_pairs={{0,1},{1,0},{2,3},{3,2},{4,5},{5,4},{6,7},{7,6},{8,9},{9,8},{10,11... | collective-permute-start | bytes 3538952 | tf_op jit(solution)/shard_map/ppermute | solution.py:573
  83.0 2.6 %place.2 = (f32[512,512]{1,0:T(8,128)}, f32[512,512]{1,0:T(8,128)}, f32[128,512]{1,0:T(8,128)}, f32[512,512]{1,0:T(8,128)}, f32[512,512]{1,0:T(8,128)}, /*index=5*/f32[1,512]{1,0:T(1,128)}) custom-call(s32[1]{0:T(128)} %bitcast.11.x_ref, s32[1]{0:T(128)} %bitcast.12.y_ref, s32[1]{0:T(128)} %bitcast.1.slice_ref, ...), custom_call_target="tpu_custom_call" | custom-call | tf_op jit(solution)/shard_map/place/pallas_call | solution.py:534
  85.7 0.0 collective-permute-done.20.ref
  85.7 2.6 %place.3 = (f32[512,512]{1,0:T(8,128)}, f32[512,512]{1,0:T(8,128)}, f32[128,512]{1,0:T(8,128)}, f32[512,512]{1,0:T(8,128)}, f32[512,512]{1,0:T(8,128)}, /*index=5*/f32[1,512]{1,0:T(1,128)}) custom-call(s32[1]{0:T(128)} %bitcast.11.x_ref, s32[1]{0:T(128)} %bitcast.12.y_ref, ...), custom_call_target="tpu_custom_call", output_to_operand_aliasing={{0}: (4, {}), {1}: (5, {}), {2}: (6, {}), {3}: (7, {}), {4}... | custom-call | tf_op jit(solution)/shard_map/place/pallas_call | solution.py:534
  (12 shorter events, 0.3 us)
Async XLA Ops:
  3.6 8.4 %collective-permute-start.2 = (bf16[80,512]{1,0:T(8,128)(2,1)}, bf16[80,512]{1,0:T(8,128)(2,1)S(1)}, u32[]{:S(2)}, u32[]{:S(2)}) collective-permute-start(bf16[80,512]{1,0:T(8,128)(2,1)} %pack.1.own_0), channel_id=1, source_target_pairs={{0,6},{1,7},{2,4},{3,5},{4,2},{5,3},{6,0},{7,1},{8,14},{9,15},{10,... | collective-permute-start | bytes 245768 | tf_op jit(solution)/shard_map/ppermute | solution.py:573
  8.7 7.0 %collective-permute-start.1 = (bf16[80,512]{1,0:T(8,128)(2,1)}, bf16[80,512]{1,0:T(8,128)(2,1)S(1)}, u32[]{:S(2)}, u32[]{:S(2)}) collective-permute-start(bf16[80,512]{1,0:T(8,128)(2,1)} %pack.1.own_0), channel_id=1, source_target_pairs={{0,4},{1,5},{2,6},{3,7},{4,0},{5,1},{6,2},{7,3},{8,12},{9,13},{10,... | collective-permute-start | bytes 245768 | tf_op jit(solution)/shard_map/ppermute | solution.py:573
  8.7 7.7 %collective-permute-start = (bf16[80,512]{1,0:T(8,128)(2,1)}, bf16[80,512]{1,0:T(8,128)(2,1)S(1)}, u32[]{:S(2)}, u32[]{:S(2)}) collective-permute-start(bf16[80,512]{1,0:T(8,128)(2,1)} %pack.1.own_0), channel_id=1, source_target_pairs={{0,2},{1,3},{2,0},{3,1},{4,6},{5,7},{6,4},{7,5},{8,10},{9,11},{10,... | collective-permute-start | bytes 245768 | tf_op jit(solution)/shard_map/ppermute | solution.py:573
  9.0 8.4 %collective-permute-start.3 = (bf16[80,512]{1,0:T(8,128)(2,1)}, bf16[80,512]{1,0:T(8,128)(2,1)S(1)}, u32[]{:S(2)}, u32[]{:S(2)}) collective-permute-start(bf16[80,512]{1,0:T(8,128)(2,1)} %pack.1.own_0), channel_id=1, source_target_pairs={{0,1},{1,0},{2,3},{3,2},{4,5},{5,4},{6,7},{7,6},{8,9},{9,8},{10,11... | collective-permute-start | bytes 245768 | tf_op jit(solution)/shard_map/ppermute | solution.py:573
  12.0 5.5 %collective-permute-start.6 = (bf16[80,512]{1,0:T(8,128)(2,1)S(1)}, bf16[80,512]{1,0:T(8,128)(2,1)S(1)}, u32[]{:S(2)}, u32[]{:S(2)}) collective-permute-start(bf16[80,512]{1,0:T(8,128)(2,1)S(1)} %collective-permute-done.2.own_3), channel_id=1, source_target_pairs={{0,1},{1,0},{2,3},{3,2},{4,5},{5,4},{6,7},{7,6},{8,9},{9,8},{10,11... | collective-permute-start | bytes 245768 | tf_op jit(solution)/shard_map/ppermute | solution.py:573
  15.8 1.7 %collective-permute-start.5 = (bf16[80,512]{1,0:T(8,128)(2,1)S(1)}, bf16[80,512]{1,0:T(8,128)(2,1)S(1)}, u32[]{:S(2)}, u32[]{:S(2)}) collective-permute-start(bf16[80,512]{1,0:T(8,128)(2,1)S(1)} %collective-permute-done.1.own_2), channel_id=1, source_target_pairs={{0,1},{1,0},{2,3},{3,2},{4,5},{5,4},{6,7},{7,6},{8,9},{9,8},{10,11... | collective-permute-start | bytes 245768 | tf_op jit(solution)/shard_map/ppermute | solution.py:573
  16.4 1.3 %collective-permute-start.4 = (bf16[80,512]{1,0:T(8,128)(2,1)S(1)}, bf16[80,512]{1,0:T(8,128)(2,1)S(1)}, u32[]{:S(2)}, u32[]{:S(2)}) collective-permute-start(bf16[80,512]{1,0:T(8,128)(2,1)S(1)} %collective-permute-done.own_1), channel_id=1, source_target_pairs={{0,1},{1,0},{2,3},{3,2},{4,5},{5,4},{6,7},{7,6},{8,9},{9,8},{10,11... | collective-permute-start | bytes 245768 | tf_op jit(solution)/shard_map/ppermute | solution.py:573
  17.7 0.9 %copy-start.2 = (bf16[80,512]{1,0:T(8,128)(2,1)S(1)}, bf16[80,512]{1,0:T(8,128)(2,1)}, u32[]{:S(2)}) copy-start(bf16[80,512]{1,0:T(8,128)(2,1)} %pack.1.own_0) | copy-start | bytes 245764
  36.1 26.5 %copy-start = (bf16[512,512]{1,0:T(8,128)(2,1)S(1)}, bf16[512,512]{1,0:T(8,128)(2,1)}, u32[]{:S(2)}) copy-start(bf16[512,512]{1,0:T(8,128)(2,1)} %ws_ref.1) | copy-start | bytes 1572868
  36.1 26.5 %copy-start.1 = (bf16[512,512]{1,0:T(8,128)(2,1)S(1)}, bf16[512,512]{1,0:T(8,128)(2,1)}, u32[]{:S(2)}) copy-start(bf16[512,512]{1,0:T(8,128)(2,1)} %wd_ref.1) | copy-start | bytes 1572868
  36.1 5.1 %collective-permute-start.7 = (bf16[4,72,128]{2,1,0:T(8,128)(2,1)S(1)}, bf16[4,72,128]{2,1,0:T(8,128)(2,1)S(1)}, u32[]{:S(2)}, u32[]{:S(2)}) collective-permute-start(bf16[4,72,128]{2,1,0:T(8,128)(2,1)S(1)} %get-tuple-element.53), channel_id=1, source_target_pairs={{0,64},{1,17},{2,66},{3,19},{4,68},{5,21},{6,70},{7,23},{8,72},{9,... | collective-permute-start | bytes 221192 | tf_op jit(solution)/shard_map/ppermute | solution.py:573
  39.0 3.2 %collective-permute-start.9 = (bf16[4,72,128]{2,1,0:T(8,128)(2,1)S(1)}, bf16[4,72,128]{2,1,0:T(8,128)(2,1)S(1)}, u32[]{:S(2)}, u32[]{:S(2)}) collective-permute-start(bf16[4,72,128]{2,1,0:T(8,128)(2,1)S(1)} %get-tuple-element.54), channel_id=1, source_target_pairs={{0,96},{1,25},{2,98},{3,27},{4,100},{5,29},{6,102},{7,31},{8,104},... | collective-permute-start | bytes 221192 | tf_op jit(solution)/shard_map/ppermute | solution.py:573
  39.8 4.4 %collective-permute-start.8 = (bf16[4,72,128]{2,1,0:T(8,128)(2,1)S(1)}, bf16[4,72,128]{2,1,0:T(8,128)(2,1)S(1)}, u32[]{:S(2)}, u32[]{:S(2)}) collective-permute-start(bf16[4,72,128]{2,1,0:T(8,128)(2,1)S(1)} %get-tuple-element.55), channel_id=1, source_target_pairs={{0,32},{1,9},{2,34},{3,11},{4,36},{5,13},{6,38},{7,15},{8,40},{9,1... | collective-permute-start | bytes 221192 | tf_op jit(solution)/shard_map/ppermute | solution.py:573
  44.2 4.3 %collective-permute-start.12 = (bf16[4,72,128]{2,1,0:T(8,128)(2,1)S(1)}, bf16[4,72,128]{2,1,0:T(8,128)(2,1)S(1)}, u32[]{:S(2)}, u32[]{:S(2)}) collective-permute-start(bf16[4,72,128]{2,1,0:T(8,128)(2,1)S(1)} %fusion.1), channel_id=1, source_target_pairs={{0,24},{1,97},{2,26},{3,99},{4,28},{5,101},{6,30},{7,103},{8,0},{9... | collective-permute-start | bytes 221192 | tf_op jit(solution)/shard_map/ppermute | solution.py:573
  46.8 5.2 %collective-permute-start.11 = (bf16[4,72,128]{2,1,0:T(8,128)(2,1)S(1)}, bf16[4,72,128]{2,1,0:T(8,128)(2,1)S(1)}, u32[]{:S(2)}, u32[]{:S(2)}) collective-permute-start(bf16[4,72,128]{2,1,0:T(8,128)(2,1)S(1)} %fusion.1), channel_id=1, source_target_pairs={{0,8},{1,33},{2,10},{3,35},{4,12},{5,37},{6,14},{7,39},{8,16},{9,4... | collective-permute-start | bytes 221192 | tf_op jit(solution)/shard_map/ppermute | solution.py:573
  46.8 5.2 %collective-permute-start.10 = (bf16[4,72,128]{2,1,0:T(8,128)(2,1)S(1)}, bf16[4,72,128]{2,1,0:T(8,128)(2,1)S(1)}, u32[]{:S(2)}, u32[]{:S(2)}) collective-permute-start(bf16[4,72,128]{2,1,0:T(8,128)(2,1)S(1)} %fusion.1), channel_id=1, source_target_pairs={{0,16},{1,65},{2,18},{3,67},{4,20},{5,69},{6,22},{7,71},{8,24},{9,... | collective-permute-start | bytes 221192 | tf_op jit(solution)/shard_map/ppermute | solution.py:573
  52.0 6.8 %collective-permute-start.13 = (bf16[4,72,128]{2,1,0:T(8,128)(2,1)S(1)}, bf16[4,72,128]{2,1,0:T(8,128)(2,1)S(1)}, u32[]{:S(2)}, u32[]{:S(2)}) collective-permute-start(bf16[4,72,128]{2,1,0:T(8,128)(2,1)S(1)} %add_convert_fusion.1), channel_id=1, source_target_pairs={{0,134},{1,135},{2,132},{3,133},{4,130},{5,131},{6,128},{7,129},{8... | collective-permute-start | bytes 221192 | tf_op jit(solution)/shard_map/ppermute | solution.py:573
  58.9 5.2 %collective-permute-start.16 = (bf16[4,72,128]{2,1,0:T(8,128)(2,1)S(1)}, bf16[4,72,128]{2,1,0:T(8,128)(2,1)S(1)}, u32[]{:S(2)}, u32[]{:S(2)}) collective-permute-start(bf16[4,72,128]{2,1,0:T(8,128)(2,1)S(1)} %get-tuple-element.52), channel_id=1, source_target_pairs={{0,6},{1,7},{2,4},{3,5},{4,2},{5,3},{6,0},{7,1},{8,14},{9,15},{10,... | collective-permute-start | bytes 221192 | tf_op jit(solution)/shard_map/ppermute | solution.py:573
  60.4 5.1 %collective-permute-start.15 = (bf16[4,72,128]{2,1,0:T(8,128)(2,1)S(1)}, bf16[4,72,128]{2,1,0:T(8,128)(2,1)S(1)}, u32[]{:S(2)}, u32[]{:S(2)}) collective-permute-start(bf16[4,72,128]{2,1,0:T(8,128)(2,1)S(1)} %get-tuple-element.52), channel_id=1, source_target_pairs={{0,4},{1,5},{2,6},{3,7},{4,0},{5,1},{6,2},{7,3},{8,12},{9,13},{10,... | collective-permute-start | bytes 221192 | tf_op jit(solution)/shard_map/ppermute | solution.py:573
  60.5 5.1 %collective-permute-start.14 = (bf16[4,72,128]{2,1,0:T(8,128)(2,1)S(1)}, bf16[4,72,128]{2,1,0:T(8,128)(2,1)S(1)}, u32[]{:S(2)}, u32[]{:S(2)}) collective-permute-start(bf16[4,72,128]{2,1,0:T(8,128)(2,1)S(1)} %get-tuple-element.52), channel_id=1, source_target_pairs={{0,2},{1,3},{2,0},{3,1},{4,6},{5,7},{6,4},{7,5},{8,10},{9,11},{10,... | collective-permute-start | bytes 221192 | tf_op jit(solution)/shard_map/ppermute | solution.py:573
  65.6 7.3 %collective-permute-start.19 = (bf16[16,72,128]{2,1,0:T(8,128)(2,1)S(1)}, bf16[16,72,128]{2,1,0:T(8,128)(2,1)S(1)}, u32[]{:S(2)}, u32[]{:S(2)}) collective-permute-start(bf16[16,72,128]{2,1,0:T(8,128)(2,1)S(1)} %pad_maximum_fusion), channel_id=1, source_target_pairs={{0,64},{1,17},{2,66},{3,19},{4,68},{5,21},{6,70},{7,23},{8,72},{9,... | collective-permute-start | bytes 884744 | tf_op jit(solution)/shard_map/ppermute | solution.py:573
  66.8 7.9 %collective-permute-start.18 = (bf16[16,72,128]{2,1,0:T(8,128)(2,1)S(1)}, bf16[16,72,128]{2,1,0:T(8,128)(2,1)S(1)}, u32[]{:S(2)}, u32[]{:S(2)}) collective-permute-start(bf16[16,72,128]{2,1,0:T(8,128)(2,1)S(1)} %pad_maximum_fusion), channel_id=1, source_target_pairs={{0,96},{1,25},{2,98},{3,27},{4,100},{5,29},{6,102},{7,31},{8,104},... | collective-permute-start | bytes 884744 | tf_op jit(solution)/shard_map/ppermute | solution.py:573
  67.9 8.4 %collective-permute-start.17 = (bf16[16,72,128]{2,1,0:T(8,128)(2,1)S(1)}, bf16[16,72,128]{2,1,0:T(8,128)(2,1)S(1)}, u32[]{:S(2)}, u32[]{:S(2)}) collective-permute-start(bf16[16,72,128]{2,1,0:T(8,128)(2,1)S(1)} %pad_maximum_fusion), channel_id=1, source_target_pairs={{0,32},{1,9},{2,34},{3,11},{4,36},{5,13},{6,38},{7,15},{8,40},{9,1... | collective-permute-start | bytes 884744 | tf_op jit(solution)/shard_map/ppermute | solution.py:573
  76.4 9.3 %collective-permute-start.20 = (bf16[64,72,128]{2,1,0:T(8,128)(2,1)S(1)}, bf16[64,72,128]{2,1,0:T(8,128)(2,1)S(1)}, u32[]{:S(2)}, u32[]{:S(2)}) collective-permute-start(bf16[64,72,128]{2,1,0:T(8,128)(2,1)S(1)} %constant_dynamic-update-slice_fusion.ref), channel_id=1, source_target_pairs={{0,1},{1,0},{2,3},{3,2},{4,5},{5,4},{6,7},{7,6},{8,9},{9,8},{10,11... | collective-permute-start | bytes 3538952 | tf_op jit(solution)/shard_map/ppermute | solution.py:573
